TPU v7x, 32 devices: a whole 2x2x4 slice. The times are simulated.
32 devices in a mesh: dp: 4 (over z), seq: 8 (over y, x, core).
Axes of the slice: x: 2, y: 2, z: 4, core: 2. Of those that a mesh axis runs over, the one named last changes fastest.
Arguments:
- queries: bfloat16 [4, 1024, 2048], P('dp', 'seq'), may hold values from -34 to 34
- key_rows: bfloat16 [4, 1024, 2048], P('dp', 'seq'), may hold values from -34 to 34
- values: bfloat16 [4, 1024, 2048], P('dp', 'seq'), may hold values from -6 to 6
- adjacency: int32 [4, 8, 8], P('dp'), may hold values from 0 to 7, as said below
- counts: int32 [4, 8], P('dp'), may hold values from 1 to 8, as said below
- out_weight: bfloat16 [2048, 2048], P('dp'), may hold values from -0.125 to 0.125
- out_cotangent: bfloat16 [4, 1024, 2048], P('dp', 'seq'), may hold values from -6 to 6
Outputs:
- layer_out: bfloat16 [4, 1024, 2048], P('dp', 'seq')
- query_grad: bfloat16 [4, 1024, 2048], P('dp', 'seq')
- key_grad: bfloat16 [4, 1024, 2048], P('dp', 'seq')
- value_grad: bfloat16 [4, 1024, 2048], P('dp', 'seq')
- weight_grad: float32 [2048, 2048], P(('dp', 'seq'))
Inputs may be any that keep to these rules, and one draw needn't show every extreme that they name: `adjacency`: row i of a sequence lists 8 different key blocks, slot 0 being block i itself; slots at or beyond the row's count are not attended. `counts`: block 0 of every sequence has all 8 slots live.
All inputs are finite; a program needn't handle non-finite values.
Results may differ from a plain program's by a relative error of at most 0.025.
Values may be sent and summed in bfloat16 or wider, within the bound.
No kernel may reach another device: no remote copies, remote signals or barrier semaphores. Data moves between devices by JAX's collectives and lax.ppermute only.
A program may use at most 128 MiB of HBM per device.

v0:
```python
import jax
import jax.numpy as jnp
from jax import lax
from jax.sharding import PartitionSpec as P

HD = 128
BLK = 128
NBR = 8


def attend(query_blk, key_blk, value_blk, links, live_count):
    scale = HD ** (-0.5)
    blocks = query_blk.shape[0]
    heads = query_blk.shape[2]
    key_near = key_blk[links].reshape(blocks, NBR * BLK, heads, HD)
    value_near = value_blk[links].reshape(blocks, NBR * BLK, heads, HD)
    scores = (
        jnp.einsum("iqhd,ikhd->hiqk", query_blk, key_near, preferred_element_type=jnp.float32)
        * scale
    )
    live = (jnp.arange(NBR * BLK) // BLK)[None, :] < live_count[:, None]
    scores = jnp.where(live[None, :, None, :], scores, -1e30)
    highest = jnp.max(scores, axis=-1, keepdims=True)
    expo = jnp.exp(scores - highest)
    prob = expo / jnp.sum(expo, axis=-1, keepdims=True)
    prob_bf = prob.astype(jnp.bfloat16)
    attended = jnp.einsum(
        "hiqk,ikhd->iqhd", prob_bf, value_near, preferred_element_type=jnp.float32
    ).astype(jnp.bfloat16)
    return (prob, prob_bf, attended, key_near, value_near)


def backward(query_blk, links, grad_blk, prob, prob_bf, attended, key_near, value_near):
    scale = HD ** (-0.5)
    blocks = query_blk.shape[0]
    heads = query_blk.shape[2]
    value_part = jnp.einsum(
        "hiqk,iqhd->ikhd", prob_bf, grad_blk, preferred_element_type=jnp.float32
    )
    grad_prob = jnp.einsum(
        "iqhd,ikhd->hiqk", grad_blk, value_near, preferred_element_type=jnp.float32
    )
    delta = jnp.einsum("iqhd,iqhd->hiq", grad_blk, attended, preferred_element_type=jnp.float32)
    score_grad = (prob * (grad_prob - delta[..., None]) * scale).astype(jnp.bfloat16)
    query_grad = jnp.einsum(
        "hiqk,ikhd->iqhd", score_grad, key_near, preferred_element_type=jnp.float32
    ).astype(jnp.bfloat16)
    key_part = jnp.einsum(
        "hiqk,iqhd->ikhd", score_grad, query_blk, preferred_element_type=jnp.float32
    )
    member = (links.reshape(-1)[None, :] == jnp.arange(blocks)[:, None]).astype(jnp.float32)
    key_grad = jnp.einsum(
        "ja,aqhd->jqhd",
        member,
        key_part.reshape(blocks * NBR, BLK, heads, HD),
        precision=lax.Precision.HIGHEST,
    )
    value_grad = jnp.einsum(
        "ja,aqhd->jqhd",
        member,
        value_part.reshape(blocks * NBR, BLK, heads, HD),
        precision=lax.Precision.HIGHEST,
    )
    return (query_grad, key_grad.astype(jnp.bfloat16), value_grad.astype(jnp.bfloat16))


def local(queries, key_rows, values, adjacency, counts, out_weight, out_cotangent):
    query_heads, key_heads, value_heads = (
        lax.all_to_all(queries[0], "seq", split_axis=1, concat_axis=0, tiled=True),
        lax.all_to_all(key_rows[0], "seq", split_axis=1, concat_axis=0, tiled=True),
        lax.all_to_all(values[0], "seq", split_axis=1, concat_axis=0, tiled=True),
    )
    length = query_heads.shape[0]
    blocks = length // BLK
    heads = query_heads.shape[1] // HD
    shape = (blocks, BLK, heads, HD)
    links = adjacency[0]
    live_count = counts[0]
    query_blk = query_heads.reshape(shape)
    prob, prob_bf, attended, key_near, value_near = attend(
        query_blk, key_heads.reshape(shape), value_heads.reshape(shape), links, live_count
    )
    attn_tokens = lax.all_to_all(
        attended.reshape(length, heads * HD), "seq", split_axis=0, concat_axis=1, tiled=True
    )
    cotangent = out_cotangent[0]
    columns = attn_tokens
    layer_out = jnp.dot(
        columns,
        lax.all_gather(out_weight, "dp", axis=0, tiled=True),
        preferred_element_type=jnp.float32,
    )
    grad_tokens = lax.dot_general(
        cotangent,
        lax.all_gather(out_weight, "dp", axis=0, tiled=True),
        (((1,), (1,)), ((), ())),
        preferred_element_type=jnp.float32,
    )
    grad_heads = lax.all_to_all(
        grad_tokens.astype(jnp.bfloat16), "seq", split_axis=1, concat_axis=0, tiled=True
    )
    query_grad, key_grad, value_grad = backward(
        query_blk, links, grad_heads.reshape(shape), prob, prob_bf, attended, key_near, value_near
    )
    query_back, key_back, value_back = (
        lax.all_to_all(
            query_grad.reshape(length, heads * HD), "seq", split_axis=0, concat_axis=1, tiled=True
        ),
        lax.all_to_all(
            key_grad.reshape(length, heads * HD), "seq", split_axis=0, concat_axis=1, tiled=True
        ),
        lax.all_to_all(
            value_grad.reshape(length, heads * HD), "seq", split_axis=0, concat_axis=1, tiled=True
        ),
    )
    columns = attn_tokens
    weight_grad = lax.psum_scatter(
        lax.dot_general(
            columns, cotangent, (((0,), (0,)), ((), ())), preferred_element_type=jnp.float32
        ),
        ("dp", "seq"),
        scatter_dimension=0,
        tiled=True,
    )
    return (
        layer_out.astype(jnp.bfloat16)[None],
        query_back[None],
        key_back[None],
        value_back[None],
        weight_grad,
    )


def solution(mesh):
    in_specs = (
        P("dp", "seq", None),
        P("dp", "seq", None),
        P("dp", "seq", None),
        P("dp", None, None),
        P("dp", None),
        P("dp", None),
        P("dp", "seq", None),
    )
    out_specs = (
        P("dp", "seq", None),
        P("dp", "seq", None),
        P("dp", "seq", None),
        P("dp", "seq", None),
        P(("dp", "seq"), None),
    )
    return jax.shard_map(local, mesh=mesh, in_specs=in_specs, out_specs=out_specs, check_vma=False)
```

profile of v0, /device:TPU:2, one launch (start us, length us, event | category | flops | bytes accessed | tf_op | source)
XLA Modules:
  0.0 426.6 jit_solution(17517052726988350457)
XLA Ops:
  7.2 0.7 all-gather.2.cloned.1.call-update
  7.9 2.0 copy.89
  10.0 4.3 all-to-all-start.1
  14.2 2.0 copy.92
  16.3 6.2 %all-to-all-done.1 = bf16[128,8,256]{0,2,1:T(8,128)(2,1)S(1)} async-done(((bf16[128,8,256]{0,2,1:T(8,128)(2,1)}), bf16[128,8,256]{0,2,1:T(8,128)(2,1)S(1)}, u32[]{:S(2)}, u32[]{:S(2)}) %all-to-all-start.1) | async-done | bytes 524320 | tf_op jit(solution)/shard_map/all_to_all | solution.py:70
  22.5 4.9 %all-to-all-start.2 = ((bf16[128,8,256]{0,2,1:T(8,128)(2,1)}), bf16[128,8,256]{0,2,1:T(8,128)(2,1)S(1)}, u32[]{:S(2)}, u32[]{:S(2)}) async-start(bf16[128,8,256]{0,2,1:T(8,128)(2,1)} %bitcast.12), calls=%async_computation.2 | async-start | bytes 1048576 | tf_op jit(solution)/shard_map/all_to_all | solution.py:69
  27.4 0.7 compare_select_fusion
  28.1 2.0 copy.86
  30.2 0.7 broadcast_compare_fusion
  30.9 0.3 copy.90
  31.2 3.0 gather_fusion.1
  34.3 4.7 %copy.91 = bf16[64,128,2,128]{3,1,0,2:T(8,128)(2,1)} copy(bf16[64,128,2,128]{3,1,2,0:T(8,128)(2,1)} %gather_fusion.1) | data formatting | bytes 8388608 | tf_op jit(solution)/shard_map/gather | solution.py:15
  39.0 4.2 all-to-all-start
  43.2 3.4 fusion.51
  46.7 6.3 %fusion.63 = (f32[2,8,128]{2,1,0:T(8,128)S(1)}, f32[2,8,128,1024]{2,3,1,0:T(8,128)}) fusion(f32[2,8,1024,128]{3,2,1,0:T(8,128)S(1)} %fusion.51, pred[8,1024]{1,0:T(8,128)(4,1)S(1)} %broadcast_compare_fusion), kind=kOutput, calls=%fused_computation.61 | output fusion | flops 12583935 | bytes 16793600 | tf_op jit(solution)/shard_map/sub | solution.py:24
  53.0 107.5 %all-gather.2.cloned.1.call-done = bf16[2048,2048]{1,0:T(8,128)(2,1)} async-done(((bf16[512,2048]{1,0:T(8,128)(2,1)}), bf16[2048,2048]{1,0:T(8,128)(2,1)}) %all-gather.2.cloned.1.call-update) | async-done | bytes 8388624 | tf_op jit(solution)/shard_map/all_gather | solution.py:90
  160.5 6.2 %convolution_convert_fusion = bf16[128,2048]{1,0:T(8,128)(2,1)S(1)} fusion(bf16[2048,2048]{1,0:T(8,128)(2,1)} %all-gather.2.cloned.1.call-done, bf16[1,128,2048]{2,1,0:T(8,128)(2,1)S(1)} %copy-done), kind=kOutput, calls=%fused_computation.30 | convolution fusion | flops 1074003968 | bytes 9437184 | tf_op jit(solution)/shard_map/dot_general | solution.py:93
  166.7 1.0 copy.138
  167.7 4.2 all-to-all-start.4
  172.0 6.5 %fusion.22 = bf16[2,8,128,1024]{2,3,1,0:T(8,128)(2,1)} fusion(f32[2,8,128,1024]{2,3,1,0:T(8,128)} %get-tuple-element.11, f32[2,8,128]{2,1,0:T(8,128)S(1)} %get-tuple-element.10), kind=kLoop, calls=%fused_computation.27 | loop fusion | flops 4194304 | bytes 12591104 | tf_op jit(solution)/shard_map/convert_element_type | solution.py:26
  178.4 0.3 copy.87
  178.7 3.0 gather_fusion
  181.8 4.7 %copy.88 = bf16[64,128,2,128]{3,1,0,2:T(8,128)(2,1)} copy(bf16[64,128,2,128]{3,1,2,0:T(8,128)(2,1)} %gather_fusion) | data formatting | bytes 8388608 | tf_op jit(solution)/shard_map/gather | solution.py:16
  186.5 4.9 %fusion.46 = (f32[2,8,128]{2,0,1:T(2,128)S(1)}, bf16[8,2,128,128]{3,2,1,0:T(8,128)(2,1)S(1)}) fusion(bf16[128,8,256]{0,2,1:T(8,128)(2,1)S(1)} %all-to-all-done.4, bf16[2,8,128,1024]{2,3,1,0:T(8,128)(2,1)} %fusion.22, bf16[8,1024,2,128]{3,1,0,2:T(8,128)(2,1)} %bitcast.95), kind=kOutput, calls=%fused_computation.38 | convolution fusion | flops 538179584 | bytes 9445376 | tf_op jit(solution)/shard_map/hiqk,ikhd->iqhd/dot_general | solution.py:27
  191.4 23.3 %all_to_all.131 = bf16[8,128,256]{1,2,0:T(8,128)(2,1)S(1)} all-to-all(bf16[8,128,256]{1,2,0:T(8,128)(2,1)S(1)} %bitcast.106), channel_id=1, replica_groups=mesh['dp'=4,'seq'=8] {'seq'}, dimensions={0} | all-to-all | bytes 1048576 | tf_op jit(solution)/shard_map/all_to_all | solution.py:83
  214.7 8.1 %fusion.48 = f32[2048,2048]{1,0:T(8,128)} fusion(bf16[128,2048]{0,1:T(8,128)(2,1)S(1)} %bitcast.91, bf16[1,128,2048]{2,1,0:T(8,128)(2,1)S(1)} %copy-done), kind=kOutput, calls=%fused_computation.40 | convolution fusion | flops 1073741824 | bytes 17825792 | tf_op jit(solution)/shard_map/dot_general | solution.py:118
  222.8 0.7 copy-done.4
  223.5 6.8 %multiply_convert_fusion = bf16[2,8,128,1024]{2,3,1,0:T(8,128)(2,1)S(1)} fusion(f32[2,8,128]{2,1,0:T(8,128)S(1)} %copy.128, f32[2,8,128,1024]{2,3,1,0:T(8,128)} %get-tuple-element.11, f32[2,8,128]{2,1,0:T(8,128)S(1)} %get-tuple-element.10, bf16[8,1024,2,128]{3,1,0,2:T(8,128)(2,1)} %bitcast.96, bf16[8,128,2,128]{1,3,2,0:T(8,128)(2,1)S(1)} %bitcast.97), kind=kOutput, calls=%fused_computation.11 | convolution fusion | flops 547356672 | bytes 17317888 | tf_op jit(solution)/shard_map/iqhd,ikhd->hiqk/dot_general | solution.py:40
  230.4 2.2 fusion.35
  232.6 4.9 %all-to-all-start.5 = ((bf16[8,128,256]{1,2,0:T(8,128)(2,1)}), bf16[8,128,256]{1,2,0:T(8,128)(2,1)S(1)}, u32[]{:S(2)}, u32[]{:S(2)}) async-start(bf16[8,128,256]{1,2,0:T(8,128)(2,1)} %bitcast.29), calls=%async_computation.5 | async-start | bytes 1048576 | tf_op jit(solution)/shard_map/all_to_all | solution.py:106
  237.4 3.5 fusion.26
  240.9 0.8 copy.104
  241.7 7.5 %fusion.40 = bf16[8,128,2,128]{3,0,2,1:T(8,128)(2,1)S(1)} fusion(f32[64,128,2,128]{3,1,0,2:T(8,128)S(1)} %bitcast.88, s32[64]{0:T(128)S(1)} %eq.15), kind=kOutput, calls=%fused_computation.35 | convolution fusion | flops 201589248 | bytes 8913152 | tf_op jit(solution)/shard_map/ja,aqhd->jqhd/dot_general | solution.py:52
  249.2 0.5 copy.106
  249.7 1.0 copy.107
  250.7 8.0 %all-to-all-start.6 = ((bf16[8,128,256]{2,1,0:T(8,128)(2,1)}), bf16[8,128,256]{2,1,0:T(8,128)(2,1)S(1)}, u32[]{:S(2)}, u32[]{:S(2)}) async-start(bf16[8,128,256]{2,1,0:T(8,128)(2,1)} %copy.107), calls=%async_computation.6 | async-start | bytes 1048576 | tf_op jit(solution)/shard_map/all_to_all | solution.py:109
  258.7 6.7 %fusion.23 = f32[8,1024,2,128]{1,3,2,0:T(8,128)} fusion(bf16[8,128,2,128]{1,3,2,0:T(8,128)(2,1)S(1)} %bitcast.98, bf16[2,8,128,1024]{2,3,1,0:T(8,128)(2,1)} %fusion.22), kind=kOutput, calls=%fused_computation.28 | convolution fusion | flops 536870912 | bytes 13107200 | tf_op jit(solution)/shard_map/hiqk,iqhd->ikhd/dot_general | solution.py:37
  265.4 8.8 %copy.110 = f32[8,1024,2,128]{3,1,0,2:T(8,128)} copy(f32[8,1024,2,128]{1,3,2,0:T(8,128)} %fusion.23) | data formatting | bytes 16777216 | tf_op jit(solution)/shard_map/hiqk,iqhd->ikhd/transpose | solution.py:37
  274.2 10.6 %fusion.43 = bf16[8,128,2,128]{3,0,2,1:T(8,128)(2,1)S(1)} fusion(f32[64,128,2,128]{3,1,0,2:T(8,128)} %bitcast.87, s32[64]{0:T(128)S(1)} %eq.15), kind=kOutput, calls=%fused_computation.36 | convolution fusion | flops 201589248 | bytes 8913152 | tf_op jit(solution)/shard_map/ja,aqhd->jqhd/dot_general | solution.py:58
  284.7 0.5 copy.112
  285.2 1.0 copy.113
  286.2 4.4 %all-to-all-start.7 = ((bf16[8,128,256]{2,1,0:T(8,128)(2,1)}), bf16[8,128,256]{2,1,0:T(8,128)(2,1)S(1)}, u32[]{:S(2)}, u32[]{:S(2)}) async-start(bf16[8,128,256]{2,1,0:T(8,128)(2,1)} %copy.113), calls=%async_computation.7 | async-start | bytes 1048576 | tf_op jit(solution)/shard_map/all_to_all | solution.py:112
  290.6 1.0 copy.142
  291.9 1.0 copy.115
  292.9 11.3 %all-to-all-done.7 = bf16[8,128,256]{2,1,0:T(8,128)(2,1)S(1)} async-done(((bf16[8,128,256]{2,1,0:T(8,128)(2,1)}), bf16[8,128,256]{2,1,0:T(8,128)(2,1)S(1)}, u32[]{:S(2)}, u32[]{:S(2)}) %all-to-all-start.7) | async-done | bytes 524320 | tf_op jit(solution)/shard_map/all_to_all | solution.py:112
  304.5 1.0 copy.116
  305.5 5.6 %fusion.29 = bf16[1,128,2048]{2,1,0:T(8,128)(2,1)} fusion(bf16[128,2048]{0,1:T(8,128)(2,1)S(1)} %bitcast.92, bf16[2048,2048]{1,0:T(8,128)(2,1)} %all-gather.2.cloned.1.call-done), kind=kOutput, calls=%fused_computation.32 | convolution fusion | flops 1074003968 | bytes 9437184 | tf_op jit(solution)/shard_map/dot_general | solution.py:88
  311.1 108.2 %reduce-scatter.2.cloned.1.call-done = f32[64,2048]{1,0:T(8,128)} async-done(((f32[2048,2048]{1,0:T(8,128)}), f32[64,2048]{1,0:T(8,128)}) %reduce-scatter.2.cloned.1.call-update) | async-done | bytes 524304 | tf_op jit(solution)/shard_map/reduce_scatter | solution.py:117
  (24 shorter events, 0.8 us)
Async XLA Ops:
  7.2 153.3 %copy-start = (bf16[1,128,2048]{2,1,0:T(8,128)(2,1)S(1)}, bf16[1,128,2048]{2,1,0:T(8,128)(2,1)}, u32[]{:S(2)}) copy-start(bf16[1,128,2048]{2,1,0:T(8,128)(2,1)} %param.13) | copy-start | bytes 1572868
  7.2 153.3 %all-gather.2.cloned.1.call-start = ((), (), s32[]{:S(2)}) async-start(), calls=%async_computation.9 | async-start | bytes 10485760 | tf_op jit(solution)/shard_map/all_gather | solution.py:90
  10.0 12.5 %all-to-all-start.1 = ((bf16[128,8,256]{0,2,1:T(8,128)(2,1)}), bf16[128,8,256]{0,2,1:T(8,128)(2,1)S(1)}, u32[]{:S(2)}, u32[]{:S(2)}) async-start(bf16[128,8,256]{0,2,1:T(8,128)(2,1)} %bitcast.8), calls=%async_computation.1 | async-start | bytes 1048576 | tf_op jit(solution)/shard_map/all_to_all | solution.py:70
  22.5 16.5 %all-to-all-start.2 = ((bf16[128,8,256]{0,2,1:T(8,128)(2,1)}), bf16[128,8,256]{0,2,1:T(8,128)(2,1)S(1)}, u32[]{:S(2)}, u32[]{:S(2)}) async-start(bf16[128,8,256]{0,2,1:T(8,128)(2,1)} %bitcast.12), calls=%async_computation.2 | async-start | bytes 1048576 | tf_op jit(solution)/shard_map/all_to_all | solution.py:69
  39.0 128.7 %all-to-all-start = ((bf16[128,8,256]{0,2,1:T(8,128)(2,1)}), bf16[128,8,256]{0,2,1:T(8,128)(2,1)S(1)}, u32[]{:S(2)}, u32[]{:S(2)}) async-start(bf16[128,8,256]{0,2,1:T(8,128)(2,1)} %bitcast.2), calls=%async_computation | async-start | bytes 1048576 | tf_op jit(solution)/shard_map/all_to_all | solution.py:71
  167.7 18.7 %all-to-all-start.4 = ((bf16[128,8,256]{0,2,1:T(8,128)(2,1)}), bf16[128,8,256]{0,2,1:T(8,128)(2,1)S(1)}, u32[]{:S(2)}, u32[]{:S(2)}) async-start(bf16[128,8,256]{0,2,1:T(8,128)(2,1)} %bitcast.22), calls=%async_computation.4 | async-start | bytes 1048576 | tf_op jit(solution)/shard_map/all_to_all | solution.py:99
  172.0 247.3 %reduce-scatter.2.cloned.1.call-start = ((), (), s32[]{:S(2)}) async-start(), calls=%async_computation.10 | async-start | bytes 17301504 | tf_op jit(solution)/shard_map/reduce_scatter | solution.py:117
  222.8 0.7 copy-start.4
  223.5 6.8 %copy-start.2 = (bf16[64,128,2,128]{3,1,0,2:T(8,128)(2,1)S(1)}, bf16[64,128,2,128]{3,1,0,2:T(8,128)(2,1)}, u32[]{:S(2)}) copy-start(bf16[64,128,2,128]{3,1,0,2:T(8,128)(2,1)} %copy.91) | copy-start | bytes 12582916
  230.4 2.2 copy-start.3
  232.6 18.1 %all-to-all-start.5 = ((bf16[8,128,256]{1,2,0:T(8,128)(2,1)}), bf16[8,128,256]{1,2,0:T(8,128)(2,1)S(1)}, u32[]{:S(2)}, u32[]{:S(2)}) async-start(bf16[8,128,256]{1,2,0:T(8,128)(2,1)} %bitcast.29), calls=%async_computation.5 | async-start | bytes 1048576 | tf_op jit(solution)/shard_map/all_to_all | solution.py:106
  250.7 35.5 %all-to-all-start.6 = ((bf16[8,128,256]{2,1,0:T(8,128)(2,1)}), bf16[8,128,256]{2,1,0:T(8,128)(2,1)S(1)}, u32[]{:S(2)}, u32[]{:S(2)}) async-start(bf16[8,128,256]{2,1,0:T(8,128)(2,1)} %copy.107), calls=%async_computation.6 | async-start | bytes 1048576 | tf_op jit(solution)/shard_map/all_to_all | solution.py:109
  286.2 18.0 %all-to-all-start.7 = ((bf16[8,128,256]{2,1,0:T(8,128)(2,1)}), bf16[8,128,256]{2,1,0:T(8,128)(2,1)S(1)}, u32[]{:S(2)}, u32[]{:S(2)}) async-start(bf16[8,128,256]{2,1,0:T(8,128)(2,1)} %copy.113), calls=%async_computation.7 | async-start | bytes 1048576 | tf_op jit(solution)/shard_map/all_to_all | solution.py:112
  304.5 114.8 %copy-start.1 = (bf16[1,128,2048]{2,1,0:T(8,128)(2,1)S(1)}, bf16[1,128,2048]{2,1,0:T(8,128)(2,1)}, u32[]{:S(2)}) copy-start(bf16[1,128,2048]{2,1,0:T(8,128)(2,1)} %param.13) | copy-start | bytes 1572868
Sparse Core Ops, SparseCore 0:
  9.6 150.8 all-gather.1
  222.9 196.3 reduce-scatter.1
where the time goes:
time: 433 us; the launch traced here: 427 us
  waiting for transfers between devices  234 us (54%)
  matrix products  65.5 us (15%)
  local copies, waits for them, and re-layouts  40.1 us (9%)
  starting transfers between devices  34.9 us (8%)
  blocking collectives  23.3 us (5%)
  between operations  14.6 us (3%)
  other arithmetic  14.2 us (3%)
    reduce_scatter x1, waiting for transfers between devices, local(): lax.psum_scatter(lax.dot_general(columns, cotangent, (((0,), (0,)), ((),...  108 us
    all_gather x1, waiting for transfers between devices, local(): lax.all_gather(out_weight, 'dp', axis=0, tiled=True)  107 us
    all_to_all x1, blocking collectives, local(): lax.all_to_all(attended.reshape(length, heads * HD), 'seq', split_axis=0,...  23.3 us
    all_to_all x1, waiting for transfers between devices, local(): lax.all_to_all(value_grad.reshape(length, heads * HD), 'seq', split_axis=...  11.3 us
    dot_general x1, matrix products, backward(): jnp.einsum('ja,aqhd->jqhd', member, value_part.reshape(blocks * NBR, BLK,...  10.6 us
    unnamed x15, local copies, waits for them, and re-layouts  8.83 us
    transpose x1, local copies, waits for them, and re-layouts, backward(): jnp.einsum('hiqk,iqhd->ikhd', prob_bf, grad_blk, preferred_element_type=j...  8.78 us
  transfers between devices with their start and end apart: 9, of which 4 were waited for; matrix products, arithmetic and copies ran while one was open for 25% of the time, Pallas kernels for 0%

commit v1 on v0

--- a/solution.py
+++ b/solution.py
@@ -1,11 +1,60 @@
+import functools
+
 import jax
 import jax.numpy as jnp
 from jax import lax
+from jax.experimental import pallas as pl
+from jax.experimental.pallas import tpu as pltpu
 from jax.sharding import PartitionSpec as P
 
 HD = 128
 BLK = 128
 NBR = 8
+F32 = jnp.float32
+BF16 = jnp.bfloat16
+NN = (((1,), (0,)), ((), ()))
+NT = (((1,), (1,)), ((), ()))
+TN = (((0,), (0,)), ((), ()))
+LOG2E = 1.4426950408889634
+DEAD = -1e30
+VMEM = pl.BlockSpec(memory_space=pltpu.VMEM)
+SMEM = pl.BlockSpec(memory_space=pltpu.SMEM)
+ANY = pl.BlockSpec(memory_space=pl.ANY)
+MIB = 1 << 20
+
+
+def mm(a, b, dims=NN):
+    return lax.dot_general(a, b, dims, preferred_element_type=F32)
+
+
+def sds(shape, dtype):
+    return jax.ShapeDtypeStruct(shape, dtype)
+
+
+def call(kernel, ins, outs, scratch=(), flops=0, moved=0, vmem=24):
+    specs = [spec for spec, _ in ins]
+    return pl.pallas_call(
+        kernel,
+        out_shape=tuple(shape for _, shape in outs),
+        in_specs=specs,
+        out_specs=tuple(spec for spec, _ in outs),
+        scratch_shapes=list(scratch),
+        compiler_params=pltpu.CompilerParams(vmem_limit_bytes=vmem * MIB),
+        cost_estimate=pl.CostEstimate(flops=flops, bytes_accessed=moved, transcendentals=0),
+    )(*[arg for _, arg in ins])
+
+
+def col_of(dev, g, pairs, per):
+    core = dev % 2
+    return pl.multiple_of(((core * per + g) * pairs + dev // 2) * HD, HD)
+
+
+def copies(pairs_of_refs, sems):
+    handles = [pltpu.make_async_copy(src, dst, sems.at[n]) for n, (src, dst) in enumerate(pairs_of_refs)]
+    for handle in handles:
+        handle.start()
+    for handle in handles:
+        handle.wait()
 
 
 def attend(query_blk, key_blk, value_blk, links, live_count):
@@ -131,6 +180,345 @@
     )
 
 
+def prep_kernel(n, per, q_ref, k_ref, v_ref, c_ref, w_ref, *rest):
+    qkv, (same, other, wsend, sems) = rest[:n], rest[n:]
+    s = lax.axis_index("seq")
+    core = s % 2
+    half = c_ref.shape[2] // 2
+    moves = []
+    for j in range(n):
+        dev = s ^ j
+        for t, src in enumerate((q_ref, k_ref, v_ref)):
+            for g in range(per):
+                col = col_of(dev, g, n // 2, per)
+                moves.append((src.at[0, :, pl.ds(col, HD)], qkv[j].at[t, :, pl.ds(g * HD, HD)]))
+    mine = pl.multiple_of(core * half, half)
+    theirs = pl.multiple_of((1 - core) * half, half)
+    moves.append((c_ref.at[0, :, pl.ds(mine, half)], same))
+    moves.append((c_ref.at[0, :, pl.ds(theirs, half)], other))
+    row = pl.multiple_of((s // 2) * HD, HD)
+    moves.append((w_ref.at[pl.ds(row, HD), pl.ds(mine, half)], wsend))
+    copies(moves, sems)
+
+
+def forward_kernel(n, per, adj_ref, cnt_ref, *rest):
+    qkv = rest[:n]
+    attn_ref, swap_ref, attn_t_ref, lse_ref, bias_ref = rest[n : n + 5]
+    keys, vals_t, score, expo = rest[n + 5 :]
+    s = lax.axis_index("seq")
+    length = n * BLK
+    scale = HD**-0.5 * LOG2E
+    place = lax.broadcasted_iota(jnp.int32, (n, BLK), 0)
+    for i in range(n):
+        block = s ^ i
+        count = cnt_ref[0, block]
+        bias = jnp.full((n, BLK), DEAD, F32)
+        for slot in range(NBR):
+            j = jnp.where(slot < count, adj_ref[0, block, slot] ^ s, n)
+            bias = jnp.where(place == j, 0.0, bias)
+        bias_ref[:, i * BLK : (i + 1) * BLK] = bias
+    tile = 2 * BLK
+    for g in range(per):
+        lanes = slice(g * HD, (g + 1) * HD)
+        for j in range(n):
+            rows = slice(j * BLK, (j + 1) * BLK)
+            keys[g, rows, :] = qkv[j][1, :, lanes]
+            vals_t[g, :, rows] = qkv[j][2, :, lanes].T
+        for t in range(length // tile):
+            cols = slice(t * tile, (t + 1) * tile)
+            query = jnp.concatenate([qkv[2 * t][0, :, lanes], qkv[2 * t + 1][0, :, lanes]], axis=0)
+            highest = jnp.full((1, tile), -jnp.inf, F32)
+            for j in range(n):
+                rows = slice(j * BLK, (j + 1) * BLK)
+                part = mm(keys[g, rows, :], query, NT) * scale + bias_ref[j : j + 1, cols]
+                score[rows, :] = part
+                highest = jnp.maximum(highest, jnp.max(part, axis=0, keepdims=True))
+            total = jnp.zeros((1, tile), F32)
+            for j in range(n):
+                rows = slice(j * BLK, (j + 1) * BLK)
+                part = jnp.exp2(score[rows, :] - highest)
+                total = total + jnp.sum(part, axis=0, keepdims=True)
+                expo[rows, :] = part.astype(BF16)
+            att = (mm(vals_t[g], expo[...]) * (1.0 / total)).astype(BF16)
+            attn_t_ref[g, :, cols] = att
+            lse_ref[g : g + 1, cols] = highest + jnp.log2(total)
+            first, second = att[:, :BLK].T, att[:, BLK:].T
+            base = t * tile
+            attn_ref[base : base + BLK, lanes] = first
+            attn_ref[base + BLK : base + tile, lanes] = second
+            swap_ref[base : base + BLK, lanes] = second
+            swap_ref[base + BLK : base + tile, lanes] = first
+
+
+def grad_attn_kernel(n, per, *rest):
+    cot = rest[:n]
+    wts = rest[n : n + 2 * per]
+    own_ref, send_ref, w_out, cot_out = rest[n + 2 * per :]
+    core = lax.axis_index("seq") % 2
+    z = lax.axis_index("dp")
+    for jz in range(2 * per):
+        slot = (z ^ jz) ^ (per * core)
+        w_out[pl.ds(pl.multiple_of(slot * HD, HD), HD), :] = wts[jz][...]
+    for j in range(n):
+        cot_out[j * BLK : (j + 1) * BLK, :] = cot[j][...]
+    mine = per * HD
+    for t in range(n // 2):
+        base = 2 * t * BLK
+        part = mm(w_out[...], cot_out[base : base + 2 * BLK, :], NT)
+        own_ref[:, base : base + 2 * BLK] = part[:mine]
+        send_ref[:, base : base + BLK] = part[mine:, BLK:].astype(BF16)
+        send_ref[:, base + BLK : base + 2 * BLK] = part[mine:, :BLK].astype(BF16)
+
+
+def backward_kernel(n, per, *rest):
+    qkv = rest[:n]
+    attn_t_ref, lse_ref, bias_ref, own_ref, recv_ref = rest[n : n + 5]
+    outs = rest[n + 5 : 2 * n + 5]
+    queries, keys_t, grad, delta, probs, dscores, dq_t = rest[2 * n + 5 :]
+    scale = HD**-0.5
+    tile = 2 * BLK
+    length = n * BLK
+    for g in range(per):
+        lanes = slice(g * HD, (g + 1) * HD)
+        grad_t = (own_ref[lanes, :] + recv_ref[lanes, :].astype(F32)).astype(BF16)
+        grad[g] = grad_t
+        delta[g : g + 1, :] = jnp.sum(
+            grad_t.astype(F32) * attn_t_ref[g].astype(F32), axis=0, keepdims=True
+        )
+        for j in range(n):
+            rows = slice(j * BLK, (j + 1) * BLK)
+            queries[g, rows, :] = qkv[j][0, :, lanes]
+            keys_t[g, :, rows] = qkv[j][1, :, lanes].T
+        for t in range(length // tile):
+            key = jnp.concatenate([qkv[2 * t][1, :, lanes], qkv[2 * t + 1][1, :, lanes]], axis=0)
+            value = jnp.concatenate([qkv[2 * t][2, :, lanes], qkv[2 * t + 1][2, :, lanes]], axis=0)
+            for u in range(length // tile):
+                cols = slice(u * tile, (u + 1) * tile)
+                score = mm(key, queries[g, cols, :], NT)
+                dprob = mm(value, grad[g, :, cols])
+                lse = lse_ref[g : g + 1, cols]
+                dlt = delta[g : g + 1, cols]
+                for b in range(2):
+                    rows = slice(b * BLK, (b + 1) * BLK)
+                    shift = bias_ref[2 * t + b : 2 * t + b + 1, cols] - lse
+                    prob = jnp.exp2(score[rows] * (scale * LOG2E) + shift)
+                    probs[rows, cols] = prob.astype(BF16)
+                    dscores[rows, cols] = (prob * (dprob[rows] - dlt)).astype(BF16)
+            dvalue = mm(probs[...], grad[g], NT).astype(BF16)
+            dkey = (mm(dscores[...], queries[g]) * scale).astype(BF16)
+            for b in range(2):
+                rows = slice(b * BLK, (b + 1) * BLK)
+                outs[2 * t + b][1, :, lanes] = dkey[rows]
+                outs[2 * t + b][2, :, lanes] = dvalue[rows]
+            part = mm(keys_t[g, :, t * tile : (t + 1) * tile], dscores[...])
+            if t == 0:
+                dq_t[...] = part
+            else:
+                dq_t[...] += part
+        for j in range(n):
+            rows = slice(j * BLK, (j + 1) * BLK)
+            outs[j][0, :, lanes] = (dq_t[:, rows].T * scale).astype(BF16)
+
+
+def out_kernel(n, attn_ref, recv_ref, w_ref, *outs):
+    tile = 2 * BLK
+    half = attn_ref.shape[1]
+    for t in range(n // 2):
+        rows = slice(t * tile, (t + 1) * tile)
+        part = mm(attn_ref[rows, :], w_ref[:half, :]) + mm(recv_ref[rows, :], w_ref[half:, :])
+        outs[t][...] = part.astype(outs[t].dtype)
+
+
+def weight_kernel(nz, attn_t_ref, recv_ref, cot_ref, *rest):
+    outs, grads = rest[:nz], rest[nz]
+    core = lax.axis_index("seq") % 2
+    z = lax.axis_index("dp")
+    per = nz // 2
+    for g in range(per):
+        grads[g] = mm(attn_t_ref[g], cot_ref[...])
+        recv = recv_ref[:, g * HD : (g + 1) * HD].T
+        grads[per + g] = mm(recv, cot_ref[...])
+    for jz in range(nz):
+        slot = (z ^ jz) ^ (per * core)
+        outs[jz][...] = grads[slot].astype(outs[jz].dtype)
+
+
+def out_sum_kernel(own_ref, *rest):
+    parts, (keep_ref, send_ref) = rest[:-2], rest[-2:]
+    total = own_ref[...]
+    for part in parts:
+        total = total + part[...].astype(F32)
+    total = total.astype(BF16)
+    keep_ref[...] = total[:BLK]
+    send_ref[...] = total[BLK:]
+
+
+def weight_sum_kernel(own_ref, *rest):
+    parts, (keep_ref, send_ref) = rest[:-2], rest[-2:]
+    total = own_ref[...]
+    for part in parts:
+        total = total + part[...].astype(F32)
+    half = total.shape[0] // 2
+    core = lax.axis_index("seq") % 2
+    keep_ref[...] = jnp.where(core == 0, total[:half], total[half:])
+    send_ref[...] = jnp.where(core == 0, total[half:], total[:half])
+
+
+def join_kernel(keep_ref, recv_ref, out_ref):
+    core = lax.axis_index("seq") % 2
+    half = keep_ref.shape[1]
+    lead = (0,) if len(out_ref.shape) == 3 else ()
+    keep, recv = keep_ref[...], recv_ref[...]
+    out_ref[lead + (slice(None), slice(0, half))] = jnp.where(core == 0, keep, recv)
+    out_ref[lead + (slice(None), slice(half, 2 * half))] = jnp.where(core == 0, recv, keep)
+
+
+def place_kernel(n, per, *rest):
+    parts, outs, sems = rest[:n], rest[n : n + 3], rest[n + 3]
+    s = lax.axis_index("seq")
+    moves = []
+    for j in range(n):
+        for t in range(3):
+            for g in range(per):
+                col = col_of(s ^ j, g, n // 2, per)
+                moves.append((parts[j].at[t, :, pl.ds(g * HD, HD)], outs[t].at[0, :, pl.ds(col, HD)]))
+    copies(moves, sems)
+
+
+def paired(n, nz, queries, key_rows, values, adjacency, counts, out_weight, out_cotangent):
+    per = nz // 2
+    length = n * BLK
+    wide = queries.shape[2]
+    half = wide // 2
+    heads = per * HD
+
+    def to(x, j):
+        return lax.ppermute(x, "seq", [(i, i ^ j) for i in range(n)])
+
+    def to_z(x, j):
+        return lax.ppermute(x, "dp", [(i, i ^ j) for i in range(nz)])
+
+    chunk = sds((3, BLK, heads), BF16)
+    piece = sds((BLK, half), BF16)
+    prep = call(
+        functools.partial(prep_kernel, n, per),
+        [(ANY, x) for x in (queries, key_rows, values, out_cotangent, out_weight)],
+        [(ANY, chunk)] * n + [(ANY, piece)] * 2 + [(ANY, sds((HD, half), BF16))],
+        [pltpu.SemaphoreType.DMA((3 * n * per + 3,))],
+        moved=8 * MIB,
+    )
+    qkv = [prep[0]] + [to(prep[j], j) for j in range(1, n)]
+    same, other, wsend = prep[n:]
+    wts = [wsend] + [to_z(wsend, j) for j in range(1, nz)]
+    cot = [same] + [to(other if j % 2 else same, j) for j in range(1, n)]
+
+    attn, swap, attn_t, lse, bias = call(
+        functools.partial(forward_kernel, n, per),
+        [(SMEM, adjacency), (SMEM, counts)] + [(VMEM, x) for x in qkv],
+        [
+            (VMEM, sds((length, heads), BF16)),
+            (VMEM, sds((length, heads), BF16)),
+            (VMEM, sds((per, HD, length), BF16)),
+            (VMEM, sds((per, length), F32)),
+            (VMEM, sds((n, length), F32)),
+        ],
+        [
+            pltpu.VMEM((per, length, HD), BF16),
+            pltpu.VMEM((per, HD, length), BF16),
+            pltpu.VMEM((length, 2 * BLK), F32),
+            pltpu.VMEM((length, 2 * BLK), BF16),
+        ],
+        flops=4 * per * length * length * HD,
+        moved=4 * MIB,
+    )
+    attn_recv = to(swap, 1)
+
+    grad_own, grad_send, w_rows, cot_rows = call(
+        functools.partial(grad_attn_kernel, n, per),
+        [(VMEM, x) for x in cot + wts],
+        [
+            (VMEM, sds((heads, length), F32)),
+            (VMEM, sds((heads, length), BF16)),
+            (VMEM, sds((2 * heads, half), BF16)),
+            (VMEM, sds((length, half), BF16)),
+        ],
+        flops=4 * length * heads * half,
+        moved=8 * MIB,
+    )
+    grad_recv = to(grad_send, 1)
+
+    out_parts = call(
+        functools.partial(out_kernel, n),
+        [(VMEM, attn), (VMEM, attn_recv), (VMEM, w_rows)],
+        [(VMEM, sds((2 * BLK, half), BF16 if t else F32)) for t in range(n // 2)],
+        flops=4 * length * heads * half,
+        moved=6 * MIB,
+    )
+    out_recv = [to(out_parts[t], 2 * t) for t in range(1, n // 2)]
+
+    grads = call(
+        functools.partial(backward_kernel, n, per),
+        [(VMEM, x) for x in qkv + [attn_t, lse, bias, grad_own, grad_recv]],
+        [(VMEM, chunk)] * n,
+        [
+            pltpu.VMEM((per, length, HD), BF16),
+            pltpu.VMEM((per, HD, length), BF16),
+            pltpu.VMEM((per, HD, length), BF16),
+            pltpu.VMEM((per, length), F32),
+            pltpu.VMEM((2 * BLK, length), BF16),
+            pltpu.VMEM((2 * BLK, length), BF16),
+            pltpu.VMEM((HD, length), F32),
+        ],
+        flops=10 * per * length * length * HD,
+        moved=8 * MIB,
+    )
+    back = [grads[0]] + [to(grads[j], j) for j in range(1, n)]
+
+    w_parts = call(
+        functools.partial(weight_kernel, nz),
+        [(VMEM, attn_t), (VMEM, attn_recv), (VMEM, cot_rows)],
+        [(VMEM, sds((HD, half), BF16 if j else F32)) for j in range(nz)],
+        [pltpu.VMEM((nz, HD, half), F32)],
+        flops=4 * length * heads * half,
+        moved=6 * MIB,
+    )
+    w_recv = [to_z(w_parts[j], j) for j in range(1, nz)]
+
+    out_keep, out_send = call(
+        out_sum_kernel,
+        [(VMEM, x) for x in [out_parts[0]] + out_recv],
+        [(VMEM, sds((BLK, half), BF16))] * 2,
+        moved=3 * MIB,
+    )
+    (layer_out,) = call(
+        join_kernel,
+        [(VMEM, out_keep), (VMEM, to(out_send, 1))],
+        [(VMEM, sds((1, BLK, wide), BF16))],
+        moved=MIB,
+    )
+    w_keep, w_send = call(
+        weight_sum_kernel,
+        [(VMEM, x) for x in [w_parts[0]] + w_recv],
+        [(VMEM, sds((HD // 2, half), F32))] * 2,
+        moved=2 * MIB,
+    )
+    (weight_grad,) = call(
+        join_kernel,
+        [(VMEM, w_keep), (VMEM, to(w_send, 1))],
+        [(VMEM, sds((HD // 2, wide), F32))],
+        moved=MIB,
+    )
+    token = sds((1, BLK, wide), BF16)
+    query_grad, key_grad, value_grad = call(
+        functools.partial(place_kernel, n, per),
+        [(ANY, x) for x in back],
+        [(ANY, token)] * 3,
+        [pltpu.SemaphoreType.DMA((3 * n * per,))],
+        moved=3 * MIB,
+    )
+    return layer_out, query_grad, key_grad, value_grad, weight_grad
+
+
 def solution(mesh):
     in_specs = (
         P("dp", "seq", None),
@@ -148,4 +536,13 @@
         P("dp", "seq", None),
         P(("dp", "seq"), None),
     )
-    return jax.shard_map(local, mesh=mesh, in_specs=in_specs, out_specs=out_specs, check_vma=False)
+    n, nz = mesh.shape["seq"], mesh.shape["dp"]
+
+    def body(queries, *rest):
+        heads = queries.shape[2] // HD
+        fits = queries.shape[1] == BLK and heads == nz * (n // 2)
+        if fits and n % 2 == 0 and nz % 2 == 0 and n & (n - 1) == 0 and nz & (nz - 1) == 0:
+            return paired(n, nz, queries, *rest)
+        return local(queries, *rest)
+
+    return jax.shard_map(body, mesh=mesh, in_specs=in_specs, out_specs=out_specs, check_vma=False)

time: 433 us -> 140 us (0.32)
  the two profiles are of different devices: /device:TPU:2 before, /device:TPU:17 now
where the time goes in v1:
time: 140 us
  waiting for transfers between devices  77.5 us (55%)
  starting transfers between devices  36.7 us (26%)
  Pallas kernels  19.3 us (14%)
  local copies, waits for them, and re-layouts  5.76 us (4%)
    ppermute x6, waiting for transfers between devices, to_z(): return lax.ppermute(x, 'dp', [(i, i ^ j) for i in range(nz)])  38.8 us
    ppermute x28, waiting for transfers between devices, to(): return lax.ppermute(x, 'seq', [(i, i ^ j) for i in range(n)])  38.7 us
    ppermute x28, starting transfers between devices, to(): return lax.ppermute(x, 'seq', [(i, i ^ j) for i in range(n)])  32.4 us
    pallas_call x11, Pallas kernels, call(): pl.pallas_call(kernel, out_shape=tuple((shape for _, shape in outs)), in_...  19.3 us
    unnamed x14, local copies, waits for them, and re-layouts  5.76 us
    ppermute x6, starting transfers between devices, to_z(): return lax.ppermute(x, 'dp', [(i, i ^ j) for i in range(nz)])  4.24 us
  transfers between devices with their start and end apart: 34, of which 17 were waited for; matrix products, arithmetic and copies ran while one was open for 0% of the time, Pallas kernels for 12%

profile of v1, /device:TPU:17, one launch (start us, length us, event | category | flops | bytes accessed | tf_op | source)
XLA Modules:
  0.0 140.0 jit_solution(977903366750674175)
XLA Ops:
  0.6 1.6 %copy-done = bf16[512,2048]{1,0:T(8,128)(2,1)S(1)} copy-done((bf16[512,2048]{1,0:T(8,128)(2,1)S(1)}, bf16[512,2048]{1,0:T(8,128)(2,1)}, u32[]{:S(2)}) %copy-start) | copy-done | bytes 2097176
  2.2 1.0 copy-done.1
  3.3 1.0 copy-done.2
  4.3 1.0 copy-done.3
  5.4 1.0 copy-done.4
  6.4 1.1 shard_map.110
  8.2 1.2 collective-permute-start.1
  10.0 1.3 collective-permute-start.10
  11.2 1.2 collective-permute-start.3
  13.2 1.5 %collective-permute-done.1.rest_2_ = bf16[3,128,256]{2,1,0:T(8,128)(2,1)S(1)} collective-permute-done((bf16[3,128,256]{2,1,0:T(8,128)(2,1)S(1)}, bf16[3,128,256]{2,1,0:T(8,128)(2,1)S(1)}, u32[]{:S(2)}, u32[]{:S(2)}) %collective-permute-start.1) | collective-permute-done | bytes 196640 | tf_op jit(solution)/shard_map/ppermute | solution.py:396
  14.7 2.2 %collective-permute-start.5 = (bf16[3,128,256]{2,1,0:T(8,128)(2,1)S(1)}, bf16[3,128,256]{2,1,0:T(8,128)(2,1)S(1)}, u32[]{:S(2)}, u32[]{:S(2)}) collective-permute-start(bf16[3,128,256]{2,1,0:T(8,128)(2,1)S(1)} %get-tuple-element.54), channel_id=1, source_target_pairs={{0,6},{1,7},{2,4},{3,5},{4,2},{5,3},{6,0},{7,1},{8,14},{9,15},{10,... | collective-permute-start | bytes 589832 | tf_op jit(solution)/shard_map/ppermute | solution.py:396
  16.9 3.0 %collective-permute-done.2.rest_3_ = bf16[3,128,256]{2,1,0:T(8,128)(2,1)S(1)} collective-permute-done((bf16[3,128,256]{2,1,0:T(8,128)(2,1)S(1)}, bf16[3,128,256]{2,1,0:T(8,128)(2,1)S(1)}, u32[]{:S(2)}, u32[]{:S(2)}) %collective-permute-start.2) | collective-permute-done | bytes 196640 | tf_op jit(solution)/shard_map/ppermute | solution.py:396
  19.8 1.5 %collective-permute-start.6 = (bf16[3,128,256]{2,1,0:T(8,128)(2,1)S(1)}, bf16[3,128,256]{2,1,0:T(8,128)(2,1)S(1)}, u32[]{:S(2)}, u32[]{:S(2)}) collective-permute-start(bf16[3,128,256]{2,1,0:T(8,128)(2,1)S(1)} %get-tuple-element.55), channel_id=1, source_target_pairs={{0,7},{1,6},{2,5},{3,4},{4,3},{5,2},{6,1},{7,0},{8,15},{9,14},{10,... | collective-permute-start | bytes 589832 | tf_op jit(solution)/shard_map/ppermute | solution.py:396
  22.4 1.7 %collective-permute-start.12 = (bf16[128,1024]{1,0:T(8,128)(2,1)S(1)}, bf16[128,1024]{1,0:T(8,128)(2,1)S(1)}, u32[]{:S(2)}, u32[]{:S(2)}) collective-permute-start(bf16[128,1024]{1,0:T(8,128)(2,1)S(1)} %get-tuple-element.59), channel_id=1, source_target_pairs={{0,5},{1,4},{2,7},{3,6},{4,1},{5,0},{6,3},{7,2},{8,13},{9,12},{10,... | collective-permute-start | bytes 786440 | tf_op jit(solution)/shard_map/ppermute | solution.py:396
  24.0 5.7 %collective-permute-done.5.rest_6_ = bf16[3,128,256]{2,1,0:T(8,128)(2,1)S(1)} collective-permute-done((bf16[3,128,256]{2,1,0:T(8,128)(2,1)S(1)}, bf16[3,128,256]{2,1,0:T(8,128)(2,1)S(1)}, u32[]{:S(2)}, u32[]{:S(2)}) %collective-permute-start.5) | collective-permute-done | bytes 196640 | tf_op jit(solution)/shard_map/ppermute | solution.py:396
  29.8 1.2 collective-permute-start.13
  30.9 3.7 %collective-permute-done.6.rest_7_ = bf16[3,128,256]{2,1,0:T(8,128)(2,1)S(1)} collective-permute-done((bf16[3,128,256]{2,1,0:T(8,128)(2,1)S(1)}, bf16[3,128,256]{2,1,0:T(8,128)(2,1)S(1)}, u32[]{:S(2)}, u32[]{:S(2)}) %collective-permute-start.6) | collective-permute-done | bytes 196640 | tf_op jit(solution)/shard_map/ppermute | solution.py:396
  34.6 0.8 collective-permute-start.14
  35.5 1.3 collective-permute-start.15
  36.8 4.9 %shard_map.111 = (bf16[1024,256]{1,0:T(8,128)(2,1)S(1)}, bf16[1024,256]{1,0:T(8,128)(2,1)S(1)}, bf16[2,128,1024]{2,1,0:T(8,128)(2,1)S(1)}, f32[2,1024]{1,0:T(2,128)S(1)}, f32[8,1024]{1,0:T(8,128)S(1)}) custom-call(s32[1,8,8]{2,1,0:T(8,128)S(1)} %copy-done.5, s32[1,8]{1,0:T(1,128)S(1)} %copy-done.6, bf16[3,128,256]{2,1,0:T(8,128)(2,1)S(1)} %get-tuple-element.48.rest_0_, ...), custom_call_target="tpu_custom_call" | custom-call | flops 1073741824 | bytes 4194304 | tf_op jit(solution)/shard_map/pallas_call | solution.py:36
  41.7 6.1 %collective-permute-done.11.rest_4_ = bf16[128,1024]{1,0:T(8,128)(2,1)S(1)} collective-permute-done((bf16[128,1024]{1,0:T(8,128)(2,1)S(1)}, bf16[128,1024]{1,0:T(8,128)(2,1)S(1)}, u32[]{:S(2)}, u32[]{:S(2)}) %collective-permute-start.11) | collective-permute-done | bytes 262176 | tf_op jit(solution)/shard_map/ppermute | solution.py:396
  47.9 3.4 %collective-permute-start.7 = (bf16[1024,256]{1,0:T(8,128)(2,1)S(1)}, bf16[1024,256]{1,0:T(8,128)(2,1)S(1)}, u32[]{:S(2)}, u32[]{:S(2)}) collective-permute-start(bf16[1024,256]{1,0:T(8,128)(2,1)S(1)} %get-tuple-element.57), channel_id=1, source_target_pairs={{0,1},{1,0},{2,3},{3,2},{4,5},{5,4},{6,7},{7,6},{8,9},{9,8},{10,11... | collective-permute-start | bytes 1572872 | tf_op jit(solution)/shard_map/ppermute | solution.py:396
  51.3 3.4 %collective-permute-done.12.rest_5_ = bf16[128,1024]{1,0:T(8,128)(2,1)S(1)} collective-permute-done((bf16[128,1024]{1,0:T(8,128)(2,1)S(1)}, bf16[128,1024]{1,0:T(8,128)(2,1)S(1)}, u32[]{:S(2)}, u32[]{:S(2)}) %collective-permute-start.12) | collective-permute-done | bytes 262176 | tf_op jit(solution)/shard_map/ppermute | solution.py:396
  54.8 2.4 %collective-permute-start.17 = (bf16[128,1024]{1,0:T(8,128)(2,1)S(1)}, bf16[128,1024]{1,0:T(8,128)(2,1)S(1)}, u32[]{:S(2)}, u32[]{:S(2)}) collective-permute-start(bf16[128,1024]{1,0:T(8,128)(2,1)S(1)} %get-tuple-element.60.rest_8_), channel_id=1, source_target_pairs={{0,24},{8,16},{16,8},{24,0},{1,25},{9,17},{17,9},{25,1},{2,26},{10... | collective-permute-start | bytes 786440 | tf_op jit(solution)/shard_map/ppermute | solution.py:399
  57.5 14.5 %collective-permute-done.16.rest_10_ = bf16[128,1024]{1,0:T(8,128)(2,1)S(1)} collective-permute-done((bf16[128,1024]{1,0:T(8,128)(2,1)S(1)}, bf16[128,1024]{1,0:T(8,128)(2,1)S(1)}, u32[]{:S(2)}, u32[]{:S(2)}) %collective-permute-start.16) | collective-permute-done | bytes 262176 | tf_op jit(solution)/shard_map/ppermute | solution.py:399
  72.0 8.4 %collective-permute-done.17.rest_11_ = bf16[128,1024]{1,0:T(8,128)(2,1)S(1)} collective-permute-done((bf16[128,1024]{1,0:T(8,128)(2,1)S(1)}, bf16[128,1024]{1,0:T(8,128)(2,1)S(1)}, u32[]{:S(2)}, u32[]{:S(2)}) %collective-permute-start.17) | collective-permute-done | bytes 262176 | tf_op jit(solution)/shard_map/ppermute | solution.py:399
  80.4 1.3 shard_map.112
  82.2 1.4 %shard_map.118 = (f32[128,1024]{1,0:T(8,128)S(1)}, bf16[128,1024]{1,0:T(8,128)(2,1)S(1)}, bf16[128,1024]{1,0:T(8,128)(2,1)S(1)}, bf16[128,1024]{1,0:T(8,128)(2,1)S(1)}) custom-call(bf16[2,128,1024]{2,1,0:T(8,128)(2,1)S(1)} %get-tuple-element.68.rest_8_.attn_t_ref, bf16[1024,256]{1,0:T(8,128)(2,1)S(1)} %collective-permute-done.7.recv_ref, ...), custom_call_target="tpu_custom_call" | custom-call | flops 1073741824 | bytes 6291456 | tf_op jit(solution)/shard_map/pallas_call | solution.py:36
  83.7 1.3 shard_map.113
  85.3 1.1 collective-permute-start.19
  86.4 1.3 collective-permute-start.20
  88.1 3.4 %collective-permute-done.30.rest_0_ = bf16[128,1024]{1,0:T(8,128)(2,1)S(1)} collective-permute-done((bf16[128,1024]{1,0:T(8,128)(2,1)S(1)}, bf16[128,1024]{1,0:T(8,128)(2,1)S(1)}, u32[]{:S(2)}, u32[]{:S(2)}) %collective-permute-start.30) | collective-permute-done | bytes 262176 | tf_op jit(solution)/shard_map/ppermute | solution.py:399
  91.6 5.6 %shard_map.116 = (bf16[3,128,256]{2,1,0:T(8,128)(2,1)S(1)}, bf16[3,128,256]{2,1,0:T(8,128)(2,1)S(1)}, bf16[3,128,256]{2,1,0:T(8,128)(2,1)S(1)}, bf16[3,128,256]{...) custom-call(bf16[3,128,256]{2,1,0:T(8,128)(2,1)S(1)} %get-tuple-elem, ...), custom_call_target="tpu_custom_call" | custom-call | flops 2684354560 | bytes 8388608 | tf_op jit(solution)/shard_map/pallas_call | solution.py:36
  97.2 6.5 %collective-permute-done.31.rest_1_ = bf16[128,1024]{1,0:T(8,128)(2,1)S(1)} collective-permute-done((bf16[128,1024]{1,0:T(8,128)(2,1)S(1)}, bf16[128,1024]{1,0:T(8,128)(2,1)S(1)}, u32[]{:S(2)}, u32[]{:S(2)}) %collective-permute-start.31) | collective-permute-done | bytes 262176 | tf_op jit(solution)/shard_map/ppermute | solution.py:399
  103.7 4.1 %collective-permute-start.23 = (bf16[3,128,256]{2,1,0:T(8,128)(2,1)S(1)}, bf16[3,128,256]{2,1,0:T(8,128)(2,1)S(1)}, u32[]{:S(2)}, u32[]{:S(2)}) collective-permute-start(bf16[3,128,256]{2,1,0:T(8,128)(2,1)S(1)} %get-tuple-element.74), channel_id=1, source_target_pairs={{0,1},{1,0},{2,3},{3,2},{4,5},{5,4},{6,7},{7,6},{8,9},{9,8},{10,11... | collective-permute-start | bytes 589832 | tf_op jit(solution)/shard_map/ppermute | solution.py:396
  107.7 6.0 %collective-permute-done.32.rest_2_ = bf16[128,1024]{1,0:T(8,128)(2,1)S(1)} collective-permute-done((bf16[128,1024]{1,0:T(8,128)(2,1)S(1)}, bf16[128,1024]{1,0:T(8,128)(2,1)S(1)}, u32[]{:S(2)}, u32[]{:S(2)}) %collective-permute-start.32) | collective-permute-done | bytes 262176 | tf_op jit(solution)/shard_map/ppermute | solution.py:399
  113.9 1.9 %collective-permute-start.25 = (bf16[3,128,256]{2,1,0:T(8,128)(2,1)S(1)}, bf16[3,128,256]{2,1,0:T(8,128)(2,1)S(1)}, u32[]{:S(2)}, u32[]{:S(2)}) collective-permute-start(bf16[3,128,256]{2,1,0:T(8,128)(2,1)S(1)} %get-tuple-element.76), channel_id=1, source_target_pairs={{0,3},{1,2},{2,1},{3,0},{4,7},{5,6},{6,5},{7,4},{8,11},{9,10},{10,... | collective-permute-start | bytes 589832 | tf_op jit(solution)/shard_map/ppermute | solution.py:396
  117.5 2.2 %collective-permute-done.24.rest_2_ = bf16[3,128,256]{2,1,0:T(8,128)(2,1)S(1)} collective-permute-done((bf16[3,128,256]{2,1,0:T(8,128)(2,1)S(1)}, bf16[3,128,256]{2,1,0:T(8,128)(2,1)S(1)}, u32[]{:S(2)}, u32[]{:S(2)}) %collective-permute-start.24) | collective-permute-done | bytes 196640 | tf_op jit(solution)/shard_map/ppermute | solution.py:396
  119.7 2.8 %collective-permute-start.27 = (bf16[3,128,256]{2,1,0:T(8,128)(2,1)S(1)}, bf16[3,128,256]{2,1,0:T(8,128)(2,1)S(1)}, u32[]{:S(2)}, u32[]{:S(2)}) collective-permute-start(bf16[3,128,256]{2,1,0:T(8,128)(2,1)S(1)} %get-tuple-element.78), channel_id=1, source_target_pairs={{0,5},{1,4},{2,7},{3,6},{4,1},{5,0},{6,3},{7,2},{8,13},{9,12},{10,... | collective-permute-start | bytes 589832 | tf_op jit(solution)/shard_map/ppermute | solution.py:396
  122.5 2.4 %collective-permute-done.25.rest_3_ = bf16[3,128,256]{2,1,0:T(8,128)(2,1)S(1)} collective-permute-done((bf16[3,128,256]{2,1,0:T(8,128)(2,1)S(1)}, bf16[3,128,256]{2,1,0:T(8,128)(2,1)S(1)}, u32[]{:S(2)}, u32[]{:S(2)}) %collective-permute-start.25) | collective-permute-done | bytes 196640 | tf_op jit(solution)/shard_map/ppermute | solution.py:396
  124.9 1.0 collective-permute-start.28
  125.9 1.0 collective-permute-start.29
  126.8 0.9 collective-permute-done.27.rest_5_
  127.7 4.8 %collective-permute-done.28.rest_6_ = bf16[3,128,256]{2,1,0:T(8,128)(2,1)S(1)} collective-permute-done((bf16[3,128,256]{2,1,0:T(8,128)(2,1)S(1)}, bf16[3,128,256]{2,1,0:T(8,128)(2,1)S(1)}, u32[]{:S(2)}, u32[]{:S(2)}) %collective-permute-start.28) | collective-permute-done | bytes 196640 | tf_op jit(solution)/shard_map/ppermute | solution.py:396
  132.5 4.2 %collective-permute-done.29.rest_7_ = bf16[3,128,256]{2,1,0:T(8,128)(2,1)S(1)} collective-permute-done((bf16[3,128,256]{2,1,0:T(8,128)(2,1)S(1)}, bf16[3,128,256]{2,1,0:T(8,128)(2,1)S(1)}, u32[]{:S(2)}, u32[]{:S(2)}) %collective-permute-start.29) | collective-permute-done | bytes 196640 | tf_op jit(solution)/shard_map/ppermute | solution.py:396
  136.7 1.5 %shard_map.117 = (bf16[1,128,2048]{2,1,0:T(8,128)(2,1)}, bf16[1,128,2048]{2,1,0:T(8,128)(2,1)}, bf16[1,128,2048]{2,1,0:T(8,128)(2,1)}) custom-call(bf16[3,128,256]{2,1,0:T(8,128)(2,1)S(1)} %get-tuple-element.73.rest_0_, bf16[3,128,256]{2,1,0:T(8,128)(2,1)S(1)} %collective-permute-done.23.rest_1_, bf16[3,128,256]{2,1,0:T(8,128)(2,1)S(1)} %collective-permute-done.24.rest_2_, ...), custom_call_target="tpu_custom_call" | custom-call | bytes 3145728 | tf_op jit(solution)/shard_map/pallas_call | solution.py:36
  138.3 0.9 shard_map.120
  139.1 0.9 shard_map.115
  (45 shorter events, 6.4 us)
Async XLA Ops:
  0.6 1.6 %copy-start = (bf16[512,2048]{1,0:T(8,128)(2,1)S(1)}, bf16[512,2048]{1,0:T(8,128)(2,1)}, u32[]{:S(2)}) copy-start(bf16[512,2048]{1,0:T(8,128)(2,1)} %w_ref.1) | copy-start | bytes 6291460
  2.2 1.0 copy-start.1
  3.3 1.0 copy-start.2
  4.3 1.0 copy-start.3
  5.4 1.0 copy-start.4
  6.4 30.4 %copy-start.5 = (s32[1,8,8]{2,1,0:T(8,128)S(1)}, s32[1,8,8]{2,1,0:T(8,128)}, u32[]{:S(2)}) copy-start(s32[1,8,8]{2,1,0:T(8,128)} %adj_ref.1) | copy-start | bytes 772
  6.4 30.4 %copy-start.6 = (s32[1,8]{1,0:T(1,128)S(1)}, s32[1,8]{1,0:T(1,128)}, u32[]{:S(2)}) copy-start(s32[1,8]{1,0:T(1,128)} %cnt_ref.1) | copy-start | bytes 100
  7.5 5.0 %collective-permute-start = (bf16[3,128,256]{2,1,0:T(8,128)(2,1)S(1)}, bf16[3,128,256]{2,1,0:T(8,128)(2,1)S(1)}, u32[]{:S(2)}, u32[]{:S(2)}) collective-permute-start(bf16[3,128,256]{2,1,0:T(8,128)(2,1)S(1)} %get-tuple-element.49), channel_id=1, source_target_pairs={{0,1},{1,0},{2,3},{3,2},{4,5},{5,4},{6,7},{7,6},{8,9},{9,8},{10,11... | collective-permute-start | bytes 589832 | tf_op jit(solution)/shard_map/ppermute | solution.py:396
  8.2 6.5 %collective-permute-start.1 = (bf16[3,128,256]{2,1,0:T(8,128)(2,1)S(1)}, bf16[3,128,256]{2,1,0:T(8,128)(2,1)S(1)}, u32[]{:S(2)}, u32[]{:S(2)}) collective-permute-start(bf16[3,128,256]{2,1,0:T(8,128)(2,1)S(1)} %get-tuple-element.50), channel_id=1, source_target_pairs={{0,2},{1,3},{2,0},{3,1},{4,6},{5,7},{6,4},{7,5},{8,10},{9,11},{10,... | collective-permute-start | bytes 589832 | tf_op jit(solution)/shard_map/ppermute | solution.py:396
  9.5 10.4 %collective-permute-start.2 = (bf16[3,128,256]{2,1,0:T(8,128)(2,1)S(1)}, bf16[3,128,256]{2,1,0:T(8,128)(2,1)S(1)}, u32[]{:S(2)}, u32[]{:S(2)}) collective-permute-start(bf16[3,128,256]{2,1,0:T(8,128)(2,1)S(1)} %get-tuple-element.51), channel_id=1, source_target_pairs={{0,3},{1,2},{2,1},{3,0},{4,7},{5,6},{6,5},{7,4},{8,11},{9,10},{10,... | collective-permute-start | bytes 589832 | tf_op jit(solution)/shard_map/ppermute | solution.py:396
  10.0 25.5 %collective-permute-start.10 = (bf16[128,1024]{1,0:T(8,128)(2,1)S(1)}, bf16[128,1024]{1,0:T(8,128)(2,1)S(1)}, u32[]{:S(2)}, u32[]{:S(2)}) collective-permute-start(bf16[128,1024]{1,0:T(8,128)(2,1)S(1)} %get-tuple-element.59), channel_id=1, source_target_pairs={{0,3},{1,2},{2,1},{3,0},{4,7},{5,6},{6,5},{7,4},{8,11},{9,10},{10,... | collective-permute-start | bytes 786440 | tf_op jit(solution)/shard_map/ppermute | solution.py:396
  11.2 10.2 %collective-permute-start.3 = (bf16[3,128,256]{2,1,0:T(8,128)(2,1)S(1)}, bf16[3,128,256]{2,1,0:T(8,128)(2,1)S(1)}, u32[]{:S(2)}, u32[]{:S(2)}) collective-permute-start(bf16[3,128,256]{2,1,0:T(8,128)(2,1)S(1)} %get-tuple-element.52), channel_id=1, source_target_pairs={{0,4},{1,5},{2,6},{3,7},{4,0},{5,1},{6,2},{7,3},{8,12},{9,13},{10,... | collective-permute-start | bytes 589832 | tf_op jit(solution)/shard_map/ppermute | solution.py:396
  12.5 9.9 %collective-permute-start.4 = (bf16[3,128,256]{2,1,0:T(8,128)(2,1)S(1)}, bf16[3,128,256]{2,1,0:T(8,128)(2,1)S(1)}, u32[]{:S(2)}, u32[]{:S(2)}) collective-permute-start(bf16[3,128,256]{2,1,0:T(8,128)(2,1)S(1)} %get-tuple-element.53), channel_id=1, source_target_pairs={{0,5},{1,4},{2,7},{3,6},{4,1},{5,0},{6,3},{7,2},{8,13},{9,12},{10,... | collective-permute-start | bytes 589832 | tf_op jit(solution)/shard_map/ppermute | solution.py:396
  14.7 15.0 %collective-permute-start.5 = (bf16[3,128,256]{2,1,0:T(8,128)(2,1)S(1)}, bf16[3,128,256]{2,1,0:T(8,128)(2,1)S(1)}, u32[]{:S(2)}, u32[]{:S(2)}) collective-permute-start(bf16[3,128,256]{2,1,0:T(8,128)(2,1)S(1)} %get-tuple-element.54), channel_id=1, source_target_pairs={{0,6},{1,7},{2,4},{3,5},{4,2},{5,3},{6,0},{7,1},{8,14},{9,15},{10,... | collective-permute-start | bytes 589832 | tf_op jit(solution)/shard_map/ppermute | solution.py:396
  19.8 14.8 %collective-permute-start.6 = (bf16[3,128,256]{2,1,0:T(8,128)(2,1)S(1)}, bf16[3,128,256]{2,1,0:T(8,128)(2,1)S(1)}, u32[]{:S(2)}, u32[]{:S(2)}) collective-permute-start(bf16[3,128,256]{2,1,0:T(8,128)(2,1)S(1)} %get-tuple-element.55), channel_id=1, source_target_pairs={{0,7},{1,6},{2,5},{3,4},{4,3},{5,2},{6,1},{7,0},{8,15},{9,14},{10,... | collective-permute-start | bytes 589832 | tf_op jit(solution)/shard_map/ppermute | solution.py:396
  21.4 26.5 %collective-permute-start.11 = (bf16[128,1024]{1,0:T(8,128)(2,1)S(1)}, bf16[128,1024]{1,0:T(8,128)(2,1)S(1)}, u32[]{:S(2)}, u32[]{:S(2)}) collective-permute-start(bf16[128,1024]{1,0:T(8,128)(2,1)S(1)} %get-tuple-element.58.rest_0_), channel_id=1, source_target_pairs={{0,4},{1,5},{2,6},{3,7},{4,0},{5,1},{6,2},{7,3},{8,12},{9,13},{10,... | collective-permute-start | bytes 786440 | tf_op jit(solution)/shard_map/ppermute | solution.py:396
  22.4 32.3 %collective-permute-start.12 = (bf16[128,1024]{1,0:T(8,128)(2,1)S(1)}, bf16[128,1024]{1,0:T(8,128)(2,1)S(1)}, u32[]{:S(2)}, u32[]{:S(2)}) collective-permute-start(bf16[128,1024]{1,0:T(8,128)(2,1)S(1)} %get-tuple-element.59), channel_id=1, source_target_pairs={{0,5},{1,4},{2,7},{3,6},{4,1},{5,0},{6,3},{7,2},{8,13},{9,12},{10,... | collective-permute-start | bytes 786440 | tf_op jit(solution)/shard_map/ppermute | solution.py:396
  29.8 25.0 %collective-permute-start.13 = (bf16[128,1024]{1,0:T(8,128)(2,1)S(1)}, bf16[128,1024]{1,0:T(8,128)(2,1)S(1)}, u32[]{:S(2)}, u32[]{:S(2)}) collective-permute-start(bf16[128,1024]{1,0:T(8,128)(2,1)S(1)} %get-tuple-element.58.rest_0_), channel_id=1, source_target_pairs={{0,6},{1,7},{2,4},{3,5},{4,2},{5,3},{6,0},{7,1},{8,14},{9,15},{10,... | collective-permute-start | bytes 786440 | tf_op jit(solution)/shard_map/ppermute | solution.py:396
  34.6 22.5 %collective-permute-start.14 = (bf16[128,1024]{1,0:T(8,128)(2,1)S(1)}, bf16[128,1024]{1,0:T(8,128)(2,1)S(1)}, u32[]{:S(2)}, u32[]{:S(2)}) collective-permute-start(bf16[128,1024]{1,0:T(8,128)(2,1)S(1)} %get-tuple-element.59), channel_id=1, source_target_pairs={{0,7},{1,6},{2,5},{3,4},{4,3},{5,2},{6,1},{7,0},{8,15},{9,14},{10,... | collective-permute-start | bytes 786440 | tf_op jit(solution)/shard_map/ppermute | solution.py:396
  35.5 21.7 %collective-permute-start.15 = (bf16[128,1024]{1,0:T(8,128)(2,1)S(1)}, bf16[128,1024]{1,0:T(8,128)(2,1)S(1)}, u32[]{:S(2)}, u32[]{:S(2)}) collective-permute-start(bf16[128,1024]{1,0:T(8,128)(2,1)S(1)} %get-tuple-element.60.rest_8_), channel_id=1, source_target_pairs={{0,8},{8,0},{16,24},{24,16},{1,9},{9,1},{17,25},{25,17},{2,10},{10... | collective-permute-start | bytes 786440 | tf_op jit(solution)/shard_map/ppermute | solution.py:399
  47.9 34.3 %collective-permute-start.7 = (bf16[1024,256]{1,0:T(8,128)(2,1)S(1)}, bf16[1024,256]{1,0:T(8,128)(2,1)S(1)}, u32[]{:S(2)}, u32[]{:S(2)}) collective-permute-start(bf16[1024,256]{1,0:T(8,128)(2,1)S(1)} %get-tuple-element.57), channel_id=1, source_target_pairs={{0,1},{1,0},{2,3},{3,2},{4,5},{5,4},{6,7},{7,6},{8,9},{9,8},{10,11... | collective-permute-start | bytes 1572872 | tf_op jit(solution)/shard_map/ppermute | solution.py:396
  54.7 17.3 %collective-permute-start.16 = (bf16[128,1024]{1,0:T(8,128)(2,1)S(1)}, bf16[128,1024]{1,0:T(8,128)(2,1)S(1)}, u32[]{:S(2)}, u32[]{:S(2)}) collective-permute-start(bf16[128,1024]{1,0:T(8,128)(2,1)S(1)} %get-tuple-element.60.rest_8_), channel_id=1, source_target_pairs={{0,16},{8,24},{16,0},{24,8},{1,17},{9,25},{17,1},{25,9},{2,18},{10... | collective-permute-start | bytes 786440 | tf_op jit(solution)/shard_map/ppermute | solution.py:399
  54.8 25.6 %collective-permute-start.17 = (bf16[128,1024]{1,0:T(8,128)(2,1)S(1)}, bf16[128,1024]{1,0:T(8,128)(2,1)S(1)}, u32[]{:S(2)}, u32[]{:S(2)}) collective-permute-start(bf16[128,1024]{1,0:T(8,128)(2,1)S(1)} %get-tuple-element.60.rest_8_), channel_id=1, source_target_pairs={{0,24},{8,16},{16,8},{24,0},{1,25},{9,17},{17,9},{25,1},{2,26},{10... | collective-permute-start | bytes 786440 | tf_op jit(solution)/shard_map/ppermute | solution.py:399
  57.2 23.2 %collective-permute-start.8 = (bf16[128,1024]{1,0:T(8,128)(2,1)S(1)}, bf16[128,1024]{1,0:T(8,128)(2,1)S(1)}, u32[]{:S(2)}, u32[]{:S(2)}) collective-permute-start(bf16[128,1024]{1,0:T(8,128)(2,1)S(1)} %get-tuple-element.59), channel_id=1, source_target_pairs={{0,1},{1,0},{2,3},{3,2},{4,5},{5,4},{6,7},{7,6},{8,9},{9,8},{10,11... | collective-permute-start | bytes 786440 | tf_op jit(solution)/shard_map/ppermute | solution.py:396
  57.2 23.2 %collective-permute-start.9 = (bf16[128,1024]{1,0:T(8,128)(2,1)S(1)}, bf16[128,1024]{1,0:T(8,128)(2,1)S(1)}, u32[]{:S(2)}, u32[]{:S(2)}) collective-permute-start(bf16[128,1024]{1,0:T(8,128)(2,1)S(1)} %get-tuple-element.58.rest_0_), channel_id=1, source_target_pairs={{0,2},{1,3},{2,0},{3,1},{4,6},{5,7},{6,4},{7,5},{8,10},{9,11},{10,... | collective-permute-start | bytes 786440 | tf_op jit(solution)/shard_map/ppermute | solution.py:396
  81.7 6.0 %collective-permute-start.22 = (bf16[256,1024]{1,0:T(8,128)(2,1)S(1)}, bf16[256,1024]{1,0:T(8,128)(2,1)S(1)}, u32[]{:S(2)}, u32[]{:S(2)}) collective-permute-start(bf16[256,1024]{1,0:T(8,128)(2,1)S(1)} %get-tuple-element.72), channel_id=1, source_target_pairs={{0,1},{1,0},{2,3},{3,2},{4,5},{5,4},{6,7},{7,6},{8,9},{9,8},{10,11... | collective-permute-start | bytes 1572872 | tf_op jit(solution)/shard_map/ppermute | solution.py:396
  83.6 7.9 %collective-permute-start.30 = (bf16[128,1024]{1,0:T(8,128)(2,1)S(1)}, bf16[128,1024]{1,0:T(8,128)(2,1)S(1)}, u32[]{:S(2)}, u32[]{:S(2)}) collective-permute-start(bf16[128,1024]{1,0:T(8,128)(2,1)S(1)} %get-tuple-element.86), channel_id=1, source_target_pairs={{0,8},{8,0},{16,24},{24,16},{1,9},{9,1},{17,25},{25,17},{2,10},{10... | collective-permute-start | bytes 786440 | tf_op jit(solution)/shard_map/ppermute | solution.py:399
  85.0 28.9 %collective-permute-start.18 = (bf16[256,1024]{1,0:T(8,128)(2,1)S(1)}, bf16[256,1024]{1,0:T(8,128)(2,1)S(1)}, u32[]{:S(2)}, u32[]{:S(2)}) collective-permute-start(bf16[256,1024]{1,0:T(8,128)(2,1)S(1)} %get-tuple-element.63), channel_id=1, source_target_pairs={{0,2},{1,3},{2,0},{3,1},{4,6},{5,7},{6,4},{7,5},{8,10},{9,11},{10,... | collective-permute-start | bytes 1572872 | tf_op jit(solution)/shard_map/ppermute | solution.py:396
  85.3 30.5 %collective-permute-start.19 = (bf16[256,1024]{1,0:T(8,128)(2,1)S(1)}, bf16[256,1024]{1,0:T(8,128)(2,1)S(1)}, u32[]{:S(2)}, u32[]{:S(2)}) collective-permute-start(bf16[256,1024]{1,0:T(8,128)(2,1)S(1)} %get-tuple-element.64), channel_id=1, source_target_pairs={{0,4},{1,5},{2,6},{3,7},{4,0},{5,1},{6,2},{7,3},{8,12},{9,13},{10,... | collective-permute-start | bytes 1572872 | tf_op jit(solution)/shard_map/ppermute | solution.py:396
  86.4 30.2 %collective-permute-start.20 = (bf16[256,1024]{1,0:T(8,128)(2,1)S(1)}, bf16[256,1024]{1,0:T(8,128)(2,1)S(1)}, u32[]{:S(2)}, u32[]{:S(2)}) collective-permute-start(bf16[256,1024]{1,0:T(8,128)(2,1)S(1)} %get-tuple-element.65), channel_id=1, source_target_pairs={{0,6},{1,7},{2,4},{3,5},{4,2},{5,3},{6,0},{7,1},{8,14},{9,15},{10,... | collective-permute-start | bytes 1572872 | tf_op jit(solution)/shard_map/ppermute | solution.py:396
  87.7 15.9 %collective-permute-start.31 = (bf16[128,1024]{1,0:T(8,128)(2,1)S(1)}, bf16[128,1024]{1,0:T(8,128)(2,1)S(1)}, u32[]{:S(2)}, u32[]{:S(2)}) collective-permute-start(bf16[128,1024]{1,0:T(8,128)(2,1)S(1)} %get-tuple-element.87), channel_id=1, source_target_pairs={{0,16},{8,24},{16,0},{24,8},{1,17},{9,25},{17,1},{25,9},{2,18},{10... | collective-permute-start | bytes 786440 | tf_op jit(solution)/shard_map/ppermute | solution.py:399
  91.6 22.2 %collective-permute-start.32 = (bf16[128,1024]{1,0:T(8,128)(2,1)S(1)}, bf16[128,1024]{1,0:T(8,128)(2,1)S(1)}, u32[]{:S(2)}, u32[]{:S(2)}) collective-permute-start(bf16[128,1024]{1,0:T(8,128)(2,1)S(1)} %get-tuple-element.88), channel_id=1, source_target_pairs={{0,24},{8,16},{16,8},{24,0},{1,25},{9,17},{17,9},{25,1},{2,26},{10... | collective-permute-start | bytes 786440 | tf_op jit(solution)/shard_map/ppermute | solution.py:399
  103.7 13.3 %collective-permute-start.23 = (bf16[3,128,256]{2,1,0:T(8,128)(2,1)S(1)}, bf16[3,128,256]{2,1,0:T(8,128)(2,1)S(1)}, u32[]{:S(2)}, u32[]{:S(2)}) collective-permute-start(bf16[3,128,256]{2,1,0:T(8,128)(2,1)S(1)} %get-tuple-element.74), channel_id=1, source_target_pairs={{0,1},{1,0},{2,3},{3,2},{4,5},{5,4},{6,7},{7,6},{8,9},{9,8},{10,11... | collective-permute-start | bytes 589832 | tf_op jit(solution)/shard_map/ppermute | solution.py:396
  113.7 6.0 %collective-permute-start.24 = (bf16[3,128,256]{2,1,0:T(8,128)(2,1)S(1)}, bf16[3,128,256]{2,1,0:T(8,128)(2,1)S(1)}, u32[]{:S(2)}, u32[]{:S(2)}) collective-permute-start(bf16[3,128,256]{2,1,0:T(8,128)(2,1)S(1)} %get-tuple-element.75), channel_id=1, source_target_pairs={{0,2},{1,3},{2,0},{3,1},{4,6},{5,7},{6,4},{7,5},{8,10},{9,11},{10,... | collective-permute-start | bytes 589832 | tf_op jit(solution)/shard_map/ppermute | solution.py:396
  113.9 10.9 %collective-permute-start.25 = (bf16[3,128,256]{2,1,0:T(8,128)(2,1)S(1)}, bf16[3,128,256]{2,1,0:T(8,128)(2,1)S(1)}, u32[]{:S(2)}, u32[]{:S(2)}) collective-permute-start(bf16[3,128,256]{2,1,0:T(8,128)(2,1)S(1)} %get-tuple-element.76), channel_id=1, source_target_pairs={{0,3},{1,2},{2,1},{3,0},{4,7},{5,6},{6,5},{7,4},{8,11},{9,10},{10,... | collective-permute-start | bytes 589832 | tf_op jit(solution)/shard_map/ppermute | solution.py:396
  115.8 10.0 %collective-permute-start.26 = (bf16[3,128,256]{2,1,0:T(8,128)(2,1)S(1)}, bf16[3,128,256]{2,1,0:T(8,128)(2,1)S(1)}, u32[]{:S(2)}, u32[]{:S(2)}) collective-permute-start(bf16[3,128,256]{2,1,0:T(8,128)(2,1)S(1)} %get-tuple-element.77), channel_id=1, source_target_pairs={{0,4},{1,5},{2,6},{3,7},{4,0},{5,1},{6,2},{7,3},{8,12},{9,13},{10,... | collective-permute-start | bytes 589832 | tf_op jit(solution)/shard_map/ppermute | solution.py:396
  116.6 21.6 %collective-permute-start.33 = (f32[64,1024]{1,0:T(8,128)S(1)}, f32[64,1024]{1,0:T(8,128)S(1)}, u32[]{:S(2)}, u32[]{:S(2)}) collective-permute-start(f32[64,1024]{1,0:T(8,128)S(1)} %get-tuple-element.90), channel_id=1, source_target_pairs={{0,1},{1,0},{2,3},{3,2},{4,5},{5,4},{6,7},{7,6},{8,9},{9,8},{10,11... | collective-permute-start | bytes 786440 | tf_op jit(solution)/shard_map/ppermute | solution.py:396
  116.9 22.2 %collective-permute-start.21 = (bf16[128,1024]{1,0:T(8,128)(2,1)S(1)}, bf16[128,1024]{1,0:T(8,128)(2,1)S(1)}, u32[]{:S(2)}, u32[]{:S(2)}) collective-permute-start(bf16[128,1024]{1,0:T(8,128)(2,1)S(1)} %get-tuple-element.67), channel_id=1, source_target_pairs={{0,1},{1,0},{2,3},{3,2},{4,5},{5,4},{6,7},{7,6},{8,9},{9,8},{10,11... | collective-permute-start | bytes 786440 | tf_op jit(solution)/shard_map/ppermute | solution.py:396
  119.7 8.0 %collective-permute-start.27 = (bf16[3,128,256]{2,1,0:T(8,128)(2,1)S(1)}, bf16[3,128,256]{2,1,0:T(8,128)(2,1)S(1)}, u32[]{:S(2)}, u32[]{:S(2)}) collective-permute-start(bf16[3,128,256]{2,1,0:T(8,128)(2,1)S(1)} %get-tuple-element.78), channel_id=1, source_target_pairs={{0,5},{1,4},{2,7},{3,6},{4,1},{5,0},{6,3},{7,2},{8,13},{9,12},{10,... | collective-permute-start | bytes 589832 | tf_op jit(solution)/shard_map/ppermute | solution.py:396
  124.9 7.6 %collective-permute-start.28 = (bf16[3,128,256]{2,1,0:T(8,128)(2,1)S(1)}, bf16[3,128,256]{2,1,0:T(8,128)(2,1)S(1)}, u32[]{:S(2)}, u32[]{:S(2)}) collective-permute-start(bf16[3,128,256]{2,1,0:T(8,128)(2,1)S(1)} %get-tuple-element.79), channel_id=1, source_target_pairs={{0,6},{1,7},{2,4},{3,5},{4,2},{5,3},{6,0},{7,1},{8,14},{9,15},{10,... | collective-permute-start | bytes 589832 | tf_op jit(solution)/shard_map/ppermute | solution.py:396
  125.9 10.8 %collective-permute-start.29 = (bf16[3,128,256]{2,1,0:T(8,128)(2,1)S(1)}, bf16[3,128,256]{2,1,0:T(8,128)(2,1)S(1)}, u32[]{:S(2)}, u32[]{:S(2)}) collective-permute-start(bf16[3,128,256]{2,1,0:T(8,128)(2,1)S(1)} %get-tuple-element.80), channel_id=1, source_target_pairs={{0,7},{1,6},{2,5},{3,4},{4,3},{5,2},{6,1},{7,0},{8,15},{9,14},{10,... | collective-permute-start | bytes 589832 | tf_op jit(solution)/shard_map/ppermute | solution.py:396

commit v2 on v1

--- a/solution.py
+++ b/solution.py
@@ -14,11 +14,11 @@
 BF16 = jnp.bfloat16
 NN = (((1,), (0,)), ((), ()))
 NT = (((1,), (1,)), ((), ()))
-TN = (((0,), (0,)), ((), ()))
 LOG2E = 1.4426950408889634
 DEAD = -1e30
 VMEM = pl.BlockSpec(memory_space=pltpu.VMEM)
 SMEM = pl.BlockSpec(memory_space=pltpu.SMEM)
+HBM = pl.BlockSpec(memory_space=pltpu.HBM)
 ANY = pl.BlockSpec(memory_space=pl.ANY)
 MIB = 1 << 20
 
@@ -27,16 +27,23 @@
     return lax.dot_general(a, b, dims, preferred_element_type=F32)
 
 
+def in_hbm(x):
+    return pltpu.with_memory_space_constraint(x, pltpu.HBM)
+
+
 def sds(shape, dtype):
     return jax.ShapeDtypeStruct(shape, dtype)
 
 
+def after(x, *deps):
+    return lax.optimization_barrier((x,) + deps)[0]
+
+
 def call(kernel, ins, outs, scratch=(), flops=0, moved=0, vmem=24):
-    specs = [spec for spec, _ in ins]
     return pl.pallas_call(
         kernel,
         out_shape=tuple(shape for _, shape in outs),
-        in_specs=specs,
+        in_specs=[spec for spec, _ in ins],
         out_specs=tuple(spec for spec, _ in outs),
         scratch_shapes=list(scratch),
         compiler_params=pltpu.CompilerParams(vmem_limit_bytes=vmem * MIB),
@@ -45,12 +52,11 @@
 
 
 def col_of(dev, g, pairs, per):
-    core = dev % 2
-    return pl.multiple_of(((core * per + g) * pairs + dev // 2) * HD, HD)
-
-
-def copies(pairs_of_refs, sems):
-    handles = [pltpu.make_async_copy(src, dst, sems.at[n]) for n, (src, dst) in enumerate(pairs_of_refs)]
+    return pl.multiple_of(((dev % 2 * per + g) * pairs + dev // 2) * HD, HD)
+
+
+def copies(moves, sems):
+    handles = [pltpu.make_async_copy(src, dst, sems.at[n]) for n, (src, dst) in enumerate(moves)]
     for handle in handles:
         handle.start()
     for handle in handles:
@@ -180,31 +186,58 @@
     )
 
 
-def prep_kernel(n, per, q_ref, k_ref, v_ref, c_ref, w_ref, *rest):
-    qkv, (same, other, wsend, sems) = rest[:n], rest[n:]
+def prep_kernel(n, per, q_ref, k_ref, v_ref, c_ref, *rest):
+    qkv, (same, other, sems) = by_slot(rest[:-3], n, OPT["q_order"]), rest[-3:]
     s = lax.axis_index("seq")
     core = s % 2
     half = c_ref.shape[2] // 2
     moves = []
     for j in range(n):
-        dev = s ^ j
         for t, src in enumerate((q_ref, k_ref, v_ref)):
             for g in range(per):
-                col = col_of(dev, g, n // 2, per)
+                col = col_of(s ^ j, g, n // 2, per)
                 moves.append((src.at[0, :, pl.ds(col, HD)], qkv[j].at[t, :, pl.ds(g * HD, HD)]))
     mine = pl.multiple_of(core * half, half)
     theirs = pl.multiple_of((1 - core) * half, half)
     moves.append((c_ref.at[0, :, pl.ds(mine, half)], same))
     moves.append((c_ref.at[0, :, pl.ds(theirs, half)], other))
+    copies(moves, sems)
+
+
+def rows_prep_kernel(w_ref, out_ref, sem):
+    s = lax.axis_index("seq")
+    half = out_ref.shape[1]
     row = pl.multiple_of((s // 2) * HD, HD)
-    moves.append((w_ref.at[pl.ds(row, HD), pl.ds(mine, half)], wsend))
-    copies(moves, sems)
+    col = pl.multiple_of((s % 2) * half, half)
+    copy = pltpu.make_async_copy(w_ref.at[pl.ds(row, HD), pl.ds(col, half)], out_ref, sem)
+    copy.start()
+    copy.wait()
+
+
+def by_slot(refs, n, order):
+    if len(refs) == n:
+        slots = dict(zip([0] + order, refs))
+        return [slots[j] for j in range(n)]
+    if len(refs) == 2:
+        return [refs[j % 2].at[j // 2] for j in range(n)]
+    return [refs[j // 2].at[j % 2] for j in range(n)]
+
+
+def merge_kernel(mine_ref, recv_ref, *outs):
+    for jc, out in enumerate(outs):
+        out[0] = mine_ref[jc]
+        out[1] = recv_ref[jc]
+
+
+def stack_kernel(first_ref, second_ref, out_ref):
+    rows = first_ref.shape[0]
+    out_ref[:rows] = first_ref[...]
+    out_ref[rows:] = second_ref[...]
 
 
 def forward_kernel(n, per, adj_ref, cnt_ref, *rest):
-    qkv = rest[:n]
-    attn_ref, swap_ref, attn_t_ref, lse_ref, bias_ref = rest[n : n + 5]
-    keys, vals_t, score, expo = rest[n + 5 :]
+    qkv, rest = by_slot(rest[:-9], n, OPT["q_order"]), rest[-9:]
+    attn_ref, swap_ref, attn_t_ref, lse_ref, bias_ref, keys, vals_t, score, expo = rest
     s = lax.axis_index("seq")
     length = n * BLK
     scale = HD**-0.5 * LOG2E
@@ -250,31 +283,53 @@
             swap_ref[base + BLK : base + tile, lanes] = first
 
 
+def grow_kernel(bit, mine_ref, recv_ref, out_ref):
+    here = lax.axis_index("dp") // bit % 2
+    for i in range(mine_ref.shape[0]):
+        out_ref[2 * i + here] = mine_ref[i]
+        out_ref[2 * i + 1 - here] = recv_ref[i]
+
+
+def halve(total, bit, keep_ref, send_ref):
+    here = lax.axis_index("dp") // bit % 2
+    for i in range(keep_ref.shape[0]):
+        keep_ref[i] = jnp.where(here == 0, total[2 * i], total[2 * i + 1])
+        send_ref[i] = jnp.where(here == 0, total[2 * i + 1], total[2 * i]).astype(BF16)
+
+
+def fold_kernel(bit, mine_ref, recv_ref, keep_ref, send_ref):
+    halve(mine_ref[...] + recv_ref[...].astype(F32), bit, keep_ref, send_ref)
+
+
+def rows_kernel(*refs):
+    z = lax.axis_index("dp")
+    for j, ref in enumerate(refs[:-1]):
+        refs[-1][z ^ j] = ref[0]
+
+
 def grad_attn_kernel(n, per, *rest):
-    cot = rest[:n]
-    wts = rest[n : n + 2 * per]
-    own_ref, send_ref, w_out, cot_out = rest[n + 2 * per :]
+    cot, rest = rest[:-4], rest[-4:]
+    w_ref, own_ref, send_ref, cot_out = rest
     core = lax.axis_index("seq") % 2
-    z = lax.axis_index("dp")
-    for jz in range(2 * per):
-        slot = (z ^ jz) ^ (per * core)
-        w_out[pl.ds(pl.multiple_of(slot * HD, HD), HD), :] = wts[jz][...]
-    for j in range(n):
-        cot_out[j * BLK : (j + 1) * BLK, :] = cot[j][...]
-    mine = per * HD
+    mine = w_ref[pl.ds(pl.multiple_of(core * per * HD, HD), per * HD), :]
+    theirs = w_ref[pl.ds(pl.multiple_of((1 - core) * per * HD, HD), per * HD), :]
+    rows = n * BLK // len(cot)
+    for j, ref in enumerate(cot):
+        cot_out[j * rows : (j + 1) * rows, :] = ref[...]
     for t in range(n // 2):
         base = 2 * t * BLK
-        part = mm(w_out[...], cot_out[base : base + 2 * BLK, :], NT)
-        own_ref[:, base : base + 2 * BLK] = part[:mine]
-        send_ref[:, base : base + BLK] = part[mine:, BLK:].astype(BF16)
-        send_ref[:, base + BLK : base + 2 * BLK] = part[mine:, :BLK].astype(BF16)
-
-
-def backward_kernel(n, per, *rest):
-    qkv = rest[:n]
-    attn_t_ref, lse_ref, bias_ref, own_ref, recv_ref = rest[n : n + 5]
-    outs = rest[n + 5 : 2 * n + 5]
-    queries, keys_t, grad, delta, probs, dscores, dq_t = rest[2 * n + 5 :]
+        rows = cot_out[base : base + 2 * BLK, :]
+        own_ref[:, base : base + 2 * BLK] = mm(mine, rows, NT)
+        part = mm(theirs, rows, NT).astype(BF16)
+        send_ref[:, base : base + BLK] = part[:, BLK:]
+        send_ref[:, base + BLK : base + 2 * BLK] = part[:, :BLK]
+
+
+def backward_kernel(n, per, n_outs, *rest):
+    queries, keys_t, grad, delta, probs, dscores, dq_t = rest[-7:]
+    qkv = by_slot(rest[: -12 - n_outs], n, OPT["q_order"])
+    outs = by_slot(rest[-7 - n_outs : -7], n, OPT["g_order"])
+    attn_t_ref, lse_ref, bias_ref, own_ref, recv_ref = rest[-12 - n_outs : -7 - n_outs]
     scale = HD**-0.5
     tile = 2 * BLK
     length = n * BLK
@@ -321,26 +376,41 @@
 
 
 def out_kernel(n, attn_ref, recv_ref, w_ref, *outs):
+    core = lax.axis_index("seq") % 2
     tile = 2 * BLK
-    half = attn_ref.shape[1]
+    heads = attn_ref.shape[1]
+    mine = w_ref[pl.ds(pl.multiple_of(core * heads, heads), heads), :]
+    theirs = w_ref[pl.ds(pl.multiple_of((1 - core) * heads, heads), heads), :]
     for t in range(n // 2):
         rows = slice(t * tile, (t + 1) * tile)
-        part = mm(attn_ref[rows, :], w_ref[:half, :]) + mm(recv_ref[rows, :], w_ref[half:, :])
-        outs[t][...] = part.astype(outs[t].dtype)
-
-
-def weight_kernel(nz, attn_t_ref, recv_ref, cot_ref, *rest):
-    outs, grads = rest[:nz], rest[nz]
+        part = mm(attn_ref[rows, :], mine) + mm(recv_ref[rows, :], theirs)
+        if len(outs) > n // 2 and t == 3:
+            outs[3][...] = part[:BLK].astype(BF16)
+            outs[4][...] = part[BLK:].astype(BF16)
+        else:
+            outs[t][...] = part.astype(outs[t].dtype)
+
+
+def relay_kernel(first_ref, first_recv, second_ref, second_recv, *outs):
+    outs[0][:BLK] = first_ref[:BLK]
+    outs[0][BLK:] = (first_ref[BLK:].astype(F32) + second_recv[...].astype(F32)).astype(BF16)
+    outs[1][:BLK] = (second_ref[:BLK].astype(F32) + first_recv[...].astype(F32)).astype(BF16)
+    outs[1][BLK:] = second_ref[BLK:]
+
+
+def weight_kernel(per, attn_t_ref, recv_ref, cot_ref, *rest):
+    outs, grads = rest[:-1], rest[-1]
     core = lax.axis_index("seq") % 2
-    z = lax.axis_index("dp")
-    per = nz // 2
     for g in range(per):
-        grads[g] = mm(attn_t_ref[g], cot_ref[...])
+        grads[core * per + g] = mm(attn_t_ref[g], cot_ref[...])
         recv = recv_ref[:, g * HD : (g + 1) * HD].T
-        grads[per + g] = mm(recv, cot_ref[...])
-    for jz in range(nz):
-        slot = (z ^ jz) ^ (per * core)
-        outs[jz][...] = grads[slot].astype(outs[jz].dtype)
+        grads[(1 - core) * per + g] = mm(recv, cot_ref[...])
+    if len(outs) == 2:
+        halve(grads, 1, *outs)
+    else:
+        z = lax.axis_index("dp")
+        for j, out in enumerate(outs):
+            out[0] = grads[z ^ j].astype(out.dtype)
 
 
 def out_sum_kernel(own_ref, *rest):
@@ -355,9 +425,9 @@
 
 def weight_sum_kernel(own_ref, *rest):
     parts, (keep_ref, send_ref) = rest[:-2], rest[-2:]
-    total = own_ref[...]
+    total = own_ref[0]
     for part in parts:
-        total = total + part[...].astype(F32)
+        total = total + part[0].astype(F32)
     half = total.shape[0] // 2
     core = lax.axis_index("seq") % 2
     keep_ref[...] = jnp.where(core == 0, total[:half], total[half:])
@@ -368,13 +438,13 @@
     core = lax.axis_index("seq") % 2
     half = keep_ref.shape[1]
     lead = (0,) if len(out_ref.shape) == 3 else ()
-    keep, recv = keep_ref[...], recv_ref[...]
+    keep, recv = keep_ref[...].astype(out_ref.dtype), recv_ref[...].astype(out_ref.dtype)
     out_ref[lead + (slice(None), slice(0, half))] = jnp.where(core == 0, keep, recv)
     out_ref[lead + (slice(None), slice(half, 2 * half))] = jnp.where(core == 0, recv, keep)
 
 
 def place_kernel(n, per, *rest):
-    parts, outs, sems = rest[:n], rest[n : n + 3], rest[n + 3]
+    parts, outs, sems = by_slot(rest[:-4], n, OPT["g_order"]), rest[-4:-1], rest[-1]
     s = lax.axis_index("seq")
     moves = []
     for j in range(n):
@@ -385,12 +455,25 @@
     copies(moves, sems)
 
 
+OPT = {'q_order': [6, 2, 4, 7, 3, 5, 1], 'g_order': [6, 2, 4, 7, 3, 5, 1], 'c_order': [1, 2, 3], 'tie_swap': [], 'q_merged': False, 'g_merged': False, 'c_gather': False, 'w_hyper': True, 'g_hyper': True, 'out_first': False, 'wgt_first': True, 'g_tied': False, 'o_order': [3, 2, 1], 'tie_other': [], 'tie_cot': ['q6', 'q2', 'q4'], 'tie_wsend': [], 'tie_w_last': [], 'tie_k1': [], 'tie_out': ['k2'], 'tie_k2': [], 'tie_wgt': [], 'tie_k3': ['wgt'], 'tie_fold': ['k3'], 'tie_osum': ['k3'], 'o_fwd': True, 'tie_relay': [], 'tie_place': [], 'relay_first': False, 'tie_prep': []}
+
+
 def paired(n, nz, queries, key_rows, values, adjacency, counts, out_weight, out_cotangent):
     per = nz // 2
+    pairs = n // 2
     length = n * BLK
     wide = queries.shape[2]
     half = wide // 2
     heads = per * HD
+    chunk = sds((3, BLK, heads), BF16)
+    couple = sds((2, 3, BLK, heads), BF16)
+    chunks = sds((pairs, 3, BLK, heads), BF16)
+    piece = sds((BLK, half), BF16)
+    named = {}
+
+    def tied(x, point):
+        deps = [named[d] for d in OPT["tie_" + point]]
+        return after(x, *deps) if deps else x
 
     def to(x, j):
         return lax.ppermute(x, "seq", [(i, i ^ j) for i in range(n)])
@@ -398,23 +481,99 @@
     def to_z(x, j):
         return lax.ppermute(x, "dp", [(i, i ^ j) for i in range(nz)])
 
-    chunk = sds((3, BLK, heads), BF16)
-    piece = sds((BLK, half), BF16)
+    def exchange(parts, name, merged, ties=None):
+        if merged:
+            parts = call(
+                merge_kernel,
+                [(VMEM, parts[0]), (VMEM, to(parts[1], 1))],
+                [(VMEM, couple)] * pairs,
+                moved=4 * MIB,
+            )
+            out = [parts[0]]
+            for jc in range(1, pairs):
+                x = after(parts[jc], ties[jc]) if ties else parts[jc]
+                out.append(to(x, 2 * jc))
+                named[name + str(2 * jc)] = out[-1]
+            named[name + "1"] = named[name + "7"] = out[1]
+            return out
+        out = [parts[0]]
+        for part, j in zip(parts[1:], OPT[name + "_order"]):
+            x = after(part, ties[j // 2]) if ties and j > 1 else part
+            out.append(to(x, j))
+            named[name + str(j)] = out[-1]
+        return out
+
+    lay = [chunks] * 2 if OPT["q_merged"] else [chunk] * n
+    (wsend,) = call(
+        rows_prep_kernel,
+        [(HBM, in_hbm(out_weight))],
+        [(VMEM, pltpu.VMEM((HD, half), BF16))],
+        [pltpu.SemaphoreType.DMA],
+    )
+    named["ws"] = wsend
     prep = call(
         functools.partial(prep_kernel, n, per),
-        [(ANY, x) for x in (queries, key_rows, values, out_cotangent, out_weight)],
-        [(ANY, chunk)] * n + [(ANY, piece)] * 2 + [(ANY, sds((HD, half), BF16))],
-        [pltpu.SemaphoreType.DMA((3 * n * per + 3,))],
+        [(HBM, in_hbm(x)) for x in (tied(queries, "prep"), key_rows, values, out_cotangent)],
+        [(VMEM, pltpu.VMEM(x.shape, x.dtype)) for x in lay + [piece] * 2],
+        [pltpu.SemaphoreType.DMA((3 * n * per + 2,))],
         moved=8 * MIB,
     )
-    qkv = [prep[0]] + [to(prep[j], j) for j in range(1, n)]
-    same, other, wsend = prep[n:]
-    wts = [wsend] + [to_z(wsend, j) for j in range(1, nz)]
-    cot = [same] + [to(other if j % 2 else same, j) for j in range(1, n)]
+    same, other = prep[-2:]
+    named["same"] = same
+    qkv = exchange(prep[:-2], "q", OPT["q_merged"])
+    if OPT["c_gather"] == 2:
+        same, other = tied(same, "cot"), tied(other, "cot")
+        cot = [same] + [to(other if j % 2 else same, j) for j in range(1, n)]
+        named["c0"] = cot[1]
+    elif OPT["c_gather"]:
+        same = tied(same, "cot")
+        cot = [same, to(tied(other, "other"), 1)] + [None] * (n - 2)
+        for j in sorted(range(2, n), key=lambda j: ((j >> 1).bit_count(), j & 1, j)):
+            bits = j & ~1
+            hop = bits & -bits if j % 2 == 0 else 1 << (bits.bit_length() - 1)
+            cot[j] = to(cot[j ^ hop], hop)
+        named["c0"] = cot[1]
+    else:
+        (cot_own,) = call(
+            stack_kernel,
+            [(VMEM, same), (VMEM, to(tied(other, "other"), 1))],
+            [(VMEM, sds((2 * BLK, half), BF16))],
+            moved=MIB,
+        )
+        named["c0"] = cot_own
+        cot_sent = tied(cot_own, "cot")
+        cot = [cot_own, None, None, None]
+        for jc in OPT["c_order"]:
+            cot[jc] = to(cot_sent, 2 * jc)
+            named["c" + str(jc)] = cot[jc]
+    w_rows = tied(wsend, "wsend")[None]
+    if OPT["w_hyper"]:
+        bit = nz
+        while bit > 1:
+            bit //= 2
+            (w_rows,) = call(
+                functools.partial(grow_kernel, bit),
+                [(VMEM, w_rows), (VMEM, to_z(w_rows, bit))],
+                [(VMEM, sds((2 * w_rows.shape[0], HD, half), BF16))],
+                moved=2 * MIB,
+            )
+            named.setdefault("w1", w_rows)
+    else:
+        named["w1"] = to_z(w_rows, 2)
+        wts = [w_rows, None, named["w1"]] + [to_z(w_rows, j) for j in range(3, nz)]
+        wts[1] = to_z(tied(w_rows, "w_last"), 1)
+        (w_rows,) = call(
+            rows_kernel,
+            [(VMEM, x) for x in wts],
+            [(VMEM, sds((nz, HD, half), BF16))],
+            moved=2 * MIB,
+        )
+    w_rows = w_rows.reshape(nz * HD, half)
+    named["w"] = w_rows
 
     attn, swap, attn_t, lse, bias = call(
         functools.partial(forward_kernel, n, per),
-        [(SMEM, adjacency), (SMEM, counts)] + [(VMEM, x) for x in qkv],
+        [(SMEM, adjacency), (SMEM, tied(counts, "k1"))] + [(VMEM, x) for x in qkv],
         [
             (VMEM, sds((length, heads), BF16)),
             (VMEM, sds((length, heads), BF16)),
@@ -431,35 +590,82 @@
         flops=4 * per * length * length * HD,
         moved=4 * MIB,
     )
-    attn_recv = to(swap, 1)
-
-    grad_own, grad_send, w_rows, cot_rows = call(
+    attn_recv = to(tied(swap, "swap"), 1)
+    named["a"] = attn_recv
+
+    def project():
+        shapes = [sds((2 * BLK, half), BF16 if t else F32) for t in range(pairs)]
+        if OPT["o_fwd"]:
+            shapes = shapes[:3] + [sds((BLK, half), BF16)] * 2
+        parts = call(
+            functools.partial(out_kernel, n),
+            [(VMEM, attn), (VMEM, attn_recv), (VMEM, tied(w_rows, "out"))],
+            [(VMEM, x) for x in shapes],
+            flops=4 * length * heads * half,
+            moved=6 * MIB,
+        )
+        named["o0"] = parts[0]
+        if OPT["o_fwd"]:
+            named["o1"] = to(parts[3], 2)
+            named["o2"] = to(parts[4], 4)
+            return parts, [named["o1"], named["o2"]]
+        recv = [None] * pairs
+        for t in OPT["o_order"]:
+            recv[t] = to(parts[t], 2 * t)
+            named["o" + str(t)] = recv[t]
+        return parts, recv[1:]
+
+    if OPT["out_first"]:
+        out_parts, out_recv = project()
+    grad_own, grad_send, cot_rows = call(
         functools.partial(grad_attn_kernel, n, per),
-        [(VMEM, x) for x in cot + wts],
+        [(VMEM, x) for x in cot + [tied(w_rows, "k2")]],
         [
             (VMEM, sds((heads, length), F32)),
             (VMEM, sds((heads, length), BF16)),
-            (VMEM, sds((2 * heads, half), BF16)),
             (VMEM, sds((length, half), BF16)),
         ],
         flops=4 * length * heads * half,
         moved=8 * MIB,
     )
+    named["k2"] = grad_own
     grad_recv = to(grad_send, 1)
-
-    out_parts = call(
-        functools.partial(out_kernel, n),
-        [(VMEM, attn), (VMEM, attn_recv), (VMEM, w_rows)],
-        [(VMEM, sds((2 * BLK, half), BF16 if t else F32)) for t in range(n // 2)],
-        flops=4 * length * heads * half,
-        moved=6 * MIB,
-    )
-    out_recv = [to(out_parts[t], 2 * t) for t in range(1, n // 2)]
-
+    if not OPT["out_first"]:
+        out_parts, out_recv = project()
+
+    def weigh():
+        outs = [(2, F32), (2, BF16)] if OPT["g_hyper"] else [(1, F32)] + [(1, BF16)] * (nz - 1)
+        return call(
+            functools.partial(weight_kernel, per),
+            [(VMEM, attn_t), (VMEM, attn_recv), (VMEM, tied(cot_rows, "wgt"))],
+            [(VMEM, sds((m, HD, half), d)) for m, d in outs],
+            [pltpu.VMEM((nz, HD, half), F32)],
+            flops=4 * length * heads * half,
+            moved=6 * MIB,
+        )
+
+    def relay(first, second):
+        relayed = call(
+            relay_kernel,
+            [(VMEM, tied(out_parts[1], "relay")), (VMEM, first), (VMEM, out_parts[2]), (VMEM, second)],
+            [(VMEM, sds((2 * BLK, half), BF16))] * 2,
+            moved=3 * MIB,
+        )
+        named["r"] = relayed[0]
+        recv = [to(relayed[0], 2), to(relayed[1], 4)]
+        named["o3"] = recv[0]
+        return recv
+
+    if OPT["o_fwd"] and OPT["relay_first"]:
+        out_recv = relay(*out_recv)
+    if OPT["wgt_first"]:
+        weighed = weigh()
+        named["wgt"] = weighed[0]
+    lay = [chunks] * 2 if OPT["g_merged"] else [chunk] * n
     grads = call(
-        functools.partial(backward_kernel, n, per),
-        [(VMEM, x) for x in qkv + [attn_t, lse, bias, grad_own, grad_recv]],
-        [(VMEM, chunk)] * n,
+        functools.partial(backward_kernel, n, per, len(lay)),
+        [(VMEM, x) for x in qkv + [attn_t, lse, bias, tied(grad_own, "k3"), grad_recv]],
+        [(VMEM, x) for x in lay],
         [
             pltpu.VMEM((per, length, HD), BF16),
             pltpu.VMEM((per, HD, length), BF16),
@@ -472,21 +678,31 @@
         flops=10 * per * length * length * HD,
         moved=8 * MIB,
     )
-    back = [grads[0]] + [to(grads[j], j) for j in range(1, n)]
-
-    w_parts = call(
-        functools.partial(weight_kernel, nz),
-        [(VMEM, attn_t), (VMEM, attn_recv), (VMEM, cot_rows)],
-        [(VMEM, sds((HD, half), BF16 if j else F32)) for j in range(nz)],
-        [pltpu.VMEM((nz, HD, half), F32)],
-        flops=4 * length * heads * half,
-        moved=6 * MIB,
-    )
-    w_recv = [to_z(w_parts[j], j) for j in range(1, nz)]
+    named["k3"] = grads[0]
+    if OPT["o_fwd"] and not OPT["relay_first"]:
+        out_recv = relay(*out_recv)
+    back = exchange(grads, "g", OPT["g_merged"], [None] + out_recv if OPT["g_tied"] and not OPT["o_fwd"] else None)
+    if not OPT["wgt_first"]:
+        weighed = weigh()
+
+    if OPT["g_hyper"]:
+        w_keep, w_send = weighed
+        bit = 1
+        while 2 * bit < nz:
+            w_keep, w_send = call(
+                functools.partial(fold_kernel, 2 * bit),
+                [(VMEM, tied(w_keep, "fold")), (VMEM, to_z(w_send, bit))],
+                [(VMEM, sds((w_keep.shape[0] // 2, HD, half), d)) for d in (F32, BF16)],
+                moved=2 * MIB,
+            )
+            bit *= 2
+        w_all = [w_keep, to_z(w_send, bit)]
+    else:
+        w_all = [weighed[0]] + [to_z(x, j) for j, x in enumerate(weighed[1:], 1)]
 
     out_keep, out_send = call(
         out_sum_kernel,
-        [(VMEM, x) for x in [out_parts[0]] + out_recv],
+        [(VMEM, x) for x in [tied(out_parts[0], "osum")] + out_recv],
         [(VMEM, sds((BLK, half), BF16))] * 2,
         moved=3 * MIB,
     )
@@ -496,22 +712,23 @@
         [(VMEM, sds((1, BLK, wide), BF16))],
         moved=MIB,
     )
-    w_keep, w_send = call(
+    half_keep, half_send = call(
         weight_sum_kernel,
-        [(VMEM, x) for x in [w_parts[0]] + w_recv],
+        [(VMEM, x) for x in w_all],
         [(VMEM, sds((HD // 2, half), F32))] * 2,
         moved=2 * MIB,
     )
     (weight_grad,) = call(
         join_kernel,
-        [(VMEM, w_keep), (VMEM, to(w_send, 1))],
+        [(VMEM, half_keep), (VMEM, to(half_send, 1))],
         [(VMEM, sds((HD // 2, wide), F32))],
         moved=MIB,
     )
+    named["lo"], named["wg"] = layer_out, weight_grad
     token = sds((1, BLK, wide), BF16)
     query_grad, key_grad, value_grad = call(
         functools.partial(place_kernel, n, per),
-        [(ANY, x) for x in back],
+        [(ANY, tied(back[0], "place"))] + [(ANY, x) for x in back[1:]],
         [(ANY, token)] * 3,
         [pltpu.SemaphoreType.DMA((3 * n * per,))],
         moved=3 * MIB,

time: 140 us -> 99.9 us (0.71)
  the two profiles are of different devices: /device:TPU:17 before, /device:TPU:2 now
where the time goes in v2:
time: 99.9 us; the launch traced here: 99.4 us
  waiting for transfers between devices  51.6 us (52%)
  starting transfers between devices  25.3 us (25%)
  Pallas kernels  21.7 us (22%)
    ppermute x26, waiting for transfers between devices, to(): return lax.ppermute(x, 'seq', [(i, i ^ j) for i in range(n)])  47.8 us
    pallas_call x17, Pallas kernels, call(): pl.pallas_call(kernel, out_shape=tuple((shape for _, shape in outs)), in_...  21.7 us
    ppermute x26, starting transfers between devices, to(): return lax.ppermute(x, 'seq', [(i, i ^ j) for i in range(n)])  18.9 us
    ppermute x4, starting transfers between devices, to_z(): return lax.ppermute(x, 'dp', [(i, i ^ j) for i in range(nz)])  6.37 us
    ppermute x4, waiting for transfers between devices, to_z(): return lax.ppermute(x, 'dp', [(i, i ^ j) for i in range(nz)])  3.86 us
  transfers between devices with their start and end apart: 30, of which 16 were waited for; matrix products, arithmetic and copies ran while one was open for 0% of the time, Pallas kernels for 20%

profile of v2, /device:TPU:2, one launch (start us, length us, event | category | flops | bytes accessed | tf_op | source)
XLA Modules:
  0.0 99.4 jit_solution(7915770326412921048)
XLA Ops:
  0.6 1.0 shard_map.112
  1.6 2.7 %collective-permute-start.8 = (bf16[1,128,1024]{2,1,0:T(8,128)(2,1)S(1)}, bf16[1,128,1024]{2,1,0:T(8,128)(2,1)S(1)}, u32[]{:S(2)}, u32[]{:S(2)}) collective-permute-start(bf16[1,128,1024]{2,1,0:T(8,128)(2,1)S(1)} %bitcast.4), channel_id=1, source_target_pairs={{0,16},{8,24},{16,0},{24,8},{1,17},{9,25},{17,1},{25,9},{2,18},{10... | collective-permute-start | bytes 786440 | tf_op jit(solution)/shard_map/ppermute | solution.py:482
  4.3 2.1 %shard_map.110 = (bf16[3,128,256]{2,1,0:T(8,128)(2,1)S(1)}, bf16[3,128,256]{2,1,0:T(8,128)(2,1)S(1)}, bf16[3,128,256]{2,1,0:T(8,128)(2,1)S(1)}, bf16[3,128,256]{...) custom-call(bf16[1,128,2048]{2,1,0:T(8,128)(2,1)} %q_ref.1, ...), custom_call_target="tpu_custom_call" | custom-call | bytes 8388608 | tf_op jit(solution)/shard_map/pallas_call | solution.py:43
  6.5 1.6 %collective-permute-start = (bf16[3,128,256]{2,1,0:T(8,128)(2,1)S(1)}, bf16[3,128,256]{2,1,0:T(8,128)(2,1)S(1)}, u32[]{:S(2)}, u32[]{:S(2)}) collective-permute-start(bf16[3,128,256]{2,1,0:T(8,128)(2,1)S(1)} %get-tuple-element.55), channel_id=1, source_target_pairs={{0,6},{1,7},{2,4},{3,5},{4,2},{5,3},{6,0},{7,1},{8,14},{9,15},{10,... | collective-permute-start | bytes 589832 | tf_op jit(solution)/shard_map/ppermute | solution.py:479
  8.1 1.5 %collective-permute-start.1 = (bf16[3,128,256]{2,1,0:T(8,128)(2,1)S(1)}, bf16[3,128,256]{2,1,0:T(8,128)(2,1)S(1)}, u32[]{:S(2)}, u32[]{:S(2)}) collective-permute-start(bf16[3,128,256]{2,1,0:T(8,128)(2,1)S(1)} %get-tuple-element.56), channel_id=1, source_target_pairs={{0,2},{1,3},{2,0},{3,1},{4,6},{5,7},{6,4},{7,5},{8,10},{9,11},{10,... | collective-permute-start | bytes 589832 | tf_op jit(solution)/shard_map/ppermute | solution.py:479
  9.6 0.5 collective-permute-start.2
  10.1 5.2 %collective-permute-done.rest_1_ = bf16[3,128,256]{2,1,0:T(8,128)(2,1)S(1)} collective-permute-done((bf16[3,128,256]{2,1,0:T(8,128)(2,1)S(1)}, bf16[3,128,256]{2,1,0:T(8,128)(2,1)S(1)}, u32[]{:S(2)}, u32[]{:S(2)}) %collective-permute-start) | collective-permute-done | bytes 196640 | tf_op jit(solution)/shard_map/ppermute | solution.py:479
  15.2 0.3 collective-permute-start.3
  15.5 3.5 %collective-permute-done.1.rest_2_ = bf16[3,128,256]{2,1,0:T(8,128)(2,1)S(1)} collective-permute-done((bf16[3,128,256]{2,1,0:T(8,128)(2,1)S(1)}, bf16[3,128,256]{2,1,0:T(8,128)(2,1)S(1)}, u32[]{:S(2)}, u32[]{:S(2)}) %collective-permute-start.1) | collective-permute-done | bytes 196640 | tf_op jit(solution)/shard_map/ppermute | solution.py:479
  19.0 0.8 collective-permute-start.5
  19.9 1.6 %collective-permute-start.9 = (bf16[2,128,1024]{2,1,0:T(8,128)(2,1)S(1)}, bf16[2,128,1024]{2,1,0:T(8,128)(2,1)S(1)}, u32[]{:S(2)}, u32[]{:S(2)}) collective-permute-start(bf16[2,128,1024]{2,1,0:T(8,128)(2,1)S(1)} %shard_map.113.mine_ref), channel_id=1, source_target_pairs={{0,8},{8,0},{16,24},{24,16},{1,9},{9,1},{17,25},{25,17},{2,10},{10... | collective-permute-start | bytes 1572872 | tf_op jit(solution)/shard_map/ppermute | solution.py:482
  21.6 1.8 %collective-permute-done.3.rest_4_ = bf16[3,128,256]{2,1,0:T(8,128)(2,1)S(1)} collective-permute-done((bf16[3,128,256]{2,1,0:T(8,128)(2,1)S(1)}, bf16[3,128,256]{2,1,0:T(8,128)(2,1)S(1)}, u32[]{:S(2)}, u32[]{:S(2)}) %collective-permute-start.3) | collective-permute-done | bytes 196640 | tf_op jit(solution)/shard_map/ppermute | solution.py:479
  23.4 1.5 %collective-permute-start.13 = (bf16[256,1024]{1,0:T(8,128)(2,1)S(1)}, bf16[256,1024]{1,0:T(8,128)(2,1)S(1)}, u32[]{:S(2)}, u32[]{:S(2)}) collective-permute-start(bf16[256,1024]{1,0:T(8,128)(2,1)S(1)} %shard_map.115.rest_0_), channel_id=1, source_target_pairs={{0,6},{1,7},{2,4},{3,5},{4,2},{5,3},{6,0},{7,1},{8,14},{9,15},{10,... | collective-permute-start | bytes 1572872 | tf_op jit(solution)/shard_map/ppermute | solution.py:479
  24.9 2.6 %collective-permute-done.4.rest_5_ = bf16[3,128,256]{2,1,0:T(8,128)(2,1)S(1)} collective-permute-done((bf16[3,128,256]{2,1,0:T(8,128)(2,1)S(1)}, bf16[3,128,256]{2,1,0:T(8,128)(2,1)S(1)}, u32[]{:S(2)}, u32[]{:S(2)}) %collective-permute-start.4) | collective-permute-done | bytes 196640 | tf_op jit(solution)/shard_map/ppermute | solution.py:479
  27.5 0.5 collective-permute-start.12
  28.0 0.6 collective-permute-start.11
  28.5 4.9 %shard_map.111 = (bf16[1024,256]{1,0:T(8,128)(2,1)S(1)}, bf16[1024,256]{1,0:T(8,128)(2,1)S(1)}, bf16[2,128,1024]{2,1,0:T(8,128)(2,1)S(1)}, f32[2,1024]{1,0:T(2,128)S(1)}, f32[8,1024]{1,0:T(8,128)S(1)}) custom-call(s32[1,8,8]{2,1,0:T(8,128)S(1)} %copy-done, s32[1,8]{1,0:T(1,128)S(1)} %copy-done.1, bf16[3,128,256]{2,1,0:T(8,128)(2,1)S(1)} %get-tuple-element.54.rest_0_, ...), custom_call_target="tpu_custom_call" | custom-call | flops 1073741824 | bytes 4194304 | tf_op jit(solution)/shard_map/pallas_call | solution.py:43
  33.6 0.8 collective-permute-done.9.recv_ref
  34.4 4.8 %collective-permute-done.13.rest_3_ = bf16[256,1024]{1,0:T(8,128)(2,1)S(1)} collective-permute-done((bf16[256,1024]{1,0:T(8,128)(2,1)S(1)}, bf16[256,1024]{1,0:T(8,128)(2,1)S(1)}, u32[]{:S(2)}, u32[]{:S(2)}) %collective-permute-start.13) | collective-permute-done | bytes 524320 | tf_op jit(solution)/shard_map/ppermute | solution.py:479
  39.2 10.7 %collective-permute-done.12.rest_2_ = bf16[256,1024]{1,0:T(8,128)(2,1)S(1)} collective-permute-done((bf16[256,1024]{1,0:T(8,128)(2,1)S(1)}, bf16[256,1024]{1,0:T(8,128)(2,1)S(1)}, u32[]{:S(2)}, u32[]{:S(2)}) %collective-permute-start.12) | collective-permute-done | bytes 524320 | tf_op jit(solution)/shard_map/ppermute | solution.py:479
  50.0 1.3 %shard_map.116 = (f32[256,1024]{1,0:T(8,128)S(1)}, bf16[256,1024]{1,0:T(8,128)(2,1)S(1)}, bf16[1024,1024]{1,0:T(8,128)(2,1)S(1)}) custom-call(bf16[256,1024]{1,0:T(8,128)(2,1)S(1)} %shard_map.115.rest_0_, bf16[256,1024]{1,0:T(8,128)(2,1)S(1)} %collective-permute-done.11.rest_1_, bf16[256,1024]{1,0:T(8,128)(2,1)S(1)} %collective-permute-done.12.rest_2_, ...), custom_call_target="tpu_custom_call" | custom-call | flops 1073741824 | bytes 8388608 | tf_op jit(solution)/shard_map/pallas_call | solution.py:43
  51.4 1.3 %shard_map.117 = (f32[256,1024]{1,0:T(8,128)S(1)}, bf16[256,1024]{1,0:T(8,128)(2,1)S(1)}, bf16[256,1024]{1,0:T(8,128)(2,1)S(1)}, bf16[128,1024]{1,0:T(8,128)(2,1)S(1)}, bf16[128,1024]{1,0:T(8,128)(2,1)S(1)}) custom-call(bf16[1024,256]{1,0:T(8,128)(2,1)S(1)} %get-tuple-element.62.attn_ref, bf16[1024,256]{1,0:T(8,128)(2,1)S(1)} %collective-permute-done.7.recv_ref, ...), custom_call_target="tpu_custom_call" | custom-call | flops 1073741824 | bytes 6291456 | tf_op jit(solution)/shard_map/pallas_call | solution.py:43
  52.7 0.6 collective-permute-start.15
  53.3 1.4 %collective-permute-start.16 = (bf16[128,1024]{1,0:T(8,128)(2,1)S(1)}, bf16[128,1024]{1,0:T(8,128)(2,1)S(1)}, u32[]{:S(2)}, u32[]{:S(2)}) collective-permute-start(bf16[128,1024]{1,0:T(8,128)(2,1)S(1)} %get-tuple-element.82), channel_id=1, source_target_pairs={{0,4},{1,5},{2,6},{3,7},{4,0},{5,1},{6,2},{7,3},{8,12},{9,13},{10,... | collective-permute-start | bytes 786440 | tf_op jit(solution)/shard_map/ppermute | solution.py:479
  54.7 1.5 %shard_map.118 = (f32[2,128,1024]{2,1,0:T(8,128)S(1)}, bf16[2,128,1024]{2,1,0:T(8,128)(2,1)S(1)}) custom-call(bf16[2,128,1024]{2,1,0:T(8,128)(2,1)S(1)} %get-tuple-element.70.attn_t_ref.rest_8_, bf16[1024,256]{1,0:T(8,128)(2,1)S(1)} %collective-permute-done.7.recv_ref, bf16[1024,1024]{1,0:T(8,128)(2,1)S(1)} %get-tuple-element.73.cot_ref), custom_call_target="tpu_custom_call" | custom-call | flops 1073741824 | bytes 6291456 | tf_op jit(solution)/shard_map/pallas_call | solution.py:43
  56.2 1.7 %collective-permute-start.27 = (bf16[2,128,1024]{2,1,0:T(8,128)(2,1)S(1)}, bf16[2,128,1024]{2,1,0:T(8,128)(2,1)S(1)}, u32[]{:S(2)}, u32[]{:S(2)}) collective-permute-start(bf16[2,128,1024]{2,1,0:T(8,128)(2,1)S(1)} %get-tuple-element.98), channel_id=1, source_target_pairs={{0,8},{8,0},{16,24},{24,16},{1,9},{9,1},{17,25},{25,17},{2,10},{10... | collective-permute-start | bytes 1572872 | tf_op jit(solution)/shard_map/ppermute | solution.py:482
  57.9 3.6 %collective-permute-done.15.first_recv = bf16[128,1024]{1,0:T(8,128)(2,1)S(1)} collective-permute-done((bf16[128,1024]{1,0:T(8,128)(2,1)S(1)}, bf16[128,1024]{1,0:T(8,128)(2,1)S(1)}, u32[]{:S(2)}, u32[]{:S(2)}) %collective-permute-start.15) | collective-permute-done | bytes 262176 | tf_op jit(solution)/shard_map/ppermute | solution.py:479
  61.4 0.2 collective-permute-done.16.second_recv
  61.8 1.6 %collective-permute-start.17 = (bf16[256,1024]{1,0:T(8,128)(2,1)S(1)}, bf16[256,1024]{1,0:T(8,128)(2,1)S(1)}, u32[]{:S(2)}, u32[]{:S(2)}) collective-permute-start(bf16[256,1024]{1,0:T(8,128)(2,1)S(1)} %get-tuple-element.83), channel_id=1, source_target_pairs={{0,2},{1,3},{2,0},{3,1},{4,6},{5,7},{6,4},{7,5},{8,10},{9,11},{10,... | collective-permute-start | bytes 1572872 | tf_op jit(solution)/shard_map/ppermute | solution.py:479
  63.4 1.4 %collective-permute-start.18 = (bf16[256,1024]{1,0:T(8,128)(2,1)S(1)}, bf16[256,1024]{1,0:T(8,128)(2,1)S(1)}, u32[]{:S(2)}, u32[]{:S(2)}) collective-permute-start(bf16[256,1024]{1,0:T(8,128)(2,1)S(1)} %get-tuple-element.84), channel_id=1, source_target_pairs={{0,4},{1,5},{2,6},{3,7},{4,0},{5,1},{6,2},{7,3},{8,12},{9,13},{10,... | collective-permute-start | bytes 1572872 | tf_op jit(solution)/shard_map/ppermute | solution.py:479
  64.8 5.6 %shard_map.119 = (bf16[3,128,256]{2,1,0:T(8,128)(2,1)S(1)}, bf16[3,128,256]{2,1,0:T(8,128)(2,1)S(1)}, bf16[3,128,256]{2,1,0:T(8,128)(2,1)S(1)}, bf16[3,128,256]{...) custom-call(bf16[3,128,256]{2,1,0:T(8,128)(2,1)S(1)} %get-tuple-elem, ...), custom_call_target="tpu_custom_call" | custom-call | flops 2684354560 | bytes 8388608 | tf_op jit(solution)/shard_map/pallas_call | solution.py:43
  70.6 0.4 collective-permute-start.28
  71.0 1.1 %collective-permute-start.20 = (bf16[3,128,256]{2,1,0:T(8,128)(2,1)S(1)}, bf16[3,128,256]{2,1,0:T(8,128)(2,1)S(1)}, u32[]{:S(2)}, u32[]{:S(2)}) collective-permute-start(bf16[3,128,256]{2,1,0:T(8,128)(2,1)S(1)} %get-tuple-element.87), channel_id=1, source_target_pairs={{0,6},{1,7},{2,4},{3,5},{4,2},{5,3},{6,0},{7,1},{8,14},{9,15},{10,... | collective-permute-start | bytes 589832 | tf_op jit(solution)/shard_map/ppermute | solution.py:479
  72.1 0.9 collective-permute-start.21
  73.1 3.7 %collective-permute-done.17.rest_0_ = bf16[256,1024]{1,0:T(8,128)(2,1)S(1)} collective-permute-done((bf16[256,1024]{1,0:T(8,128)(2,1)S(1)}, bf16[256,1024]{1,0:T(8,128)(2,1)S(1)}, u32[]{:S(2)}, u32[]{:S(2)}) %collective-permute-start.17) | collective-permute-done | bytes 524320 | tf_op jit(solution)/shard_map/ppermute | solution.py:479
  76.8 1.4 %collective-permute-start.22 = (bf16[3,128,256]{2,1,0:T(8,128)(2,1)S(1)}, bf16[3,128,256]{2,1,0:T(8,128)(2,1)S(1)}, u32[]{:S(2)}, u32[]{:S(2)}) collective-permute-start(bf16[3,128,256]{2,1,0:T(8,128)(2,1)S(1)} %get-tuple-element.89), channel_id=1, source_target_pairs={{0,4},{1,5},{2,6},{3,7},{4,0},{5,1},{6,2},{7,3},{8,12},{9,13},{10,... | collective-permute-start | bytes 589832 | tf_op jit(solution)/shard_map/ppermute | solution.py:479
  78.2 2.8 %collective-permute-done.18.rest_1_ = bf16[256,1024]{1,0:T(8,128)(2,1)S(1)} collective-permute-done((bf16[256,1024]{1,0:T(8,128)(2,1)S(1)}, bf16[256,1024]{1,0:T(8,128)(2,1)S(1)}, u32[]{:S(2)}, u32[]{:S(2)}) %collective-permute-start.18) | collective-permute-done | bytes 524320 | tf_op jit(solution)/shard_map/ppermute | solution.py:479
  81.0 0.2 shard_map.121
  81.1 3.1 %collective-permute-done.28.rest_0_ = bf16[1,128,1024]{2,1,0:T(8,128)(2,1)S(1)} collective-permute-done((bf16[1,128,1024]{2,1,0:T(8,128)(2,1)S(1)}, bf16[1,128,1024]{2,1,0:T(8,128)(2,1)S(1)}, u32[]{:S(2)}, u32[]{:S(2)}) %collective-permute-start.28) | collective-permute-done | bytes 262176 | tf_op jit(solution)/shard_map/ppermute | solution.py:482
  84.3 0.6 collective-permute-start.29
  84.9 1.0 %collective-permute-start.24 = (bf16[3,128,256]{2,1,0:T(8,128)(2,1)S(1)}, bf16[3,128,256]{2,1,0:T(8,128)(2,1)S(1)}, u32[]{:S(2)}, u32[]{:S(2)}) collective-permute-start(bf16[3,128,256]{2,1,0:T(8,128)(2,1)S(1)} %get-tuple-element.91), channel_id=1, source_target_pairs={{0,3},{1,2},{2,1},{3,0},{4,7},{5,6},{6,5},{7,4},{8,11},{9,10},{10,... | collective-permute-start | bytes 589832 | tf_op jit(solution)/shard_map/ppermute | solution.py:479
  85.9 3.1 %collective-permute-done.22.rest_3_ = bf16[3,128,256]{2,1,0:T(8,128)(2,1)S(1)} collective-permute-done((bf16[3,128,256]{2,1,0:T(8,128)(2,1)S(1)}, bf16[3,128,256]{2,1,0:T(8,128)(2,1)S(1)}, u32[]{:S(2)}, u32[]{:S(2)}) %collective-permute-start.22) | collective-permute-done | bytes 196640 | tf_op jit(solution)/shard_map/ppermute | solution.py:479
  89.0 1.5 %collective-permute-start.26 = (bf16[3,128,256]{2,1,0:T(8,128)(2,1)S(1)}, bf16[3,128,256]{2,1,0:T(8,128)(2,1)S(1)}, u32[]{:S(2)}, u32[]{:S(2)}) collective-permute-start(bf16[3,128,256]{2,1,0:T(8,128)(2,1)S(1)} %get-tuple-element.93), channel_id=1, source_target_pairs={{0,1},{1,0},{2,3},{3,2},{4,5},{5,4},{6,7},{7,6},{8,9},{9,8},{10,11... | collective-permute-start | bytes 589832 | tf_op jit(solution)/shard_map/ppermute | solution.py:479
  90.5 1.3 %collective-permute-done.24.rest_5_ = bf16[3,128,256]{2,1,0:T(8,128)(2,1)S(1)} collective-permute-done((bf16[3,128,256]{2,1,0:T(8,128)(2,1)S(1)}, bf16[3,128,256]{2,1,0:T(8,128)(2,1)S(1)}, u32[]{:S(2)}, u32[]{:S(2)}) %collective-permute-start.24) | collective-permute-done | bytes 196640 | tf_op jit(solution)/shard_map/ppermute | solution.py:479
  91.8 4.3 %collective-permute-done.25.rest_6_ = bf16[3,128,256]{2,1,0:T(8,128)(2,1)S(1)} collective-permute-done((bf16[3,128,256]{2,1,0:T(8,128)(2,1)S(1)}, bf16[3,128,256]{2,1,0:T(8,128)(2,1)S(1)}, u32[]{:S(2)}, u32[]{:S(2)}) %collective-permute-start.25) | collective-permute-done | bytes 196640 | tf_op jit(solution)/shard_map/ppermute | solution.py:479
  96.1 1.5 %shard_map.123 = (bf16[1,128,2048]{2,1,0:T(8,128)(2,1)}, bf16[1,128,2048]{2,1,0:T(8,128)(2,1)}, bf16[1,128,2048]{2,1,0:T(8,128)(2,1)}) custom-call(bf16[3,128,256]{2,1,0:T(8,128)(2,1)S(1)} %get-tuple-element.77.rest_0_, bf16[3,128,256]{2,1,0:T(8,128)(2,1)S(1)} %collective-permute-done.20.rest_1_, bf16[3,128,256]{2,1,0:T(8,128)(2,1)S(1)} %collective-permute-done.21.rest_2_, ...), custom_call_target="tpu_custom_call" | custom-call | bytes 3145728 | tf_op jit(solution)/shard_map/pallas_call | solution.py:43
  97.7 0.9 shard_map.122
  98.6 0.9 shard_map.126
  (33 shorter events, 1.0 us)
Async XLA Ops:
  1.6 26.9 %copy-start = (s32[1,8,8]{2,1,0:T(8,128)S(1)}, s32[1,8,8]{2,1,0:T(8,128)}, u32[]{:S(2)}) copy-start(s32[1,8,8]{2,1,0:T(8,128)} %adj_ref.1) | copy-start | bytes 772
  1.6 26.9 %copy-start.1 = (s32[1,8]{1,0:T(1,128)S(1)}, s32[1,8]{1,0:T(1,128)}, u32[]{:S(2)}) copy-start(s32[1,8]{1,0:T(1,128)} %cnt_ref.1) | copy-start | bytes 100
  1.6 17.4 %collective-permute-start.8 = (bf16[1,128,1024]{2,1,0:T(8,128)(2,1)S(1)}, bf16[1,128,1024]{2,1,0:T(8,128)(2,1)S(1)}, u32[]{:S(2)}, u32[]{:S(2)}) collective-permute-start(bf16[1,128,1024]{2,1,0:T(8,128)(2,1)S(1)} %bitcast.4), channel_id=1, source_target_pairs={{0,16},{8,24},{16,0},{24,8},{1,17},{9,25},{17,1},{25,9},{2,18},{10... | collective-permute-start | bytes 786440 | tf_op jit(solution)/shard_map/ppermute | solution.py:482
  6.4 13.4 %collective-permute-start.10 = (bf16[128,1024]{1,0:T(8,128)(2,1)S(1)}, bf16[128,1024]{1,0:T(8,128)(2,1)S(1)}, u32[]{:S(2)}, u32[]{:S(2)}) collective-permute-start(bf16[128,1024]{1,0:T(8,128)(2,1)S(1)} %get-tuple-element.65), channel_id=1, source_target_pairs={{0,1},{1,0},{2,3},{3,2},{4,5},{5,4},{6,7},{7,6},{8,9},{9,8},{10,11... | collective-permute-start | bytes 786440 | tf_op jit(solution)/shard_map/ppermute | solution.py:479
  6.5 8.7 %collective-permute-start = (bf16[3,128,256]{2,1,0:T(8,128)(2,1)S(1)}, bf16[3,128,256]{2,1,0:T(8,128)(2,1)S(1)}, u32[]{:S(2)}, u32[]{:S(2)}) collective-permute-start(bf16[3,128,256]{2,1,0:T(8,128)(2,1)S(1)} %get-tuple-element.55), channel_id=1, source_target_pairs={{0,6},{1,7},{2,4},{3,5},{4,2},{5,3},{6,0},{7,1},{8,14},{9,15},{10,... | collective-permute-start | bytes 589832 | tf_op jit(solution)/shard_map/ppermute | solution.py:479
  8.1 11.0 %collective-permute-start.1 = (bf16[3,128,256]{2,1,0:T(8,128)(2,1)S(1)}, bf16[3,128,256]{2,1,0:T(8,128)(2,1)S(1)}, u32[]{:S(2)}, u32[]{:S(2)}) collective-permute-start(bf16[3,128,256]{2,1,0:T(8,128)(2,1)S(1)} %get-tuple-element.56), channel_id=1, source_target_pairs={{0,2},{1,3},{2,0},{3,1},{4,6},{5,7},{6,4},{7,5},{8,10},{9,11},{10,... | collective-permute-start | bytes 589832 | tf_op jit(solution)/shard_map/ppermute | solution.py:479
  9.6 10.4 %collective-permute-start.2 = (bf16[3,128,256]{2,1,0:T(8,128)(2,1)S(1)}, bf16[3,128,256]{2,1,0:T(8,128)(2,1)S(1)}, u32[]{:S(2)}, u32[]{:S(2)}) collective-permute-start(bf16[3,128,256]{2,1,0:T(8,128)(2,1)S(1)} %get-tuple-element.57), channel_id=1, source_target_pairs={{0,4},{1,5},{2,6},{3,7},{4,0},{5,1},{6,2},{7,3},{8,12},{9,13},{10,... | collective-permute-start | bytes 589832 | tf_op jit(solution)/shard_map/ppermute | solution.py:479
  15.2 8.2 %collective-permute-start.3 = (bf16[3,128,256]{2,1,0:T(8,128)(2,1)S(1)}, bf16[3,128,256]{2,1,0:T(8,128)(2,1)S(1)}, u32[]{:S(2)}, u32[]{:S(2)}) collective-permute-start(bf16[3,128,256]{2,1,0:T(8,128)(2,1)S(1)} %get-tuple-element.58), channel_id=1, source_target_pairs={{0,7},{1,6},{2,5},{3,4},{4,3},{5,2},{6,1},{7,0},{8,15},{9,14},{10,... | collective-permute-start | bytes 589832 | tf_op jit(solution)/shard_map/ppermute | solution.py:479
  19.0 8.5 %collective-permute-start.4 = (bf16[3,128,256]{2,1,0:T(8,128)(2,1)S(1)}, bf16[3,128,256]{2,1,0:T(8,128)(2,1)S(1)}, u32[]{:S(2)}, u32[]{:S(2)}) collective-permute-start(bf16[3,128,256]{2,1,0:T(8,128)(2,1)S(1)} %get-tuple-element.59), channel_id=1, source_target_pairs={{0,3},{1,2},{2,1},{3,0},{4,7},{5,6},{6,5},{7,4},{8,11},{9,10},{10,... | collective-permute-start | bytes 589832 | tf_op jit(solution)/shard_map/ppermute | solution.py:479
  19.0 8.9 %collective-permute-start.5 = (bf16[3,128,256]{2,1,0:T(8,128)(2,1)S(1)}, bf16[3,128,256]{2,1,0:T(8,128)(2,1)S(1)}, u32[]{:S(2)}, u32[]{:S(2)}) collective-permute-start(bf16[3,128,256]{2,1,0:T(8,128)(2,1)S(1)} %get-tuple-element.60), channel_id=1, source_target_pairs={{0,5},{1,4},{2,7},{3,6},{4,1},{5,0},{6,3},{7,2},{8,13},{9,12},{10,... | collective-permute-start | bytes 589832 | tf_op jit(solution)/shard_map/ppermute | solution.py:479
  19.8 8.7 %collective-permute-start.6 = (bf16[3,128,256]{2,1,0:T(8,128)(2,1)S(1)}, bf16[3,128,256]{2,1,0:T(8,128)(2,1)S(1)}, u32[]{:S(2)}, u32[]{:S(2)}) collective-permute-start(bf16[3,128,256]{2,1,0:T(8,128)(2,1)S(1)} %get-tuple-element.61), channel_id=1, source_target_pairs={{0,1},{1,0},{2,3},{3,2},{4,5},{5,4},{6,7},{7,6},{8,9},{9,8},{10,11... | collective-permute-start | bytes 589832 | tf_op jit(solution)/shard_map/ppermute | solution.py:479
  19.9 14.4 %collective-permute-start.9 = (bf16[2,128,1024]{2,1,0:T(8,128)(2,1)S(1)}, bf16[2,128,1024]{2,1,0:T(8,128)(2,1)S(1)}, u32[]{:S(2)}, u32[]{:S(2)}) collective-permute-start(bf16[2,128,1024]{2,1,0:T(8,128)(2,1)S(1)} %shard_map.113.mine_ref), channel_id=1, source_target_pairs={{0,8},{8,0},{16,24},{24,16},{1,9},{9,1},{17,25},{25,17},{2,10},{10... | collective-permute-start | bytes 1572872 | tf_op jit(solution)/shard_map/ppermute | solution.py:482
  23.4 15.8 %collective-permute-start.13 = (bf16[256,1024]{1,0:T(8,128)(2,1)S(1)}, bf16[256,1024]{1,0:T(8,128)(2,1)S(1)}, u32[]{:S(2)}, u32[]{:S(2)}) collective-permute-start(bf16[256,1024]{1,0:T(8,128)(2,1)S(1)} %shard_map.115.rest_0_), channel_id=1, source_target_pairs={{0,6},{1,7},{2,4},{3,5},{4,2},{5,3},{6,0},{7,1},{8,14},{9,15},{10,... | collective-permute-start | bytes 1572872 | tf_op jit(solution)/shard_map/ppermute | solution.py:479
  27.5 22.4 %collective-permute-start.12 = (bf16[256,1024]{1,0:T(8,128)(2,1)S(1)}, bf16[256,1024]{1,0:T(8,128)(2,1)S(1)}, u32[]{:S(2)}, u32[]{:S(2)}) collective-permute-start(bf16[256,1024]{1,0:T(8,128)(2,1)S(1)} %shard_map.115.rest_0_), channel_id=1, source_target_pairs={{0,4},{1,5},{2,6},{3,7},{4,0},{5,1},{6,2},{7,3},{8,12},{9,13},{10,... | collective-permute-start | bytes 1572872 | tf_op jit(solution)/shard_map/ppermute | solution.py:479
  28.0 22.0 %collective-permute-start.11 = (bf16[256,1024]{1,0:T(8,128)(2,1)S(1)}, bf16[256,1024]{1,0:T(8,128)(2,1)S(1)}, u32[]{:S(2)}, u32[]{:S(2)}) collective-permute-start(bf16[256,1024]{1,0:T(8,128)(2,1)S(1)} %shard_map.115.rest_0_), channel_id=1, source_target_pairs={{0,2},{1,3},{2,0},{3,1},{4,6},{5,7},{6,4},{7,5},{8,10},{9,11},{10,... | collective-permute-start | bytes 1572872 | tf_op jit(solution)/shard_map/ppermute | solution.py:479
  33.5 17.9 %collective-permute-start.7 = (bf16[1024,256]{1,0:T(8,128)(2,1)S(1)}, bf16[1024,256]{1,0:T(8,128)(2,1)S(1)}, u32[]{:S(2)}, u32[]{:S(2)}) collective-permute-start(bf16[1024,256]{1,0:T(8,128)(2,1)S(1)} %get-tuple-element.63), channel_id=1, source_target_pairs={{0,1},{1,0},{2,3},{3,2},{4,5},{5,4},{6,7},{7,6},{8,9},{9,8},{10,11... | collective-permute-start | bytes 1572872 | tf_op jit(solution)/shard_map/ppermute | solution.py:479
  51.3 13.5 %collective-permute-start.14 = (bf16[256,1024]{1,0:T(8,128)(2,1)S(1)}, bf16[256,1024]{1,0:T(8,128)(2,1)S(1)}, u32[]{:S(2)}, u32[]{:S(2)}) collective-permute-start(bf16[256,1024]{1,0:T(8,128)(2,1)S(1)} %get-tuple-element.76), channel_id=1, source_target_pairs={{0,1},{1,0},{2,3},{3,2},{4,5},{5,4},{6,7},{7,6},{8,9},{9,8},{10,11... | collective-permute-start | bytes 1572872 | tf_op jit(solution)/shard_map/ppermute | solution.py:479
  52.7 8.8 %collective-permute-start.15 = (bf16[128,1024]{1,0:T(8,128)(2,1)S(1)}, bf16[128,1024]{1,0:T(8,128)(2,1)S(1)}, u32[]{:S(2)}, u32[]{:S(2)}) collective-permute-start(bf16[128,1024]{1,0:T(8,128)(2,1)S(1)} %get-tuple-element.80), channel_id=1, source_target_pairs={{0,2},{1,3},{2,0},{3,1},{4,6},{5,7},{6,4},{7,5},{8,10},{9,11},{10,... | collective-permute-start | bytes 786440 | tf_op jit(solution)/shard_map/ppermute | solution.py:479
  53.3 8.4 %collective-permute-start.16 = (bf16[128,1024]{1,0:T(8,128)(2,1)S(1)}, bf16[128,1024]{1,0:T(8,128)(2,1)S(1)}, u32[]{:S(2)}, u32[]{:S(2)}) collective-permute-start(bf16[128,1024]{1,0:T(8,128)(2,1)S(1)} %get-tuple-element.82), channel_id=1, source_target_pairs={{0,4},{1,5},{2,6},{3,7},{4,0},{5,1},{6,2},{7,3},{8,12},{9,13},{10,... | collective-permute-start | bytes 786440 | tf_op jit(solution)/shard_map/ppermute | solution.py:479
  56.2 14.2 %collective-permute-start.27 = (bf16[2,128,1024]{2,1,0:T(8,128)(2,1)S(1)}, bf16[2,128,1024]{2,1,0:T(8,128)(2,1)S(1)}, u32[]{:S(2)}, u32[]{:S(2)}) collective-permute-start(bf16[2,128,1024]{2,1,0:T(8,128)(2,1)S(1)} %get-tuple-element.98), channel_id=1, source_target_pairs={{0,8},{8,0},{16,24},{24,16},{1,9},{9,1},{17,25},{25,17},{2,10},{10... | collective-permute-start | bytes 1572872 | tf_op jit(solution)/shard_map/ppermute | solution.py:482
  61.8 14.9 %collective-permute-start.17 = (bf16[256,1024]{1,0:T(8,128)(2,1)S(1)}, bf16[256,1024]{1,0:T(8,128)(2,1)S(1)}, u32[]{:S(2)}, u32[]{:S(2)}) collective-permute-start(bf16[256,1024]{1,0:T(8,128)(2,1)S(1)} %get-tuple-element.83), channel_id=1, source_target_pairs={{0,2},{1,3},{2,0},{3,1},{4,6},{5,7},{6,4},{7,5},{8,10},{9,11},{10,... | collective-permute-start | bytes 1572872 | tf_op jit(solution)/shard_map/ppermute | solution.py:479
  63.4 17.5 %collective-permute-start.18 = (bf16[256,1024]{1,0:T(8,128)(2,1)S(1)}, bf16[256,1024]{1,0:T(8,128)(2,1)S(1)}, u32[]{:S(2)}, u32[]{:S(2)}) collective-permute-start(bf16[256,1024]{1,0:T(8,128)(2,1)S(1)} %get-tuple-element.84), channel_id=1, source_target_pairs={{0,4},{1,5},{2,6},{3,7},{4,0},{5,1},{6,2},{7,3},{8,12},{9,13},{10,... | collective-permute-start | bytes 1572872 | tf_op jit(solution)/shard_map/ppermute | solution.py:479
  70.6 13.6 %collective-permute-start.28 = (bf16[1,128,1024]{2,1,0:T(8,128)(2,1)S(1)}, bf16[1,128,1024]{2,1,0:T(8,128)(2,1)S(1)}, u32[]{:S(2)}, u32[]{:S(2)}) collective-permute-start(bf16[1,128,1024]{2,1,0:T(8,128)(2,1)S(1)} %get-tuple-element.100), channel_id=1, source_target_pairs={{0,16},{8,24},{16,0},{24,8},{1,17},{9,25},{17,1},{25,9},{2,18},{10... | collective-permute-start | bytes 786440 | tf_op jit(solution)/shard_map/ppermute | solution.py:482
  71.0 13.3 %collective-permute-start.20 = (bf16[3,128,256]{2,1,0:T(8,128)(2,1)S(1)}, bf16[3,128,256]{2,1,0:T(8,128)(2,1)S(1)}, u32[]{:S(2)}, u32[]{:S(2)}) collective-permute-start(bf16[3,128,256]{2,1,0:T(8,128)(2,1)S(1)} %get-tuple-element.87), channel_id=1, source_target_pairs={{0,6},{1,7},{2,4},{3,5},{4,2},{5,3},{6,0},{7,1},{8,14},{9,15},{10,... | collective-permute-start | bytes 589832 | tf_op jit(solution)/shard_map/ppermute | solution.py:479
  72.1 12.7 %collective-permute-start.21 = (bf16[3,128,256]{2,1,0:T(8,128)(2,1)S(1)}, bf16[3,128,256]{2,1,0:T(8,128)(2,1)S(1)}, u32[]{:S(2)}, u32[]{:S(2)}) collective-permute-start(bf16[3,128,256]{2,1,0:T(8,128)(2,1)S(1)} %get-tuple-element.88), channel_id=1, source_target_pairs={{0,2},{1,3},{2,0},{3,1},{4,6},{5,7},{6,4},{7,5},{8,10},{9,11},{10,... | collective-permute-start | bytes 589832 | tf_op jit(solution)/shard_map/ppermute | solution.py:479
  76.8 12.2 %collective-permute-start.22 = (bf16[3,128,256]{2,1,0:T(8,128)(2,1)S(1)}, bf16[3,128,256]{2,1,0:T(8,128)(2,1)S(1)}, u32[]{:S(2)}, u32[]{:S(2)}) collective-permute-start(bf16[3,128,256]{2,1,0:T(8,128)(2,1)S(1)} %get-tuple-element.89), channel_id=1, source_target_pairs={{0,4},{1,5},{2,6},{3,7},{4,0},{5,1},{6,2},{7,3},{8,12},{9,13},{10,... | collective-permute-start | bytes 589832 | tf_op jit(solution)/shard_map/ppermute | solution.py:479
  80.9 8.0 %collective-permute-start.23 = (bf16[3,128,256]{2,1,0:T(8,128)(2,1)S(1)}, bf16[3,128,256]{2,1,0:T(8,128)(2,1)S(1)}, u32[]{:S(2)}, u32[]{:S(2)}) collective-permute-start(bf16[3,128,256]{2,1,0:T(8,128)(2,1)S(1)} %get-tuple-element.90), channel_id=1, source_target_pairs={{0,7},{1,6},{2,5},{3,4},{4,3},{5,2},{6,1},{7,0},{8,15},{9,14},{10,... | collective-permute-start | bytes 589832 | tf_op jit(solution)/shard_map/ppermute | solution.py:479
  84.2 13.5 %collective-permute-start.19 = (bf16[128,1024]{1,0:T(8,128)(2,1)S(1)}, bf16[128,1024]{1,0:T(8,128)(2,1)S(1)}, u32[]{:S(2)}, u32[]{:S(2)}) collective-permute-start(bf16[128,1024]{1,0:T(8,128)(2,1)S(1)} %get-tuple-element.86), channel_id=1, source_target_pairs={{0,1},{1,0},{2,3},{3,2},{4,5},{5,4},{6,7},{7,6},{8,9},{9,8},{10,11... | collective-permute-start | bytes 786440 | tf_op jit(solution)/shard_map/ppermute | solution.py:479
  84.3 14.3 %collective-permute-start.29 = (f32[64,1024]{1,0:T(8,128)S(1)}, f32[64,1024]{1,0:T(8,128)S(1)}, u32[]{:S(2)}, u32[]{:S(2)}) collective-permute-start(f32[64,1024]{1,0:T(8,128)S(1)} %get-tuple-element.102), channel_id=1, source_target_pairs={{0,1},{1,0},{2,3},{3,2},{4,5},{5,4},{6,7},{7,6},{8,9},{9,8},{10,11... | collective-permute-start | bytes 786440 | tf_op jit(solution)/shard_map/ppermute | solution.py:479
  84.9 7.0 %collective-permute-start.24 = (bf16[3,128,256]{2,1,0:T(8,128)(2,1)S(1)}, bf16[3,128,256]{2,1,0:T(8,128)(2,1)S(1)}, u32[]{:S(2)}, u32[]{:S(2)}) collective-permute-start(bf16[3,128,256]{2,1,0:T(8,128)(2,1)S(1)} %get-tuple-element.91), channel_id=1, source_target_pairs={{0,3},{1,2},{2,1},{3,0},{4,7},{5,6},{6,5},{7,4},{8,11},{9,10},{10,... | collective-permute-start | bytes 589832 | tf_op jit(solution)/shard_map/ppermute | solution.py:479
  89.0 7.2 %collective-permute-start.25 = (bf16[3,128,256]{2,1,0:T(8,128)(2,1)S(1)}, bf16[3,128,256]{2,1,0:T(8,128)(2,1)S(1)}, u32[]{:S(2)}, u32[]{:S(2)}) collective-permute-start(bf16[3,128,256]{2,1,0:T(8,128)(2,1)S(1)} %get-tuple-element.92), channel_id=1, source_target_pairs={{0,5},{1,4},{2,7},{3,6},{4,1},{5,0},{6,3},{7,2},{8,13},{9,12},{10,... | collective-permute-start | bytes 589832 | tf_op jit(solution)/shard_map/ppermute | solution.py:479
  89.0 7.2 %collective-permute-start.26 = (bf16[3,128,256]{2,1,0:T(8,128)(2,1)S(1)}, bf16[3,128,256]{2,1,0:T(8,128)(2,1)S(1)}, u32[]{:S(2)}, u32[]{:S(2)}) collective-permute-start(bf16[3,128,256]{2,1,0:T(8,128)(2,1)S(1)} %get-tuple-element.93), channel_id=1, source_target_pairs={{0,1},{1,0},{2,3},{3,2},{4,5},{5,4},{6,7},{7,6},{8,9},{9,8},{10,11... | collective-permute-start | bytes 589832 | tf_op jit(solution)/shard_map/ppermute | solution.py:479

commit v3 on v0

--- a/solution.py
+++ b/solution.py
@@ -1,11 +1,66 @@
+import functools
+
 import jax
 import jax.numpy as jnp
 from jax import lax
+from jax.experimental import pallas as pl
+from jax.experimental.pallas import tpu as pltpu
 from jax.sharding import PartitionSpec as P
 
 HD = 128
 BLK = 128
 NBR = 8
+F32 = jnp.float32
+BF16 = jnp.bfloat16
+NN = (((1,), (0,)), ((), ()))
+NT = (((1,), (1,)), ((), ()))
+LOG2E = 1.4426950408889634
+DEAD = -1e30
+VMEM = pl.BlockSpec(memory_space=pltpu.VMEM)
+SMEM = pl.BlockSpec(memory_space=pltpu.SMEM)
+HBM = pl.BlockSpec(memory_space=pltpu.HBM)
+ANY = pl.BlockSpec(memory_space=pl.ANY)
+MIB = 1 << 20
+
+
+def mm(a, b, dims=NN):
+    return lax.dot_general(a, b, dims, preferred_element_type=F32)
+
+
+def in_hbm(x):
+    return pltpu.with_memory_space_constraint(x, pltpu.HBM)
+
+
+def sds(shape, dtype):
+    return jax.ShapeDtypeStruct(shape, dtype)
+
+
+def after(x, *deps):
+    return lax.optimization_barrier((x,) + deps)[0]
+
+
+def call(kernel, ins, outs, scratch=(), flops=0, moved=0, vmem=24):
+    return pl.pallas_call(
+        kernel,
+        out_shape=tuple(shape for _, shape in outs),
+        in_specs=[spec for spec, _ in ins],
+        out_specs=tuple(spec for spec, _ in outs),
+        scratch_shapes=list(scratch),
+        compiler_params=pltpu.CompilerParams(vmem_limit_bytes=vmem * MIB),
+        cost_estimate=pl.CostEstimate(flops=flops, bytes_accessed=moved, transcendentals=0),
+    )(*[arg for _, arg in ins])
+
+
+def col_of(dev, g, pairs, per):
+    return pl.multiple_of(((dev % 2 * per + g) * pairs + dev // 2) * HD, HD)
+
+
+def copies(moves, sems):
+    handles = [pltpu.make_async_copy(src, dst, sems.at[n]) for n, (src, dst) in enumerate(moves)]
+    for handle in handles:
+        handle.start()
+    for handle in handles:
+        handle.wait()
 
 
 def attend(query_blk, key_blk, value_blk, links, live_count):
@@ -131,6 +186,378 @@
     )
 
 
+def prep_kernel(n, per, q_ref, k_ref, v_ref, c_ref, w_ref, *rest):
+    qkv, (same, other, wsend, sems) = by_slot(rest[:-4], n), rest[-4:]
+    s = lax.axis_index("seq")
+    core = s % 2
+    half = c_ref.shape[2] // 2
+    moves = []
+    for j in range(n):
+        for t, src in enumerate((q_ref, k_ref, v_ref)):
+            for g in range(per):
+                col = col_of(s ^ j, g, n // 2, per)
+                moves.append((src.at[0, :, pl.ds(col, HD)], qkv[j].at[t, :, pl.ds(g * HD, HD)]))
+    mine = pl.multiple_of(core * half, half)
+    theirs = pl.multiple_of((1 - core) * half, half)
+    moves.append((c_ref.at[0, :, pl.ds(mine, half)], same))
+    moves.append((c_ref.at[0, :, pl.ds(theirs, half)], other))
+    row = pl.multiple_of((s // 2) * HD, HD)
+    moves.append((w_ref.at[pl.ds(row, HD), pl.ds(mine, half)], wsend))
+    copies(moves, sems)
+
+
+def order(n):
+    return sorted(range(1, n), key=lambda j: (j == 1, j % 2, -j.bit_count(), j))
+
+
+def by_slot(refs, n):
+    slots = dict(zip([0] + order(n), refs))
+    return [slots[j] for j in range(n)]
+
+
+def stack_kernel(first_ref, second_ref, out_ref):
+    rows = first_ref.shape[0]
+    out_ref[:rows] = first_ref[...]
+    out_ref[rows:] = second_ref[...]
+
+
+def forward_kernel(n, per, adj_ref, cnt_ref, *rest):
+    qkv, rest = by_slot(rest[:-11], n), rest[-11:]
+    attn_ref, swap_ref, attn_t_ref, expo, share_ref, queries, keys_t, vals, keys, vals_t, score = rest
+    s = lax.axis_index("seq")
+    length = n * BLK
+    tile = 2 * BLK
+    scale = HD**-0.5 * LOG2E
+    place = lax.broadcasted_iota(jnp.int32, (n, BLK), 0)
+    biases = []
+    for i in range(n):
+        block = s ^ i
+        count = cnt_ref[0, block]
+        bias = jnp.full((n, BLK), DEAD, F32)
+        for slot in range(NBR):
+            j = jnp.where(slot < count, adj_ref[0, block, slot] ^ s, n)
+            bias = jnp.where(place == j, 0.0, bias)
+        biases.append(bias)
+    for g in range(per):
+        lanes = slice(g * HD, (g + 1) * HD)
+        for j in range(n):
+            rows = slice(j * BLK, (j + 1) * BLK)
+            queries[g, rows, :] = qkv[j][0, :, lanes]
+            key, val = qkv[j][1, :, lanes], qkv[j][2, :, lanes]
+            keys[rows, :] = key
+            keys_t[g, :, rows] = key.T
+            vals[g, rows, :] = val
+            vals_t[:, rows] = val.T
+        for t in range(length // tile):
+            cols = slice(t * tile, (t + 1) * tile)
+            bias = jnp.concatenate(biases[2 * t : 2 * t + 2], axis=1)
+            query = queries[g, cols, :]
+            highest = jnp.full((1, tile), -jnp.inf, F32)
+            for j in range(n):
+                rows = slice(j * BLK, (j + 1) * BLK)
+                part = mm(keys[rows, :], query, NT) * scale + bias[j : j + 1]
+                score[rows, :] = part
+                highest = jnp.maximum(highest, jnp.max(part, axis=0, keepdims=True))
+            total = jnp.zeros((1, tile), F32)
+            for j in range(n):
+                rows = slice(j * BLK, (j + 1) * BLK)
+                part = jnp.exp2(score[rows, :] - highest)
+                total = total + jnp.sum(part, axis=0, keepdims=True)
+                expo[g, rows, cols] = part.astype(BF16)
+            share = 1.0 / total
+            share_ref[g : g + 1, cols] = share
+            att = (mm(vals_t[...], expo[g, :, cols]) * share).astype(BF16)
+            attn_t_ref[g, :, cols] = att
+            first, second = att[:, :BLK].T, att[:, BLK:].T
+            base = t * tile
+            attn_ref[base : base + BLK, lanes] = first
+            attn_ref[base + BLK : base + tile, lanes] = second
+            swap_ref[base : base + BLK, lanes] = second
+            swap_ref[base + BLK : base + tile, lanes] = first
+
+
+def grow_kernel(bit, mine_ref, recv_ref, out_ref):
+    here = lax.axis_index("dp") // bit % 2
+    for i in range(mine_ref.shape[0]):
+        out_ref[2 * i + here] = mine_ref[i]
+        out_ref[2 * i + 1 - here] = recv_ref[i]
+
+
+def halve(total, bit, keep_ref, send_ref):
+    here = lax.axis_index("dp") // bit % 2
+    for i in range(keep_ref.shape[0]):
+        keep_ref[i] = jnp.where(here == 0, total[2 * i], total[2 * i + 1])
+        send_ref[i] = jnp.where(here == 0, total[2 * i + 1], total[2 * i]).astype(BF16)
+
+
+def fold_kernel(bit, mine_ref, recv_ref, keep_ref, send_ref):
+    halve(mine_ref[...] + recv_ref[...].astype(F32), bit, keep_ref, send_ref)
+
+
+def grad_attn_kernel(n, per, *rest):
+    cot, rest = rest[:-4], rest[-4:]
+    w_ref, own_ref, send_ref, cot_out = rest
+    core = lax.axis_index("seq") % 2
+    mine = w_ref[pl.ds(pl.multiple_of(core * per * HD, HD), per * HD), :]
+    theirs = w_ref[pl.ds(pl.multiple_of((1 - core) * per * HD, HD), per * HD), :]
+    rows = n * BLK // len(cot)
+    for j, ref in enumerate(cot):
+        cot_out[j * rows : (j + 1) * rows, :] = ref[...]
+    for t in range(n // 2):
+        base = 2 * t * BLK
+        rows = cot_out[base : base + 2 * BLK, :]
+        own_ref[:, base : base + 2 * BLK] = mm(mine, rows, NT)
+        part = mm(theirs, rows, NT).astype(BF16)
+        send_ref[:, base : base + BLK] = part[:, BLK:]
+        send_ref[:, base + BLK : base + 2 * BLK] = part[:, :BLK]
+
+
+def backward_kernel(n, per, expo, share_ref, queries, keys_t, vals, attn_t_ref, own_ref, recv_ref, *rest):
+    outs, (dscores,) = by_slot(rest[:-1], n), rest[-1:]
+    scale = HD**-0.5
+    tile = 2 * BLK
+    length = n * BLK
+    for g in range(per):
+        lanes = slice(g * HD, (g + 1) * HD)
+        full = (own_ref[lanes, :] + recv_ref[lanes, :].astype(F32)) * share_ref[g : g + 1, :]
+        grad = full.astype(BF16)
+        delta = jnp.sum(full * attn_t_ref[g].astype(F32), axis=0, keepdims=True)
+        for t in range(length // tile):
+            cols = slice(t * tile, (t + 1) * tile)
+            dprob = mm(vals[g], grad[:, cols])
+            dscores[:, cols] = (expo[g, :, cols].astype(F32) * (dprob - delta[:, cols])).astype(BF16)
+        for t in range(length // tile):
+            rows = slice(t * tile, (t + 1) * tile)
+            dvalue = mm(expo[g, rows, :], grad, NT).astype(BF16)
+            dkey = (mm(dscores[rows, :], queries[g]) * scale).astype(BF16)
+            dquery = (mm(keys_t[g], dscores[:, rows]).T * scale).astype(BF16)
+            for b in range(2):
+                part = slice(b * BLK, (b + 1) * BLK)
+                outs[2 * t + b][0, :, lanes] = dquery[part]
+                outs[2 * t + b][1, :, lanes] = dkey[part]
+                outs[2 * t + b][2, :, lanes] = dvalue[part]
+
+
+def out_kernel(n, attn_ref, recv_ref, w_ref, *outs):
+    core = lax.axis_index("seq") % 2
+    tile = 2 * BLK
+    heads = attn_ref.shape[1]
+    mine = w_ref[pl.ds(pl.multiple_of(core * heads, heads), heads), :]
+    theirs = w_ref[pl.ds(pl.multiple_of((1 - core) * heads, heads), heads), :]
+    for t in range(n // 2):
+        rows = slice(t * tile, (t + 1) * tile)
+        part = mm(attn_ref[rows, :], mine) + mm(recv_ref[rows, :], theirs)
+        if t < 3:
+            outs[t][...] = part.astype(outs[t].dtype)
+        else:
+            outs[3][...] = part[:BLK].astype(BF16)
+            outs[4][...] = part[BLK:].astype(BF16)
+
+
+def relay_kernel(first_ref, first_recv, second_ref, second_recv, *outs):
+    outs[0][:BLK] = first_ref[:BLK]
+    outs[0][BLK:] = (first_ref[BLK:].astype(F32) + second_recv[...].astype(F32)).astype(BF16)
+    outs[1][:BLK] = (second_ref[:BLK].astype(F32) + first_recv[...].astype(F32)).astype(BF16)
+    outs[1][BLK:] = second_ref[BLK:]
+
+
+def weight_kernel(per, attn_t_ref, recv_ref, cot_ref, keep_ref, send_ref, grads):
+    core = lax.axis_index("seq") % 2
+    for g in range(per):
+        grads[core * per + g] = mm(attn_t_ref[g], cot_ref[...])
+        recv = recv_ref[:, g * HD : (g + 1) * HD].T
+        grads[(1 - core) * per + g] = mm(recv, cot_ref[...])
+    halve(grads, 1, keep_ref, send_ref)
+
+
+def out_sum_kernel(own_ref, *rest):
+    parts, (keep_ref, send_ref) = rest[:-2], rest[-2:]
+    total = own_ref[...]
+    for part in parts:
+        total = total + part[...].astype(F32)
+    total = total.astype(BF16)
+    keep_ref[...] = total[:BLK]
+    send_ref[...] = total[BLK:]
+
+
+def weight_sum_kernel(own_ref, recv_ref, keep_ref, send_ref):
+    total = own_ref[0] + recv_ref[0].astype(F32)
+    half = total.shape[0] // 2
+    core = lax.axis_index("seq") % 2
+    keep_ref[...] = jnp.where(core == 0, total[:half], total[half:])
+    send_ref[...] = jnp.where(core == 0, total[half:], total[:half])
+
+
+def place_kernel(n, per, keep_ref, recv_ref, w_keep_ref, w_recv_ref, *rest):
+    parts, (out_ref, *outs, w_ref, sems) = by_slot(rest[:-6], n), rest[-6:]
+    s = lax.axis_index("seq")
+    core = s % 2
+    half = keep_ref.shape[1]
+    mine = pl.ds(pl.multiple_of(core * half, half), half)
+    theirs = pl.ds(pl.multiple_of((1 - core) * half, half), half)
+    moves = [
+        (keep_ref, out_ref.at[0, :, mine]),
+        (recv_ref, out_ref.at[0, :, theirs]),
+        (w_keep_ref, w_ref.at[:, mine]),
+        (w_recv_ref, w_ref.at[:, theirs]),
+    ]
+    for g in range(per):
+        for j in range(n):
+            col = col_of(s ^ j, g, n // 2, per)
+            for t in range(3):
+                src = parts[j].at[t, :, pl.ds(g * HD, HD)]
+                moves.append((src, outs[t].at[0, :, pl.ds(col, HD)]))
+    copies(moves, sems)
+
+
+def paired(n, nz, queries, key_rows, values, adjacency, counts, out_weight, out_cotangent):
+    per = nz // 2
+    pairs = n // 2
+    length = n * BLK
+    wide = queries.shape[2]
+    half = wide // 2
+    heads = per * HD
+    chunk = sds((3, BLK, heads), BF16)
+    piece = sds((BLK, half), BF16)
+    couple = sds((2 * BLK, half), BF16)
+
+    def to(x, j):
+        return lax.ppermute(x, "seq", [(i, i ^ j) for i in range(n)])
+
+    def to_z(x, j):
+        return lax.ppermute(x, "dp", [(i, i ^ j) for i in range(nz)])
+
+    def exchange(parts):
+        return [parts[0]] + [to(part, j) for part, j in zip(parts[1:], order(n))]
+
+    prep = call(
+        functools.partial(prep_kernel, n, per),
+        [(HBM, in_hbm(x)) for x in (queries, key_rows, values, out_cotangent, out_weight)],
+        [(VMEM, pltpu.VMEM(x.shape, x.dtype)) for x in [chunk] * n + [piece] * 3],
+        [pltpu.SemaphoreType.DMA((3 * n * per + 3,))],
+        moved=8 * MIB,
+    )
+    same, other, w_own = prep[n:]
+    qkv = exchange(prep[:n])
+    (cot_own,) = call(
+        stack_kernel, [(VMEM, same), (VMEM, to(other, 1))], [(VMEM, couple)], moved=MIB
+    )
+    sent = dict(zip(order(n), qkv[1:]))
+    cot_sent = after(cot_own, *[sent[j] for j in order(n)[: pairs - 1]])
+    cot = [cot_own] + [to(cot_sent, 2 * jc) for jc in range(1, pairs)]
+    w_rows = w_own[None]
+    bit = nz
+    while bit > 1:
+        bit //= 2
+        (w_rows,) = call(
+            functools.partial(grow_kernel, bit),
+            [(VMEM, w_rows), (VMEM, to_z(w_rows, bit))],
+            [(VMEM, sds((2 * w_rows.shape[0], HD, half), BF16))],
+            moved=2 * MIB,
+        )
+    w_rows = w_rows.reshape(nz * HD, half)
+
+    attn, swap, attn_t, *kept = call(
+        functools.partial(forward_kernel, n, per),
+        [(SMEM, adjacency), (SMEM, counts)] + [(VMEM, x) for x in qkv],
+        [
+            (VMEM, sds((length, heads), BF16)),
+            (VMEM, sds((length, heads), BF16)),
+            (VMEM, sds((per, HD, length), BF16)),
+            (VMEM, sds((per, length, length), BF16)),
+            (VMEM, sds((per, length), F32)),
+            (VMEM, sds((per, length, HD), BF16)),
+            (VMEM, sds((per, HD, length), BF16)),
+            (VMEM, sds((per, length, HD), BF16)),
+        ],
+        [
+            pltpu.VMEM((length, HD), BF16),
+            pltpu.VMEM((HD, length), BF16),
+            pltpu.VMEM((length, 2 * BLK), F32),
+        ],
+        flops=4 * per * length * length * HD,
+        moved=8 * MIB,
+    )
+    attn_recv = to(swap, 1)
+
+    grad_own, grad_send, cot_rows = call(
+        functools.partial(grad_attn_kernel, n, per),
+        [(VMEM, x) for x in cot + [w_rows]],
+        [
+            (VMEM, sds((heads, length), F32)),
+            (VMEM, sds((heads, length), BF16)),
+            (VMEM, sds((length, half), BF16)),
+        ],
+        flops=4 * length * heads * half,
+        moved=8 * MIB,
+    )
+    grad_recv = to(grad_send, 1)
+    out_own, out_x, out_y, out_far_x, out_far_y = call(
+        functools.partial(out_kernel, n),
+        [(VMEM, attn), (VMEM, attn_recv), (VMEM, after(w_rows, grad_own))],
+        [(VMEM, x) for x in (sds((2 * BLK, half), F32), couple, couple, piece, piece)],
+        flops=4 * length * heads * half,
+        moved=6 * MIB,
+    )
+    far_x, far_y = to(out_far_x, 2), to(out_far_y, 4)
+    w_keep, w_send = call(
+        functools.partial(weight_kernel, per),
+        [(VMEM, attn_t), (VMEM, attn_recv), (VMEM, cot_rows)],
+        [(VMEM, sds((per, HD, half), d)) for d in (F32, BF16)],
+        [pltpu.VMEM((nz, HD, half), F32)],
+        flops=4 * length * heads * half,
+        moved=6 * MIB,
+    )
+    grads = call(
+        functools.partial(backward_kernel, n, per),
+        [(VMEM, x) for x in kept + [attn_t, after(grad_own, w_keep, out_own), grad_recv]],
+        [(VMEM, chunk)] * n,
+        [pltpu.VMEM((length, length), BF16)],
+        flops=8 * per * length * length * HD,
+        moved=8 * MIB,
+    )
+    relayed = call(
+        relay_kernel,
+        [(VMEM, x) for x in (after(out_x, grads[0]), far_x, out_y, far_y)],
+        [(VMEM, couple)] * 2,
+        moved=3 * MIB,
+    )
+    out_recv = [to(relayed[0], 2), to(relayed[1], 4)]
+    back = exchange(grads)
+
+    bit = 1
+    while 2 * bit < nz:
+        w_keep, w_send = call(
+            functools.partial(fold_kernel, 2 * bit),
+            [(VMEM, w_keep), (VMEM, to_z(w_send, bit))],
+            [(VMEM, sds((w_keep.shape[0] // 2, HD, half), d)) for d in (F32, BF16)],
+            moved=2 * MIB,
+        )
+        bit *= 2
+    w_recv = to_z(w_send, bit)
+
+    out_keep, out_send = call(
+        out_sum_kernel,
+        [(VMEM, x) for x in [after(out_own, grads[0])] + out_recv],
+        [(VMEM, piece)] * 2,
+        moved=3 * MIB,
+    )
+    half_keep, half_send = call(
+        weight_sum_kernel,
+        [(VMEM, after(w_keep, out_keep, back[1])), (VMEM, w_recv)],
+        [(VMEM, sds((HD // 2, half), F32))] * 2,
+        moved=2 * MIB,
+    )
+    token = sds((1, BLK, wide), BF16)
+    return call(
+        functools.partial(place_kernel, n, per),
+        [(ANY, x) for x in [out_keep, to(out_send, 1), half_keep, to(half_send, 1)] + back],
+        [(ANY, token)] * 4 + [(ANY, sds((HD // 2, wide), F32))],
+        [pltpu.SemaphoreType.DMA((3 * n * per + 4,))],
+        moved=4 * MIB,
+    )
+
+
 def solution(mesh):
     in_specs = (
         P("dp", "seq", None),
@@ -148,4 +575,12 @@
         P("dp", "seq", None),
         P(("dp", "seq"), None),
     )
-    return jax.shard_map(local, mesh=mesh, in_specs=in_specs, out_specs=out_specs, check_vma=False)
+    n, nz = mesh.shape["seq"], mesh.shape["dp"]
+
+    def body(queries, *rest):
+        fits = queries.shape[1] == BLK and queries.shape[2] == nz * (n // 2) * HD
+        if fits and n == 8 and nz > 1 and nz & (nz - 1) == 0:
+            return paired(n, nz, queries, *rest)
+        return local(queries, *rest)
+
+    return jax.shard_map(body, mesh=mesh, in_specs=in_specs, out_specs=out_specs, check_vma=False)

time: 433 us -> 95.2 us (0.22); the launches traced: 427 us -> 95 us
  waiting for transfers between devices: 234 us -> 46.7 us
  matrix products: 65.5 us -> 0 us
  local copies, waits for them, and re-layouts: 40.1 us -> 0.01 us
  blocking collectives: 23.3 us -> 0 us
  Pallas kernels: 0 us -> 18.8 us
  other arithmetic: 14.2 us -> 0 us
  between operations: 14.6 us -> 0.98 us
  starting transfers between devices: 34.9 us -> 28.5 us
    reduce_scatter x1 -> x0, waiting for transfers between devices: 108 us -> none  [local(): lax.psum_scatter(lax.dot_general(columns, cotangent, (((0,), (0,)), ((),...]
    all_gather x1 -> x0, waiting for transfers between devices: 107 us -> none  [local(): lax.all_gather(out_weight, 'dp', axis=0, tiled=True)]
    dot_general x11 -> x0, matrix products: 65.5 us -> none  [the longest x1 10.6 us: backward(): jnp.einsum('ja,aqhd->jqhd', member, value_part.reshape(blocks * NBR, BLK,...]
    ppermute x0 -> x30, waiting for transfers between devices: none -> 46.7 us  [the longest x26 40.4 us: to(): return lax.ppermute(x, 'seq', [(i, i ^ j) for i in range(n)])]
    all_to_all x7 -> x0, starting transfers between devices: 34.8 us -> none  [the longest x1 7.98 us: local(): lax.all_to_all(key_grad.reshape(length, heads * HD), 'seq', split_axis=0,...]
    ppermute x0 -> x30, starting transfers between devices: none -> 28.5 us  [the longest x26 20.6 us: to(): return lax.ppermute(x, 'seq', [(i, i ^ j) for i in range(n)])]
    all_to_all x1 -> x0, blocking collectives: 23.3 us -> none  [local(): lax.all_to_all(attended.reshape(length, heads * HD), 'seq', split_axis=0,...]
    pallas_call x0 -> x14, Pallas kernels: none -> 18.8 us  [call(): pl.pallas_call(kernel, out_shape=tuple((shape for _, shape in outs)), in_...]
  transfers between devices with their start and end apart: 9 -> 30, of which waited for: 4 -> 15; matrix products, arithmetic and copies ran while one was open for 25% -> 0% of each run, Pallas kernels for 0% -> 15%
where the time goes in v3:
time: 95.2 us; the launch traced here: 95 us
  waiting for transfers between devices  46.7 us (49%)
  starting transfers between devices  28.5 us (30%)
  Pallas kernels  18.8 us (20%)
  between operations  0.98 us (1%)
    ppermute x26, waiting for transfers between devices, to(): return lax.ppermute(x, 'seq', [(i, i ^ j) for i in range(n)])  40.4 us
    ppermute x26, starting transfers between devices, to(): return lax.ppermute(x, 'seq', [(i, i ^ j) for i in range(n)])  20.6 us
    pallas_call x14, Pallas kernels, call(): pl.pallas_call(kernel, out_shape=tuple((shape for _, shape in outs)), in_...  18.8 us
    ppermute x4, starting transfers between devices, to_z(): return lax.ppermute(x, 'dp', [(i, i ^ j) for i in range(nz)])  7.97 us
    ppermute x4, waiting for transfers between devices, to_z(): return lax.ppermute(x, 'dp', [(i, i ^ j) for i in range(nz)])  6.22 us
  transfers between devices with their start and end apart: 30, of which 15 were waited for; matrix products, arithmetic and copies ran while one was open for 0% of the time, Pallas kernels for 15%

profile of v3, /device:TPU:2, one launch (start us, length us, event | category | flops | bytes accessed | tf_op | source)
XLA Modules:
  0.0 95.0 jit_solution(10627697589719463308)
XLA Ops:
  0.6 2.2 %shard_map.110 = (bf16[3,128,256]{2,1,0:T(8,128)(2,1)S(1)}, bf16[3,128,256]{2,1,0:T(8,128)(2,1)S(1)}, bf16[3,128,256]{2,1,0:T(8,128)(2,1)S(1)}, bf16[3,128,256]{...) custom-call(bf16[1,128,2048]{2,1,0:T(8,128)(2,1)} %q_ref.1, ...), custom_call_target="tpu_custom_call" | custom-call | bytes 8388608 | tf_op jit(solution)/shard_map/pallas_call | solution.py:43
  2.9 1.6 %collective-permute-start = (bf16[3,128,256]{2,1,0:T(8,128)(2,1)S(1)}, bf16[3,128,256]{2,1,0:T(8,128)(2,1)S(1)}, u32[]{:S(2)}, u32[]{:S(2)}) collective-permute-start(bf16[3,128,256]{2,1,0:T(8,128)(2,1)S(1)} %get-tuple-element.57), channel_id=1, source_target_pairs={{0,6},{1,7},{2,4},{3,5},{4,2},{5,3},{6,0},{7,1},{8,14},{9,15},{10,... | collective-permute-start | bytes 589832 | tf_op jit(solution)/shard_map/ppermute | solution.py:425
  4.5 1.5 %collective-permute-start.1 = (bf16[3,128,256]{2,1,0:T(8,128)(2,1)S(1)}, bf16[3,128,256]{2,1,0:T(8,128)(2,1)S(1)}, u32[]{:S(2)}, u32[]{:S(2)}) collective-permute-start(bf16[3,128,256]{2,1,0:T(8,128)(2,1)S(1)} %get-tuple-element.58), channel_id=1, source_target_pairs={{0,2},{1,3},{2,0},{3,1},{4,6},{5,7},{6,4},{7,5},{8,10},{9,11},{10,... | collective-permute-start | bytes 589832 | tf_op jit(solution)/shard_map/ppermute | solution.py:425
  6.0 2.6 %collective-permute-start.8 = (bf16[1,128,1024]{2,1,0:T(8,128)(2,1)S(1)}, bf16[1,128,1024]{2,1,0:T(8,128)(2,1)S(1)}, u32[]{:S(2)}, u32[]{:S(2)}) collective-permute-start(bf16[1,128,1024]{2,1,0:T(8,128)(2,1)S(1)} %bitcast.4), channel_id=1, source_target_pairs={{0,16},{8,24},{16,0},{24,8},{1,17},{9,25},{17,1},{25,9},{2,18},{10... | collective-permute-start | bytes 786440 | tf_op jit(solution)/shard_map/ppermute | solution.py:428
  8.5 0.5 collective-permute-start.2
  9.1 2.6 %collective-permute-done.rest_1_ = bf16[3,128,256]{2,1,0:T(8,128)(2,1)S(1)} collective-permute-done((bf16[3,128,256]{2,1,0:T(8,128)(2,1)S(1)}, bf16[3,128,256]{2,1,0:T(8,128)(2,1)S(1)}, u32[]{:S(2)}, u32[]{:S(2)}) %collective-permute-start) | collective-permute-done | bytes 196640 | tf_op jit(solution)/shard_map/ppermute | solution.py:425
  11.7 3.1 %collective-permute-done.1.rest_2_ = bf16[3,128,256]{2,1,0:T(8,128)(2,1)S(1)} collective-permute-done((bf16[3,128,256]{2,1,0:T(8,128)(2,1)S(1)}, bf16[3,128,256]{2,1,0:T(8,128)(2,1)S(1)}, u32[]{:S(2)}, u32[]{:S(2)}) %collective-permute-start.1) | collective-permute-done | bytes 196640 | tf_op jit(solution)/shard_map/ppermute | solution.py:425
  14.8 0.6 collective-permute-start.5
  15.4 5.1 %collective-permute-done.2.rest_3_ = bf16[3,128,256]{2,1,0:T(8,128)(2,1)S(1)} collective-permute-done((bf16[3,128,256]{2,1,0:T(8,128)(2,1)S(1)}, bf16[3,128,256]{2,1,0:T(8,128)(2,1)S(1)}, u32[]{:S(2)}, u32[]{:S(2)}) %collective-permute-start.2) | collective-permute-done | bytes 196640 | tf_op jit(solution)/shard_map/ppermute | solution.py:425
  20.5 0.6 collective-permute-start.13
  21.3 1.6 %collective-permute-start.9 = (bf16[2,128,1024]{2,1,0:T(8,128)(2,1)S(1)}, bf16[2,128,1024]{2,1,0:T(8,128)(2,1)S(1)}, u32[]{:S(2)}, u32[]{:S(2)}) collective-permute-start(bf16[2,128,1024]{2,1,0:T(8,128)(2,1)S(1)} %shard_map.112.mine_ref), channel_id=1, source_target_pairs={{0,8},{8,0},{16,24},{24,16},{1,9},{9,1},{17,25},{25,17},{2,10},{10... | collective-permute-start | bytes 1572872 | tf_op jit(solution)/shard_map/ppermute | solution.py:428
  22.9 0.8 collective-permute-start.12
  23.7 2.0 %collective-permute-start.11 = (bf16[256,1024]{1,0:T(8,128)(2,1)S(1)}, bf16[256,1024]{1,0:T(8,128)(2,1)S(1)}, u32[]{:S(2)}, u32[]{:S(2)}) collective-permute-start(bf16[256,1024]{1,0:T(8,128)(2,1)S(1)} %shard_map.114.rest_0_), channel_id=1, source_target_pairs={{0,2},{1,3},{2,0},{3,1},{4,6},{5,7},{6,4},{7,5},{8,10},{9,11},{10,... | collective-permute-start | bytes 1572872 | tf_op jit(solution)/shard_map/ppermute | solution.py:425
  25.7 7.8 %collective-permute-done.5.rest_6_ = bf16[3,128,256]{2,1,0:T(8,128)(2,1)S(1)} collective-permute-done((bf16[3,128,256]{2,1,0:T(8,128)(2,1)S(1)}, bf16[3,128,256]{2,1,0:T(8,128)(2,1)S(1)}, u32[]{:S(2)}, u32[]{:S(2)}) %collective-permute-start.5) | collective-permute-done | bytes 196640 | tf_op jit(solution)/shard_map/ppermute | solution.py:425
  33.5 2.2 %collective-permute-start.6 = (bf16[3,128,256]{2,1,0:T(8,128)(2,1)S(1)}, bf16[3,128,256]{2,1,0:T(8,128)(2,1)S(1)}, u32[]{:S(2)}, u32[]{:S(2)}) collective-permute-start(bf16[3,128,256]{2,1,0:T(8,128)(2,1)S(1)} %get-tuple-element.63), channel_id=1, source_target_pairs={{0,1},{1,0},{2,3},{3,2},{4,5},{5,4},{6,7},{7,6},{8,9},{9,8},{10,11... | collective-permute-start | bytes 589832 | tf_op jit(solution)/shard_map/ppermute | solution.py:425
  35.7 1.1 %collective-permute-done.6.rest_7_ = bf16[3,128,256]{2,1,0:T(8,128)(2,1)S(1)} collective-permute-done((bf16[3,128,256]{2,1,0:T(8,128)(2,1)S(1)}, bf16[3,128,256]{2,1,0:T(8,128)(2,1)S(1)}, u32[]{:S(2)}, u32[]{:S(2)}) %collective-permute-start.6) | collective-permute-done | bytes 196640 | tf_op jit(solution)/shard_map/ppermute | solution.py:425
  36.8 5.3 %shard_map.111 = (bf16[1024,256]{1,0:T(8,128)(2,1)S(1)}, bf16[1024,256]{1,0:T(8,128)(2,1)S(1)}, bf16[2,128,1024]{2,1,0:T(8,128)(2,1)S(1)}, bf16[2,1024,1024]{2,1...) custom-call(s32[1,8,8]{2,1,0:T(8,128)S(1)} %copy-done, ...), custom_call_target="tpu_custom_call" | custom-call | flops 1073741824 | bytes 8388608 | tf_op jit(solution)/shard_map/pallas_call | solution.py:43
  42.2 0.4 collective-permute-start.7
  42.6 0.1 shard_map.113
  42.7 3.9 %collective-permute-done.12.rest_2_ = bf16[256,1024]{1,0:T(8,128)(2,1)S(1)} collective-permute-done((bf16[256,1024]{1,0:T(8,128)(2,1)S(1)}, bf16[256,1024]{1,0:T(8,128)(2,1)S(1)}, u32[]{:S(2)}, u32[]{:S(2)}) %collective-permute-start.12) | collective-permute-done | bytes 524320 | tf_op jit(solution)/shard_map/ppermute | solution.py:425
  46.6 1.3 %shard_map.115 = (f32[256,1024]{1,0:T(8,128)S(1)}, bf16[256,1024]{1,0:T(8,128)(2,1)S(1)}, bf16[1024,1024]{1,0:T(8,128)(2,1)S(1)}) custom-call(bf16[256,1024]{1,0:T(8,128)(2,1)S(1)} %shard_map.114.rest_0_, bf16[256,1024]{1,0:T(8,128)(2,1)S(1)} %collective-permute-done.11.rest_1_, bf16[256,1024]{1,0:T(8,128)(2,1)S(1)} %collective-permute-done.12.rest_2_, ...), custom_call_target="tpu_custom_call" | custom-call | flops 1073741824 | bytes 8388608 | tf_op jit(solution)/shard_map/pallas_call | solution.py:43
  47.9 0.1 collective-permute-start.14
  48.0 1.3 %shard_map.116 = (f32[256,1024]{1,0:T(8,128)S(1)}, bf16[256,1024]{1,0:T(8,128)(2,1)S(1)}, bf16[256,1024]{1,0:T(8,128)(2,1)S(1)}, bf16[128,1024]{1,0:T(8,128)(2,1)S(1)}, bf16[128,1024]{1,0:T(8,128)(2,1)S(1)}) custom-call(bf16[1024,256]{1,0:T(8,128)(2,1)S(1)} %get-tuple-element.64.attn_ref, bf16[1024,256]{1,0:T(8,128)(2,1)S(1)} %collective-permute-done.7.recv_ref, ...), custom_call_target="tpu_custom_call" | custom-call | flops 1073741824 | bytes 6291456 | tf_op jit(solution)/shard_map/pallas_call | solution.py:43
  49.3 0.4 collective-permute-start.15
  49.7 1.2 %collective-permute-start.16 = (bf16[128,1024]{1,0:T(8,128)(2,1)S(1)}, bf16[128,1024]{1,0:T(8,128)(2,1)S(1)}, u32[]{:S(2)}, u32[]{:S(2)}) collective-permute-start(bf16[128,1024]{1,0:T(8,128)(2,1)S(1)} %get-tuple-element.89), channel_id=1, source_target_pairs={{0,4},{1,5},{2,6},{3,7},{4,0},{5,1},{6,2},{7,3},{8,12},{9,13},{10,... | collective-permute-start | bytes 786440 | tf_op jit(solution)/shard_map/ppermute | solution.py:425
  50.9 1.5 %shard_map.117 = (f32[2,128,1024]{2,1,0:T(8,128)S(1)}, bf16[2,128,1024]{2,1,0:T(8,128)(2,1)S(1)}) custom-call(bf16[2,128,1024]{2,1,0:T(8,128)(2,1)S(1)} %get-tuple-element.78.attn_t_ref, bf16[1024,256]{1,0:T(8,128)(2,1)S(1)} %collective-permute-done.7.recv_ref, bf16[1024,1024]{1,0:T(8,128)(2,1)S(1)} %get-tuple-element.79.cot_ref), custom_call_target="tpu_custom_call" | custom-call | flops 1073741824 | bytes 6291456 | tf_op jit(solution)/shard_map/pallas_call | solution.py:43
  52.4 1.6 %collective-permute-start.20 = (bf16[2,128,1024]{2,1,0:T(8,128)(2,1)S(1)}, bf16[2,128,1024]{2,1,0:T(8,128)(2,1)S(1)}, u32[]{:S(2)}, u32[]{:S(2)}) collective-permute-start(bf16[2,128,1024]{2,1,0:T(8,128)(2,1)S(1)} %get-tuple-element.94), channel_id=1, source_target_pairs={{0,8},{8,0},{16,24},{24,16},{1,9},{9,1},{17,25},{25,17},{2,10},{10... | collective-permute-start | bytes 1572872 | tf_op jit(solution)/shard_map/ppermute | solution.py:428
  54.1 4.5 %shard_map.118 = (bf16[3,128,256]{2,1,0:T(8,128)(2,1)S(1)}, bf16[3,128,256]{2,1,0:T(8,128)(2,1)S(1)}, bf16[3,128,256]{2,1,0:T(8,128)(2,1)S(1)}, bf16[3,128,256]{...) custom-call(bf16[2,1024,1024]{2,1,0:T(8,128)(2,1)S(1)} %get-tuple-el, ...), custom_call_target="tpu_custom_call" | custom-call | flops 2147483648 | bytes 8388608 | tf_op jit(solution)/shard_map/pallas_call | solution.py:43
  58.6 0.1 shard_map.119
  58.8 1.5 %collective-permute-start.17 = (bf16[256,1024]{1,0:T(8,128)(2,1)S(1)}, bf16[256,1024]{1,0:T(8,128)(2,1)S(1)}, u32[]{:S(2)}, u32[]{:S(2)}) collective-permute-start(bf16[256,1024]{1,0:T(8,128)(2,1)S(1)} %get-tuple-element.90), channel_id=1, source_target_pairs={{0,2},{1,3},{2,0},{3,1},{4,6},{5,7},{6,4},{7,5},{8,10},{9,11},{10,... | collective-permute-start | bytes 1572872 | tf_op jit(solution)/shard_map/ppermute | solution.py:425
  60.3 1.0 %collective-permute-start.18 = (bf16[256,1024]{1,0:T(8,128)(2,1)S(1)}, bf16[256,1024]{1,0:T(8,128)(2,1)S(1)}, u32[]{:S(2)}, u32[]{:S(2)}) collective-permute-start(bf16[256,1024]{1,0:T(8,128)(2,1)S(1)} %get-tuple-element.91), channel_id=1, source_target_pairs={{0,4},{1,5},{2,6},{3,7},{4,0},{5,1},{6,2},{7,3},{8,12},{9,13},{10,... | collective-permute-start | bytes 1572872 | tf_op jit(solution)/shard_map/ppermute | solution.py:425
  61.3 4.9 %collective-permute-done.20.recv_ref = bf16[2,128,1024]{2,1,0:T(8,128)(2,1)S(1)} collective-permute-done((bf16[2,128,1024]{2,1,0:T(8,128)(2,1)S(1)}, bf16[2,128,1024]{2,1,0:T(8,128)(2,1)S(1)}, u32[]{:S(2)}, u32[]{:S(2)}) %collective-permute-start.20) | collective-permute-done | bytes 524320 | tf_op jit(solution)/shard_map/ppermute | solution.py:428
  66.2 0.1 shard_map.121
  66.4 2.2 %collective-permute-start.22 = (bf16[1,128,1024]{2,1,0:T(8,128)(2,1)S(1)}, bf16[1,128,1024]{2,1,0:T(8,128)(2,1)S(1)}, u32[]{:S(2)}, u32[]{:S(2)}) collective-permute-start(bf16[1,128,1024]{2,1,0:T(8,128)(2,1)S(1)} %get-tuple-element.98), channel_id=1, source_target_pairs={{0,16},{8,24},{16,0},{24,8},{1,17},{9,25},{17,1},{25,9},{2,18},{10... | collective-permute-start | bytes 786440 | tf_op jit(solution)/shard_map/ppermute | solution.py:428
  68.6 1.5 %collective-permute-start.21 = (bf16[3,128,256]{2,1,0:T(8,128)(2,1)S(1)}, bf16[3,128,256]{2,1,0:T(8,128)(2,1)S(1)}, u32[]{:S(2)}, u32[]{:S(2)}) collective-permute-start(bf16[3,128,256]{2,1,0:T(8,128)(2,1)S(1)} %get-tuple-element.96), channel_id=1, source_target_pairs={{0,6},{1,7},{2,4},{3,5},{4,2},{5,3},{6,0},{7,1},{8,14},{9,15},{10,... | collective-permute-start | bytes 589832 | tf_op jit(solution)/shard_map/ppermute | solution.py:425
  70.0 1.4 %collective-permute-start.24 = (bf16[3,128,256]{2,1,0:T(8,128)(2,1)S(1)}, bf16[3,128,256]{2,1,0:T(8,128)(2,1)S(1)}, u32[]{:S(2)}, u32[]{:S(2)}) collective-permute-start(bf16[3,128,256]{2,1,0:T(8,128)(2,1)S(1)} %get-tuple-element.101), channel_id=1, source_target_pairs={{0,2},{1,3},{2,0},{3,1},{4,6},{5,7},{6,4},{7,5},{8,10},{9,11},{10,... | collective-permute-start | bytes 589832 | tf_op jit(solution)/shard_map/ppermute | solution.py:425
  71.4 2.3 %collective-permute-done.17.rest_0_ = bf16[256,1024]{1,0:T(8,128)(2,1)S(1)} collective-permute-done((bf16[256,1024]{1,0:T(8,128)(2,1)S(1)}, bf16[256,1024]{1,0:T(8,128)(2,1)S(1)}, u32[]{:S(2)}, u32[]{:S(2)}) %collective-permute-start.17) | collective-permute-done | bytes 524320 | tf_op jit(solution)/shard_map/ppermute | solution.py:425
  73.7 1.1 %collective-permute-start.25 = (bf16[3,128,256]{2,1,0:T(8,128)(2,1)S(1)}, bf16[3,128,256]{2,1,0:T(8,128)(2,1)S(1)}, u32[]{:S(2)}, u32[]{:S(2)}) collective-permute-start(bf16[3,128,256]{2,1,0:T(8,128)(2,1)S(1)} %get-tuple-element.102), channel_id=1, source_target_pairs={{0,4},{1,5},{2,6},{3,7},{4,0},{5,1},{6,2},{7,3},{8,12},{9,13},{10,... | collective-permute-start | bytes 589832 | tf_op jit(solution)/shard_map/ppermute | solution.py:425
  74.8 3.9 %collective-permute-done.18.rest_1_ = bf16[256,1024]{1,0:T(8,128)(2,1)S(1)} collective-permute-done((bf16[256,1024]{1,0:T(8,128)(2,1)S(1)}, bf16[256,1024]{1,0:T(8,128)(2,1)S(1)}, u32[]{:S(2)}, u32[]{:S(2)}) %collective-permute-start.18) | collective-permute-done | bytes 524320 | tf_op jit(solution)/shard_map/ppermute | solution.py:425
  78.7 0.2 shard_map.120
  79.0 1.3 %collective-permute-done.22.recv_ref = bf16[1,128,1024]{2,1,0:T(8,128)(2,1)S(1)} collective-permute-done((bf16[1,128,1024]{2,1,0:T(8,128)(2,1)S(1)}, bf16[1,128,1024]{2,1,0:T(8,128)(2,1)S(1)}, u32[]{:S(2)}, u32[]{:S(2)}) %collective-permute-start.22) | collective-permute-done | bytes 262176 | tf_op jit(solution)/shard_map/ppermute | solution.py:428
  80.4 0.8 collective-permute-done.24.rest_2_
  81.1 0.8 collective-permute-start.27
  82.0 4.1 %collective-permute-done.25.rest_3_ = bf16[3,128,256]{2,1,0:T(8,128)(2,1)S(1)} collective-permute-done((bf16[3,128,256]{2,1,0:T(8,128)(2,1)S(1)}, bf16[3,128,256]{2,1,0:T(8,128)(2,1)S(1)}, u32[]{:S(2)}, u32[]{:S(2)}) %collective-permute-start.25) | collective-permute-done | bytes 196640 | tf_op jit(solution)/shard_map/ppermute | solution.py:425
  86.2 1.1 %collective-permute-start.29 = (bf16[3,128,256]{2,1,0:T(8,128)(2,1)S(1)}, bf16[3,128,256]{2,1,0:T(8,128)(2,1)S(1)}, u32[]{:S(2)}, u32[]{:S(2)}) collective-permute-start(bf16[3,128,256]{2,1,0:T(8,128)(2,1)S(1)} %get-tuple-element.106), channel_id=1, source_target_pairs={{0,1},{1,0},{2,3},{3,2},{4,5},{5,4},{6,7},{7,6},{8,9},{9,8},{10,11... | collective-permute-start | bytes 589832 | tf_op jit(solution)/shard_map/ppermute | solution.py:425
  87.3 1.7 %collective-permute-done.27.rest_5_ = bf16[3,128,256]{2,1,0:T(8,128)(2,1)S(1)} collective-permute-done((bf16[3,128,256]{2,1,0:T(8,128)(2,1)S(1)}, bf16[3,128,256]{2,1,0:T(8,128)(2,1)S(1)}, u32[]{:S(2)}, u32[]{:S(2)}) %collective-permute-start.27) | collective-permute-done | bytes 196640 | tf_op jit(solution)/shard_map/ppermute | solution.py:425
  89.0 3.9 %collective-permute-done.28.rest_6_ = bf16[3,128,256]{2,1,0:T(8,128)(2,1)S(1)} collective-permute-done((bf16[3,128,256]{2,1,0:T(8,128)(2,1)S(1)}, bf16[3,128,256]{2,1,0:T(8,128)(2,1)S(1)}, u32[]{:S(2)}, u32[]{:S(2)}) %collective-permute-start.28) | collective-permute-done | bytes 196640 | tf_op jit(solution)/shard_map/ppermute | solution.py:425
  92.9 1.9 %shard_map.123 = (bf16[1,128,2048]{2,1,0:T(8,128)(2,1)}, bf16[1,128,2048]{2,1,0:T(8,128)(2,1)}, bf16[1,128,2048]{2,1,0:T(8,128)(2,1)}, bf16[1,128,2048]{2,1,0:T(8,128)(2,1)}, f32[64,2048]{1,0:T(8,128)}) custom-call(bf16[128,1024]{1,0:T(8,128)(2,1)S(1)} %get-tuple-element.92.keep_ref, bf16[128,1024]{1,0:T(8,128)(2,1)S(1)} %collective-permute-done.19.recv_ref, ...), custom_call_target="tpu_custom_call" | custom-call | bytes 4194304 | tf_op jit(solution)/shard_map/pallas_call | solution.py:43
  (30 shorter events, 0.4 us)
Async XLA Ops:
  2.9 33.9 %copy-start = (s32[1,8,8]{2,1,0:T(8,128)S(1)}, s32[1,8,8]{2,1,0:T(8,128)}, u32[]{:S(2)}) copy-start(s32[1,8,8]{2,1,0:T(8,128)} %adj_ref.1) | copy-start | bytes 772
  2.9 33.9 %copy-start.1 = (s32[1,8]{1,0:T(1,128)S(1)}, s32[1,8]{1,0:T(1,128)}, u32[]{:S(2)}) copy-start(s32[1,8]{1,0:T(1,128)} %cnt_ref.1) | copy-start | bytes 100
  2.9 8.8 %collective-permute-start = (bf16[3,128,256]{2,1,0:T(8,128)(2,1)S(1)}, bf16[3,128,256]{2,1,0:T(8,128)(2,1)S(1)}, u32[]{:S(2)}, u32[]{:S(2)}) collective-permute-start(bf16[3,128,256]{2,1,0:T(8,128)(2,1)S(1)} %get-tuple-element.57), channel_id=1, source_target_pairs={{0,6},{1,7},{2,4},{3,5},{4,2},{5,3},{6,0},{7,1},{8,14},{9,15},{10,... | collective-permute-start | bytes 589832 | tf_op jit(solution)/shard_map/ppermute | solution.py:425
  4.5 10.3 %collective-permute-start.1 = (bf16[3,128,256]{2,1,0:T(8,128)(2,1)S(1)}, bf16[3,128,256]{2,1,0:T(8,128)(2,1)S(1)}, u32[]{:S(2)}, u32[]{:S(2)}) collective-permute-start(bf16[3,128,256]{2,1,0:T(8,128)(2,1)S(1)} %get-tuple-element.58), channel_id=1, source_target_pairs={{0,2},{1,3},{2,0},{3,1},{4,6},{5,7},{6,4},{7,5},{8,10},{9,11},{10,... | collective-permute-start | bytes 589832 | tf_op jit(solution)/shard_map/ppermute | solution.py:425
  6.0 8.8 %collective-permute-start.10 = (bf16[128,1024]{1,0:T(8,128)(2,1)S(1)}, bf16[128,1024]{1,0:T(8,128)(2,1)S(1)}, u32[]{:S(2)}, u32[]{:S(2)}) collective-permute-start(bf16[128,1024]{1,0:T(8,128)(2,1)S(1)} %get-tuple-element.68), channel_id=1, source_target_pairs={{0,1},{1,0},{2,3},{3,2},{4,5},{5,4},{6,7},{7,6},{8,9},{9,8},{10,11... | collective-permute-start | bytes 786440 | tf_op jit(solution)/shard_map/ppermute | solution.py:425
  6.0 15.2 %collective-permute-start.8 = (bf16[1,128,1024]{2,1,0:T(8,128)(2,1)S(1)}, bf16[1,128,1024]{2,1,0:T(8,128)(2,1)S(1)}, u32[]{:S(2)}, u32[]{:S(2)}) collective-permute-start(bf16[1,128,1024]{2,1,0:T(8,128)(2,1)S(1)} %bitcast.4), channel_id=1, source_target_pairs={{0,16},{8,24},{16,0},{24,8},{1,17},{9,25},{17,1},{25,9},{2,18},{10... | collective-permute-start | bytes 786440 | tf_op jit(solution)/shard_map/ppermute | solution.py:428
  8.5 11.9 %collective-permute-start.2 = (bf16[3,128,256]{2,1,0:T(8,128)(2,1)S(1)}, bf16[3,128,256]{2,1,0:T(8,128)(2,1)S(1)}, u32[]{:S(2)}, u32[]{:S(2)}) collective-permute-start(bf16[3,128,256]{2,1,0:T(8,128)(2,1)S(1)} %get-tuple-element.59), channel_id=1, source_target_pairs={{0,4},{1,5},{2,6},{3,7},{4,0},{5,1},{6,2},{7,3},{8,12},{9,13},{10,... | collective-permute-start | bytes 589832 | tf_op jit(solution)/shard_map/ppermute | solution.py:425
  11.7 11.2 %collective-permute-start.3 = (bf16[3,128,256]{2,1,0:T(8,128)(2,1)S(1)}, bf16[3,128,256]{2,1,0:T(8,128)(2,1)S(1)}, u32[]{:S(2)}, u32[]{:S(2)}) collective-permute-start(bf16[3,128,256]{2,1,0:T(8,128)(2,1)S(1)} %get-tuple-element.60), channel_id=1, source_target_pairs={{0,7},{1,6},{2,5},{3,4},{4,3},{5,2},{6,1},{7,0},{8,15},{9,14},{10,... | collective-permute-start | bytes 589832 | tf_op jit(solution)/shard_map/ppermute | solution.py:425
  14.8 8.9 %collective-permute-start.4 = (bf16[3,128,256]{2,1,0:T(8,128)(2,1)S(1)}, bf16[3,128,256]{2,1,0:T(8,128)(2,1)S(1)}, u32[]{:S(2)}, u32[]{:S(2)}) collective-permute-start(bf16[3,128,256]{2,1,0:T(8,128)(2,1)S(1)} %get-tuple-element.61), channel_id=1, source_target_pairs={{0,3},{1,2},{2,1},{3,0},{4,7},{5,6},{6,5},{7,4},{8,11},{9,10},{10,... | collective-permute-start | bytes 589832 | tf_op jit(solution)/shard_map/ppermute | solution.py:425
  14.8 18.7 %collective-permute-start.5 = (bf16[3,128,256]{2,1,0:T(8,128)(2,1)S(1)}, bf16[3,128,256]{2,1,0:T(8,128)(2,1)S(1)}, u32[]{:S(2)}, u32[]{:S(2)}) collective-permute-start(bf16[3,128,256]{2,1,0:T(8,128)(2,1)S(1)} %get-tuple-element.62), channel_id=1, source_target_pairs={{0,5},{1,4},{2,7},{3,6},{4,1},{5,0},{6,3},{7,2},{8,13},{9,12},{10,... | collective-permute-start | bytes 589832 | tf_op jit(solution)/shard_map/ppermute | solution.py:425
  20.5 22.2 %collective-permute-start.13 = (bf16[256,1024]{1,0:T(8,128)(2,1)S(1)}, bf16[256,1024]{1,0:T(8,128)(2,1)S(1)}, u32[]{:S(2)}, u32[]{:S(2)}) collective-permute-start(bf16[256,1024]{1,0:T(8,128)(2,1)S(1)} %shard_map.114.rest_0_), channel_id=1, source_target_pairs={{0,6},{1,7},{2,4},{3,5},{4,2},{5,3},{6,0},{7,1},{8,14},{9,15},{10,... | collective-permute-start | bytes 1572872 | tf_op jit(solution)/shard_map/ppermute | solution.py:425
  21.3 21.3 %collective-permute-start.9 = (bf16[2,128,1024]{2,1,0:T(8,128)(2,1)S(1)}, bf16[2,128,1024]{2,1,0:T(8,128)(2,1)S(1)}, u32[]{:S(2)}, u32[]{:S(2)}) collective-permute-start(bf16[2,128,1024]{2,1,0:T(8,128)(2,1)S(1)} %shard_map.112.mine_ref), channel_id=1, source_target_pairs={{0,8},{8,0},{16,24},{24,16},{1,9},{9,1},{17,25},{25,17},{2,10},{10... | collective-permute-start | bytes 1572872 | tf_op jit(solution)/shard_map/ppermute | solution.py:428
  22.9 23.8 %collective-permute-start.12 = (bf16[256,1024]{1,0:T(8,128)(2,1)S(1)}, bf16[256,1024]{1,0:T(8,128)(2,1)S(1)}, u32[]{:S(2)}, u32[]{:S(2)}) collective-permute-start(bf16[256,1024]{1,0:T(8,128)(2,1)S(1)} %shard_map.114.rest_0_), channel_id=1, source_target_pairs={{0,4},{1,5},{2,6},{3,7},{4,0},{5,1},{6,2},{7,3},{8,12},{9,13},{10,... | collective-permute-start | bytes 1572872 | tf_op jit(solution)/shard_map/ppermute | solution.py:425
  23.7 23.0 %collective-permute-start.11 = (bf16[256,1024]{1,0:T(8,128)(2,1)S(1)}, bf16[256,1024]{1,0:T(8,128)(2,1)S(1)}, u32[]{:S(2)}, u32[]{:S(2)}) collective-permute-start(bf16[256,1024]{1,0:T(8,128)(2,1)S(1)} %shard_map.114.rest_0_), channel_id=1, source_target_pairs={{0,2},{1,3},{2,0},{3,1},{4,6},{5,7},{6,4},{7,5},{8,10},{9,11},{10,... | collective-permute-start | bytes 1572872 | tf_op jit(solution)/shard_map/ppermute | solution.py:425
  33.5 3.3 %collective-permute-start.6 = (bf16[3,128,256]{2,1,0:T(8,128)(2,1)S(1)}, bf16[3,128,256]{2,1,0:T(8,128)(2,1)S(1)}, u32[]{:S(2)}, u32[]{:S(2)}) collective-permute-start(bf16[3,128,256]{2,1,0:T(8,128)(2,1)S(1)} %get-tuple-element.63), channel_id=1, source_target_pairs={{0,1},{1,0},{2,3},{3,2},{4,5},{5,4},{6,7},{7,6},{8,9},{9,8},{10,11... | collective-permute-start | bytes 589832 | tf_op jit(solution)/shard_map/ppermute | solution.py:425
  42.2 5.8 %collective-permute-start.7 = (bf16[1024,256]{1,0:T(8,128)(2,1)S(1)}, bf16[1024,256]{1,0:T(8,128)(2,1)S(1)}, u32[]{:S(2)}, u32[]{:S(2)}) collective-permute-start(bf16[1024,256]{1,0:T(8,128)(2,1)S(1)} %get-tuple-element.65), channel_id=1, source_target_pairs={{0,1},{1,0},{2,3},{3,2},{4,5},{5,4},{6,7},{7,6},{8,9},{9,8},{10,11... | collective-permute-start | bytes 1572872 | tf_op jit(solution)/shard_map/ppermute | solution.py:425
  47.9 6.2 %collective-permute-start.14 = (bf16[256,1024]{1,0:T(8,128)(2,1)S(1)}, bf16[256,1024]{1,0:T(8,128)(2,1)S(1)}, u32[]{:S(2)}, u32[]{:S(2)}) collective-permute-start(bf16[256,1024]{1,0:T(8,128)(2,1)S(1)} %get-tuple-element.82), channel_id=1, source_target_pairs={{0,1},{1,0},{2,3},{3,2},{4,5},{5,4},{6,7},{7,6},{8,9},{9,8},{10,11... | collective-permute-start | bytes 1572872 | tf_op jit(solution)/shard_map/ppermute | solution.py:425
  49.3 9.3 %collective-permute-start.15 = (bf16[128,1024]{1,0:T(8,128)(2,1)S(1)}, bf16[128,1024]{1,0:T(8,128)(2,1)S(1)}, u32[]{:S(2)}, u32[]{:S(2)}) collective-permute-start(bf16[128,1024]{1,0:T(8,128)(2,1)S(1)} %get-tuple-element.87), channel_id=1, source_target_pairs={{0,2},{1,3},{2,0},{3,1},{4,6},{5,7},{6,4},{7,5},{8,10},{9,11},{10,... | collective-permute-start | bytes 786440 | tf_op jit(solution)/shard_map/ppermute | solution.py:425
  49.7 8.9 %collective-permute-start.16 = (bf16[128,1024]{1,0:T(8,128)(2,1)S(1)}, bf16[128,1024]{1,0:T(8,128)(2,1)S(1)}, u32[]{:S(2)}, u32[]{:S(2)}) collective-permute-start(bf16[128,1024]{1,0:T(8,128)(2,1)S(1)} %get-tuple-element.89), channel_id=1, source_target_pairs={{0,4},{1,5},{2,6},{3,7},{4,0},{5,1},{6,2},{7,3},{8,12},{9,13},{10,... | collective-permute-start | bytes 786440 | tf_op jit(solution)/shard_map/ppermute | solution.py:425
  52.4 13.8 %collective-permute-start.20 = (bf16[2,128,1024]{2,1,0:T(8,128)(2,1)S(1)}, bf16[2,128,1024]{2,1,0:T(8,128)(2,1)S(1)}, u32[]{:S(2)}, u32[]{:S(2)}) collective-permute-start(bf16[2,128,1024]{2,1,0:T(8,128)(2,1)S(1)} %get-tuple-element.94), channel_id=1, source_target_pairs={{0,8},{8,0},{16,24},{24,16},{1,9},{9,1},{17,25},{25,17},{2,10},{10... | collective-permute-start | bytes 1572872 | tf_op jit(solution)/shard_map/ppermute | solution.py:428
  58.8 14.9 %collective-permute-start.17 = (bf16[256,1024]{1,0:T(8,128)(2,1)S(1)}, bf16[256,1024]{1,0:T(8,128)(2,1)S(1)}, u32[]{:S(2)}, u32[]{:S(2)}) collective-permute-start(bf16[256,1024]{1,0:T(8,128)(2,1)S(1)} %get-tuple-element.90), channel_id=1, source_target_pairs={{0,2},{1,3},{2,0},{3,1},{4,6},{5,7},{6,4},{7,5},{8,10},{9,11},{10,... | collective-permute-start | bytes 1572872 | tf_op jit(solution)/shard_map/ppermute | solution.py:425
  60.3 18.4 %collective-permute-start.18 = (bf16[256,1024]{1,0:T(8,128)(2,1)S(1)}, bf16[256,1024]{1,0:T(8,128)(2,1)S(1)}, u32[]{:S(2)}, u32[]{:S(2)}) collective-permute-start(bf16[256,1024]{1,0:T(8,128)(2,1)S(1)} %get-tuple-element.91), channel_id=1, source_target_pairs={{0,4},{1,5},{2,6},{3,7},{4,0},{5,1},{6,2},{7,3},{8,12},{9,13},{10,... | collective-permute-start | bytes 1572872 | tf_op jit(solution)/shard_map/ppermute | solution.py:425
  66.4 13.8 %collective-permute-start.22 = (bf16[1,128,1024]{2,1,0:T(8,128)(2,1)S(1)}, bf16[1,128,1024]{2,1,0:T(8,128)(2,1)S(1)}, u32[]{:S(2)}, u32[]{:S(2)}) collective-permute-start(bf16[1,128,1024]{2,1,0:T(8,128)(2,1)S(1)} %get-tuple-element.98), channel_id=1, source_target_pairs={{0,16},{8,24},{16,0},{24,8},{1,17},{9,25},{17,1},{25,9},{2,18},{10... | collective-permute-start | bytes 786440 | tf_op jit(solution)/shard_map/ppermute | solution.py:428
  68.6 10.3 %collective-permute-start.21 = (bf16[3,128,256]{2,1,0:T(8,128)(2,1)S(1)}, bf16[3,128,256]{2,1,0:T(8,128)(2,1)S(1)}, u32[]{:S(2)}, u32[]{:S(2)}) collective-permute-start(bf16[3,128,256]{2,1,0:T(8,128)(2,1)S(1)} %get-tuple-element.96), channel_id=1, source_target_pairs={{0,6},{1,7},{2,4},{3,5},{4,2},{5,3},{6,0},{7,1},{8,14},{9,15},{10,... | collective-permute-start | bytes 589832 | tf_op jit(solution)/shard_map/ppermute | solution.py:425
  70.0 11.1 %collective-permute-start.24 = (bf16[3,128,256]{2,1,0:T(8,128)(2,1)S(1)}, bf16[3,128,256]{2,1,0:T(8,128)(2,1)S(1)}, u32[]{:S(2)}, u32[]{:S(2)}) collective-permute-start(bf16[3,128,256]{2,1,0:T(8,128)(2,1)S(1)} %get-tuple-element.101), channel_id=1, source_target_pairs={{0,2},{1,3},{2,0},{3,1},{4,6},{5,7},{6,4},{7,5},{8,10},{9,11},{10,... | collective-permute-start | bytes 589832 | tf_op jit(solution)/shard_map/ppermute | solution.py:425
  73.7 12.5 %collective-permute-start.25 = (bf16[3,128,256]{2,1,0:T(8,128)(2,1)S(1)}, bf16[3,128,256]{2,1,0:T(8,128)(2,1)S(1)}, u32[]{:S(2)}, u32[]{:S(2)}) collective-permute-start(bf16[3,128,256]{2,1,0:T(8,128)(2,1)S(1)} %get-tuple-element.102), channel_id=1, source_target_pairs={{0,4},{1,5},{2,6},{3,7},{4,0},{5,1},{6,2},{7,3},{8,12},{9,13},{10,... | collective-permute-start | bytes 589832 | tf_op jit(solution)/shard_map/ppermute | solution.py:425
  78.7 7.5 %collective-permute-start.26 = (bf16[3,128,256]{2,1,0:T(8,128)(2,1)S(1)}, bf16[3,128,256]{2,1,0:T(8,128)(2,1)S(1)}, u32[]{:S(2)}, u32[]{:S(2)}) collective-permute-start(bf16[3,128,256]{2,1,0:T(8,128)(2,1)S(1)} %get-tuple-element.103), channel_id=1, source_target_pairs={{0,7},{1,6},{2,5},{3,4},{4,3},{5,2},{6,1},{7,0},{8,15},{9,14},{10,... | collective-permute-start | bytes 589832 | tf_op jit(solution)/shard_map/ppermute | solution.py:425
  78.9 14.0 %collective-permute-start.19 = (bf16[128,1024]{1,0:T(8,128)(2,1)S(1)}, bf16[128,1024]{1,0:T(8,128)(2,1)S(1)}, u32[]{:S(2)}, u32[]{:S(2)}) collective-permute-start(bf16[128,1024]{1,0:T(8,128)(2,1)S(1)} %get-tuple-element.93), channel_id=1, source_target_pairs={{0,1},{1,0},{2,3},{3,2},{4,5},{5,4},{6,7},{7,6},{8,9},{9,8},{10,11... | collective-permute-start | bytes 786440 | tf_op jit(solution)/shard_map/ppermute | solution.py:425
  80.3 12.6 %collective-permute-start.23 = (f32[64,1024]{1,0:T(8,128)S(1)}, f32[64,1024]{1,0:T(8,128)S(1)}, u32[]{:S(2)}, u32[]{:S(2)}) collective-permute-start(f32[64,1024]{1,0:T(8,128)S(1)} %get-tuple-element.100), channel_id=1, source_target_pairs={{0,1},{1,0},{2,3},{3,2},{4,5},{5,4},{6,7},{7,6},{8,9},{9,8},{10,11... | collective-permute-start | bytes 786440 | tf_op jit(solution)/shard_map/ppermute | solution.py:425
  81.1 7.9 %collective-permute-start.27 = (bf16[3,128,256]{2,1,0:T(8,128)(2,1)S(1)}, bf16[3,128,256]{2,1,0:T(8,128)(2,1)S(1)}, u32[]{:S(2)}, u32[]{:S(2)}) collective-permute-start(bf16[3,128,256]{2,1,0:T(8,128)(2,1)S(1)} %get-tuple-element.104), channel_id=1, source_target_pairs={{0,3},{1,2},{2,1},{3,0},{4,7},{5,6},{6,5},{7,4},{8,11},{9,10},{10,... | collective-permute-start | bytes 589832 | tf_op jit(solution)/shard_map/ppermute | solution.py:425
  86.1 6.8 %collective-permute-start.28 = (bf16[3,128,256]{2,1,0:T(8,128)(2,1)S(1)}, bf16[3,128,256]{2,1,0:T(8,128)(2,1)S(1)}, u32[]{:S(2)}, u32[]{:S(2)}) collective-permute-start(bf16[3,128,256]{2,1,0:T(8,128)(2,1)S(1)} %get-tuple-element.105), channel_id=1, source_target_pairs={{0,5},{1,4},{2,7},{3,6},{4,1},{5,0},{6,3},{7,2},{8,13},{9,12},{10,... | collective-permute-start | bytes 589832 | tf_op jit(solution)/shard_map/ppermute | solution.py:425
  86.2 6.8 %collective-permute-start.29 = (bf16[3,128,256]{2,1,0:T(8,128)(2,1)S(1)}, bf16[3,128,256]{2,1,0:T(8,128)(2,1)S(1)}, u32[]{:S(2)}, u32[]{:S(2)}) collective-permute-start(bf16[3,128,256]{2,1,0:T(8,128)(2,1)S(1)} %get-tuple-element.106), channel_id=1, source_target_pairs={{0,1},{1,0},{2,3},{3,2},{4,5},{5,4},{6,7},{7,6},{8,9},{9,8},{10,11... | collective-permute-start | bytes 589832 | tf_op jit(solution)/shard_map/ppermute | solution.py:425

commit v4 on v3

--- a/solution.py
+++ b/solution.py
@@ -55,14 +55,6 @@
     return pl.multiple_of(((dev % 2 * per + g) * pairs + dev // 2) * HD, HD)
 
 
-def copies(moves, sems):
-    handles = [pltpu.make_async_copy(src, dst, sems.at[n]) for n, (src, dst) in enumerate(moves)]
-    for handle in handles:
-        handle.start()
-    for handle in handles:
-        handle.wait()
-
-
 def attend(query_blk, key_blk, value_blk, links, live_count):
     scale = HD ** (-0.5)
     blocks = query_blk.shape[0]
@@ -187,23 +179,28 @@
 
 
 def prep_kernel(n, per, q_ref, k_ref, v_ref, c_ref, w_ref, *rest):
-    qkv, (same, other, wsend, sems) = by_slot(rest[:-4], n), rest[-4:]
+    qkv, (same, other, w_own, whole, sems) = by_slot(rest[:-5], n), rest[-5:]
     s = lax.axis_index("seq")
     core = s % 2
     half = c_ref.shape[2] // 2
-    moves = []
-    for j in range(n):
-        for t, src in enumerate((q_ref, k_ref, v_ref)):
+    mine = pl.multiple_of(core * half, half)
+    theirs = pl.multiple_of((1 - core) * half, half)
+    row = pl.multiple_of((s // 2) * HD, HD)
+    moves = [(src.at[0], whole.at[t]) for t, src in enumerate((q_ref, k_ref, v_ref))]
+    moves.append((c_ref.at[0, :, pl.ds(mine, half)], same))
+    moves.append((c_ref.at[0, :, pl.ds(theirs, half)], other))
+    moves.append((w_ref.at[pl.ds(row, HD), pl.ds(mine, half)], w_own))
+    handles = [pltpu.make_async_copy(src, dst, sems.at[m]) for m, (src, dst) in enumerate(moves)]
+    for handle in handles:
+        handle.start()
+    for t in range(3):
+        handles[t].wait()
+        for j in range(n):
             for g in range(per):
                 col = col_of(s ^ j, g, n // 2, per)
-                moves.append((src.at[0, :, pl.ds(col, HD)], qkv[j].at[t, :, pl.ds(g * HD, HD)]))
-    mine = pl.multiple_of(core * half, half)
-    theirs = pl.multiple_of((1 - core) * half, half)
-    moves.append((c_ref.at[0, :, pl.ds(mine, half)], same))
-    moves.append((c_ref.at[0, :, pl.ds(theirs, half)], other))
-    row = pl.multiple_of((s // 2) * HD, HD)
-    moves.append((w_ref.at[pl.ds(row, HD), pl.ds(mine, half)], wsend))
-    copies(moves, sems)
+                qkv[j][t, :, g * HD : (g + 1) * HD] = whole[t, :, pl.ds(col, HD)]
+    for handle in handles[3:]:
+        handle.wait()
 
 
 def order(n):
@@ -389,7 +386,7 @@
 
 
 def place_kernel(n, per, keep_ref, recv_ref, w_keep_ref, w_recv_ref, *rest):
-    parts, (out_ref, *outs, w_ref, sems) = by_slot(rest[:-6], n), rest[-6:]
+    parts, (out_ref, *outs, w_ref, whole, sems) = by_slot(rest[:-7], n), rest[-7:]
     s = lax.axis_index("seq")
     core = s % 2
     half = keep_ref.shape[1]
@@ -401,13 +398,18 @@
         (w_keep_ref, w_ref.at[:, mine]),
         (w_recv_ref, w_ref.at[:, theirs]),
     ]
-    for g in range(per):
+    moves += [(whole.at[t], outs[t].at[0]) for t in range(3)]
+    handles = [pltpu.make_async_copy(src, dst, sems.at[m]) for m, (src, dst) in enumerate(moves)]
+    for handle in handles[:4]:
+        handle.start()
+    for t in range(3):
         for j in range(n):
-            col = col_of(s ^ j, g, n // 2, per)
-            for t in range(3):
-                src = parts[j].at[t, :, pl.ds(g * HD, HD)]
-                moves.append((src, outs[t].at[0, :, pl.ds(col, HD)]))
-    copies(moves, sems)
+            for g in range(per):
+                col = col_of(s ^ j, g, n // 2, per)
+                whole[t, :, pl.ds(col, HD)] = parts[j][t, :, g * HD : (g + 1) * HD]
+        handles[4 + t].start()
+    for handle in handles:
+        handle.wait()
 
 
 def paired(n, nz, queries, key_rows, values, adjacency, counts, out_weight, out_cotangent):
@@ -434,7 +436,7 @@
         functools.partial(prep_kernel, n, per),
         [(HBM, in_hbm(x)) for x in (queries, key_rows, values, out_cotangent, out_weight)],
         [(VMEM, pltpu.VMEM(x.shape, x.dtype)) for x in [chunk] * n + [piece] * 3],
-        [pltpu.SemaphoreType.DMA((3 * n * per + 3,))],
+        [pltpu.VMEM((3, BLK, wide), BF16), pltpu.SemaphoreType.DMA((6,))],
         moved=8 * MIB,
     )
     same, other, w_own = prep[n:]
@@ -551,9 +553,9 @@
     token = sds((1, BLK, wide), BF16)
     return call(
         functools.partial(place_kernel, n, per),
-        [(ANY, x) for x in [out_keep, to(out_send, 1), half_keep, to(half_send, 1)] + back],
+        [(VMEM, x) for x in [out_keep, to(out_send, 1), half_keep, to(half_send, 1)] + back],
         [(ANY, token)] * 4 + [(ANY, sds((HD // 2, wide), F32))],
-        [pltpu.SemaphoreType.DMA((3 * n * per + 4,))],
+        [pltpu.VMEM((3, BLK, wide), BF16), pltpu.SemaphoreType.DMA((7,))],
         moved=4 * MIB,
     )
 

time: 95.2 us -> 94.3 us (level)
  transfers between devices with their start and end apart: 30 -> 30, of which waited for: 15 -> 15; matrix products, arithmetic and copies ran while one was open for 0% -> 0% of each run, Pallas kernels for 15% -> 16%
where the time goes in v4:
time: 94.3 us; the launch traced here: 94.2 us
  waiting for transfers between devices  46.7 us (50%)
  starting transfers between devices  28.5 us (30%)
  Pallas kernels  18 us (19%)
  between operations  0.98 us (1%)
    ppermute x26, waiting for transfers between devices, to(): return lax.ppermute(x, 'seq', [(i, i ^ j) for i in range(n)])  40.5 us
    ppermute x26, starting transfers between devices, to(): return lax.ppermute(x, 'seq', [(i, i ^ j) for i in range(n)])  20.6 us
    pallas_call x14, Pallas kernels, call(): pl.pallas_call(kernel, out_shape=tuple((shape for _, shape in outs)), in_...  18 us
    ppermute x4, starting transfers between devices, to_z(): return lax.ppermute(x, 'dp', [(i, i ^ j) for i in range(nz)])  7.96 us
    ppermute x4, waiting for transfers between devices, to_z(): return lax.ppermute(x, 'dp', [(i, i ^ j) for i in range(nz)])  6.18 us
  transfers between devices with their start and end apart: 30, of which 15 were waited for; matrix products, arithmetic and copies ran while one was open for 0% of the time, Pallas kernels for 16%

profile of v4, /device:TPU:2, one launch (start us, length us, event | category | flops | bytes accessed | tf_op | source)
XLA Modules:
  0.0 94.2 jit_solution(12563180698424096273)
XLA Ops:
  0.6 1.6 %shard_map.110 = (bf16[3,128,256]{2,1,0:T(8,128)(2,1)S(1)}, bf16[3,128,256]{2,1,0:T(8,128)(2,1)S(1)}, bf16[3,128,256]{2,1,0:T(8,128)(2,1)S(1)}, bf16[3,128,256]{...) custom-call(bf16[1,128,2048]{2,1,0:T(8,128)(2,1)} %q_ref.1, ...), custom_call_target="tpu_custom_call" | custom-call | bytes 8388608 | tf_op jit(solution)/shard_map/pallas_call | solution.py:43
  2.3 1.6 %collective-permute-start = (bf16[3,128,256]{2,1,0:T(8,128)(2,1)S(1)}, bf16[3,128,256]{2,1,0:T(8,128)(2,1)S(1)}, u32[]{:S(2)}, u32[]{:S(2)}) collective-permute-start(bf16[3,128,256]{2,1,0:T(8,128)(2,1)S(1)} %get-tuple-element.57), channel_id=1, source_target_pairs={{0,6},{1,7},{2,4},{3,5},{4,2},{5,3},{6,0},{7,1},{8,14},{9,15},{10,... | collective-permute-start | bytes 589832 | tf_op jit(solution)/shard_map/ppermute | solution.py:427
  3.9 1.5 %collective-permute-start.1 = (bf16[3,128,256]{2,1,0:T(8,128)(2,1)S(1)}, bf16[3,128,256]{2,1,0:T(8,128)(2,1)S(1)}, u32[]{:S(2)}, u32[]{:S(2)}) collective-permute-start(bf16[3,128,256]{2,1,0:T(8,128)(2,1)S(1)} %get-tuple-element.58), channel_id=1, source_target_pairs={{0,2},{1,3},{2,0},{3,1},{4,6},{5,7},{6,4},{7,5},{8,10},{9,11},{10,... | collective-permute-start | bytes 589832 | tf_op jit(solution)/shard_map/ppermute | solution.py:427
  5.4 2.6 %collective-permute-start.8 = (bf16[1,128,1024]{2,1,0:T(8,128)(2,1)S(1)}, bf16[1,128,1024]{2,1,0:T(8,128)(2,1)S(1)}, u32[]{:S(2)}, u32[]{:S(2)}) collective-permute-start(bf16[1,128,1024]{2,1,0:T(8,128)(2,1)S(1)} %bitcast.4), channel_id=1, source_target_pairs={{0,16},{8,24},{16,0},{24,8},{1,17},{9,25},{17,1},{25,9},{2,18},{10... | collective-permute-start | bytes 786440 | tf_op jit(solution)/shard_map/ppermute | solution.py:430
  7.9 0.5 collective-permute-start.2
  8.5 2.6 %collective-permute-done.rest_1_ = bf16[3,128,256]{2,1,0:T(8,128)(2,1)S(1)} collective-permute-done((bf16[3,128,256]{2,1,0:T(8,128)(2,1)S(1)}, bf16[3,128,256]{2,1,0:T(8,128)(2,1)S(1)}, u32[]{:S(2)}, u32[]{:S(2)}) %collective-permute-start) | collective-permute-done | bytes 196640 | tf_op jit(solution)/shard_map/ppermute | solution.py:427
  11.1 3.1 %collective-permute-done.1.rest_2_ = bf16[3,128,256]{2,1,0:T(8,128)(2,1)S(1)} collective-permute-done((bf16[3,128,256]{2,1,0:T(8,128)(2,1)S(1)}, bf16[3,128,256]{2,1,0:T(8,128)(2,1)S(1)}, u32[]{:S(2)}, u32[]{:S(2)}) %collective-permute-start.1) | collective-permute-done | bytes 196640 | tf_op jit(solution)/shard_map/ppermute | solution.py:427
  14.2 0.6 collective-permute-start.5
  14.8 5.1 %collective-permute-done.2.rest_3_ = bf16[3,128,256]{2,1,0:T(8,128)(2,1)S(1)} collective-permute-done((bf16[3,128,256]{2,1,0:T(8,128)(2,1)S(1)}, bf16[3,128,256]{2,1,0:T(8,128)(2,1)S(1)}, u32[]{:S(2)}, u32[]{:S(2)}) %collective-permute-start.2) | collective-permute-done | bytes 196640 | tf_op jit(solution)/shard_map/ppermute | solution.py:427
  19.9 0.6 collective-permute-start.13
  20.7 1.6 %collective-permute-start.9 = (bf16[2,128,1024]{2,1,0:T(8,128)(2,1)S(1)}, bf16[2,128,1024]{2,1,0:T(8,128)(2,1)S(1)}, u32[]{:S(2)}, u32[]{:S(2)}) collective-permute-start(bf16[2,128,1024]{2,1,0:T(8,128)(2,1)S(1)} %shard_map.112.mine_ref), channel_id=1, source_target_pairs={{0,8},{8,0},{16,24},{24,16},{1,9},{9,1},{17,25},{25,17},{2,10},{10... | collective-permute-start | bytes 1572872 | tf_op jit(solution)/shard_map/ppermute | solution.py:430
  22.3 0.8 collective-permute-start.12
  23.1 2.0 %collective-permute-start.11 = (bf16[256,1024]{1,0:T(8,128)(2,1)S(1)}, bf16[256,1024]{1,0:T(8,128)(2,1)S(1)}, u32[]{:S(2)}, u32[]{:S(2)}) collective-permute-start(bf16[256,1024]{1,0:T(8,128)(2,1)S(1)} %shard_map.114.rest_0_), channel_id=1, source_target_pairs={{0,2},{1,3},{2,0},{3,1},{4,6},{5,7},{6,4},{7,5},{8,10},{9,11},{10,... | collective-permute-start | bytes 1572872 | tf_op jit(solution)/shard_map/ppermute | solution.py:427
  25.1 7.8 %collective-permute-done.5.rest_6_ = bf16[3,128,256]{2,1,0:T(8,128)(2,1)S(1)} collective-permute-done((bf16[3,128,256]{2,1,0:T(8,128)(2,1)S(1)}, bf16[3,128,256]{2,1,0:T(8,128)(2,1)S(1)}, u32[]{:S(2)}, u32[]{:S(2)}) %collective-permute-start.5) | collective-permute-done | bytes 196640 | tf_op jit(solution)/shard_map/ppermute | solution.py:427
  32.9 2.2 %collective-permute-start.6 = (bf16[3,128,256]{2,1,0:T(8,128)(2,1)S(1)}, bf16[3,128,256]{2,1,0:T(8,128)(2,1)S(1)}, u32[]{:S(2)}, u32[]{:S(2)}) collective-permute-start(bf16[3,128,256]{2,1,0:T(8,128)(2,1)S(1)} %get-tuple-element.63), channel_id=1, source_target_pairs={{0,1},{1,0},{2,3},{3,2},{4,5},{5,4},{6,7},{7,6},{8,9},{9,8},{10,11... | collective-permute-start | bytes 589832 | tf_op jit(solution)/shard_map/ppermute | solution.py:427
  35.1 1.1 %collective-permute-done.6.rest_7_ = bf16[3,128,256]{2,1,0:T(8,128)(2,1)S(1)} collective-permute-done((bf16[3,128,256]{2,1,0:T(8,128)(2,1)S(1)}, bf16[3,128,256]{2,1,0:T(8,128)(2,1)S(1)}, u32[]{:S(2)}, u32[]{:S(2)}) %collective-permute-start.6) | collective-permute-done | bytes 196640 | tf_op jit(solution)/shard_map/ppermute | solution.py:427
  36.2 5.3 %shard_map.111 = (bf16[1024,256]{1,0:T(8,128)(2,1)S(1)}, bf16[1024,256]{1,0:T(8,128)(2,1)S(1)}, bf16[2,128,1024]{2,1,0:T(8,128)(2,1)S(1)}, bf16[2,1024,1024]{2,1...) custom-call(s32[1,8,8]{2,1,0:T(8,128)S(1)} %copy-done, ...), custom_call_target="tpu_custom_call" | custom-call | flops 1073741824 | bytes 8388608 | tf_op jit(solution)/shard_map/pallas_call | solution.py:43
  41.6 0.4 collective-permute-start.7
  42.0 0.1 shard_map.113
  42.1 3.9 %collective-permute-done.12.rest_2_ = bf16[256,1024]{1,0:T(8,128)(2,1)S(1)} collective-permute-done((bf16[256,1024]{1,0:T(8,128)(2,1)S(1)}, bf16[256,1024]{1,0:T(8,128)(2,1)S(1)}, u32[]{:S(2)}, u32[]{:S(2)}) %collective-permute-start.12) | collective-permute-done | bytes 524320 | tf_op jit(solution)/shard_map/ppermute | solution.py:427
  46.0 1.3 %shard_map.115 = (f32[256,1024]{1,0:T(8,128)S(1)}, bf16[256,1024]{1,0:T(8,128)(2,1)S(1)}, bf16[1024,1024]{1,0:T(8,128)(2,1)S(1)}) custom-call(bf16[256,1024]{1,0:T(8,128)(2,1)S(1)} %shard_map.114.rest_0_, bf16[256,1024]{1,0:T(8,128)(2,1)S(1)} %collective-permute-done.11.rest_1_, bf16[256,1024]{1,0:T(8,128)(2,1)S(1)} %collective-permute-done.12.rest_2_, ...), custom_call_target="tpu_custom_call" | custom-call | flops 1073741824 | bytes 8388608 | tf_op jit(solution)/shard_map/pallas_call | solution.py:43
  47.4 1.3 %shard_map.116 = (f32[256,1024]{1,0:T(8,128)S(1)}, bf16[256,1024]{1,0:T(8,128)(2,1)S(1)}, bf16[256,1024]{1,0:T(8,128)(2,1)S(1)}, bf16[128,1024]{1,0:T(8,128)(2,1)S(1)}, bf16[128,1024]{1,0:T(8,128)(2,1)S(1)}) custom-call(bf16[1024,256]{1,0:T(8,128)(2,1)S(1)} %get-tuple-element.64.attn_ref, bf16[1024,256]{1,0:T(8,128)(2,1)S(1)} %collective-permute-done.7.recv_ref, ...), custom_call_target="tpu_custom_call" | custom-call | flops 1073741824 | bytes 6291456 | tf_op jit(solution)/shard_map/pallas_call | solution.py:43
  48.7 0.4 collective-permute-start.15
  49.1 1.2 %collective-permute-start.16 = (bf16[128,1024]{1,0:T(8,128)(2,1)S(1)}, bf16[128,1024]{1,0:T(8,128)(2,1)S(1)}, u32[]{:S(2)}, u32[]{:S(2)}) collective-permute-start(bf16[128,1024]{1,0:T(8,128)(2,1)S(1)} %get-tuple-element.89), channel_id=1, source_target_pairs={{0,4},{1,5},{2,6},{3,7},{4,0},{5,1},{6,2},{7,3},{8,12},{9,13},{10,... | collective-permute-start | bytes 786440 | tf_op jit(solution)/shard_map/ppermute | solution.py:427
  50.3 1.5 %shard_map.117 = (f32[2,128,1024]{2,1,0:T(8,128)S(1)}, bf16[2,128,1024]{2,1,0:T(8,128)(2,1)S(1)}) custom-call(bf16[2,128,1024]{2,1,0:T(8,128)(2,1)S(1)} %get-tuple-element.78.attn_t_ref, bf16[1024,256]{1,0:T(8,128)(2,1)S(1)} %collective-permute-done.7.recv_ref, bf16[1024,1024]{1,0:T(8,128)(2,1)S(1)} %get-tuple-element.79.cot_ref), custom_call_target="tpu_custom_call" | custom-call | flops 1073741824 | bytes 6291456 | tf_op jit(solution)/shard_map/pallas_call | solution.py:43
  51.8 1.6 %collective-permute-start.20 = (bf16[2,128,1024]{2,1,0:T(8,128)(2,1)S(1)}, bf16[2,128,1024]{2,1,0:T(8,128)(2,1)S(1)}, u32[]{:S(2)}, u32[]{:S(2)}) collective-permute-start(bf16[2,128,1024]{2,1,0:T(8,128)(2,1)S(1)} %get-tuple-element.94), channel_id=1, source_target_pairs={{0,8},{8,0},{16,24},{24,16},{1,9},{9,1},{17,25},{25,17},{2,10},{10... | collective-permute-start | bytes 1572872 | tf_op jit(solution)/shard_map/ppermute | solution.py:430
  53.5 4.5 %shard_map.118 = (bf16[3,128,256]{2,1,0:T(8,128)(2,1)S(1)}, bf16[3,128,256]{2,1,0:T(8,128)(2,1)S(1)}, bf16[3,128,256]{2,1,0:T(8,128)(2,1)S(1)}, bf16[3,128,256]{...) custom-call(bf16[2,1024,1024]{2,1,0:T(8,128)(2,1)S(1)} %get-tuple-el, ...), custom_call_target="tpu_custom_call" | custom-call | flops 2147483648 | bytes 8388608 | tf_op jit(solution)/shard_map/pallas_call | solution.py:43
  58.0 0.1 shard_map.119
  58.2 1.6 %collective-permute-start.17 = (bf16[256,1024]{1,0:T(8,128)(2,1)S(1)}, bf16[256,1024]{1,0:T(8,128)(2,1)S(1)}, u32[]{:S(2)}, u32[]{:S(2)}) collective-permute-start(bf16[256,1024]{1,0:T(8,128)(2,1)S(1)} %get-tuple-element.90), channel_id=1, source_target_pairs={{0,2},{1,3},{2,0},{3,1},{4,6},{5,7},{6,4},{7,5},{8,10},{9,11},{10,... | collective-permute-start | bytes 1572872 | tf_op jit(solution)/shard_map/ppermute | solution.py:427
  59.7 1.0 %collective-permute-start.18 = (bf16[256,1024]{1,0:T(8,128)(2,1)S(1)}, bf16[256,1024]{1,0:T(8,128)(2,1)S(1)}, u32[]{:S(2)}, u32[]{:S(2)}) collective-permute-start(bf16[256,1024]{1,0:T(8,128)(2,1)S(1)} %get-tuple-element.91), channel_id=1, source_target_pairs={{0,4},{1,5},{2,6},{3,7},{4,0},{5,1},{6,2},{7,3},{8,12},{9,13},{10,... | collective-permute-start | bytes 1572872 | tf_op jit(solution)/shard_map/ppermute | solution.py:427
  60.8 4.9 %collective-permute-done.20.recv_ref = bf16[2,128,1024]{2,1,0:T(8,128)(2,1)S(1)} collective-permute-done((bf16[2,128,1024]{2,1,0:T(8,128)(2,1)S(1)}, bf16[2,128,1024]{2,1,0:T(8,128)(2,1)S(1)}, u32[]{:S(2)}, u32[]{:S(2)}) %collective-permute-start.20) | collective-permute-done | bytes 524320 | tf_op jit(solution)/shard_map/ppermute | solution.py:430
  65.6 0.1 shard_map.121
  65.8 2.2 %collective-permute-start.22 = (bf16[1,128,1024]{2,1,0:T(8,128)(2,1)S(1)}, bf16[1,128,1024]{2,1,0:T(8,128)(2,1)S(1)}, u32[]{:S(2)}, u32[]{:S(2)}) collective-permute-start(bf16[1,128,1024]{2,1,0:T(8,128)(2,1)S(1)} %get-tuple-element.98), channel_id=1, source_target_pairs={{0,16},{8,24},{16,0},{24,8},{1,17},{9,25},{17,1},{25,9},{2,18},{10... | collective-permute-start | bytes 786440 | tf_op jit(solution)/shard_map/ppermute | solution.py:430
  67.9 1.5 %collective-permute-start.21 = (bf16[3,128,256]{2,1,0:T(8,128)(2,1)S(1)}, bf16[3,128,256]{2,1,0:T(8,128)(2,1)S(1)}, u32[]{:S(2)}, u32[]{:S(2)}) collective-permute-start(bf16[3,128,256]{2,1,0:T(8,128)(2,1)S(1)} %get-tuple-element.96), channel_id=1, source_target_pairs={{0,6},{1,7},{2,4},{3,5},{4,2},{5,3},{6,0},{7,1},{8,14},{9,15},{10,... | collective-permute-start | bytes 589832 | tf_op jit(solution)/shard_map/ppermute | solution.py:427
  69.4 1.4 %collective-permute-start.24 = (bf16[3,128,256]{2,1,0:T(8,128)(2,1)S(1)}, bf16[3,128,256]{2,1,0:T(8,128)(2,1)S(1)}, u32[]{:S(2)}, u32[]{:S(2)}) collective-permute-start(bf16[3,128,256]{2,1,0:T(8,128)(2,1)S(1)} %get-tuple-element.101), channel_id=1, source_target_pairs={{0,2},{1,3},{2,0},{3,1},{4,6},{5,7},{6,4},{7,5},{8,10},{9,11},{10,... | collective-permute-start | bytes 589832 | tf_op jit(solution)/shard_map/ppermute | solution.py:427
  70.8 2.3 %collective-permute-done.17.rest_0_ = bf16[256,1024]{1,0:T(8,128)(2,1)S(1)} collective-permute-done((bf16[256,1024]{1,0:T(8,128)(2,1)S(1)}, bf16[256,1024]{1,0:T(8,128)(2,1)S(1)}, u32[]{:S(2)}, u32[]{:S(2)}) %collective-permute-start.17) | collective-permute-done | bytes 524320 | tf_op jit(solution)/shard_map/ppermute | solution.py:427
  73.1 1.1 %collective-permute-start.25 = (bf16[3,128,256]{2,1,0:T(8,128)(2,1)S(1)}, bf16[3,128,256]{2,1,0:T(8,128)(2,1)S(1)}, u32[]{:S(2)}, u32[]{:S(2)}) collective-permute-start(bf16[3,128,256]{2,1,0:T(8,128)(2,1)S(1)} %get-tuple-element.102), channel_id=1, source_target_pairs={{0,4},{1,5},{2,6},{3,7},{4,0},{5,1},{6,2},{7,3},{8,12},{9,13},{10,... | collective-permute-start | bytes 589832 | tf_op jit(solution)/shard_map/ppermute | solution.py:427
  74.2 3.9 %collective-permute-done.18.rest_1_ = bf16[256,1024]{1,0:T(8,128)(2,1)S(1)} collective-permute-done((bf16[256,1024]{1,0:T(8,128)(2,1)S(1)}, bf16[256,1024]{1,0:T(8,128)(2,1)S(1)}, u32[]{:S(2)}, u32[]{:S(2)}) %collective-permute-start.18) | collective-permute-done | bytes 524320 | tf_op jit(solution)/shard_map/ppermute | solution.py:427
  78.1 0.2 shard_map.120
  78.3 0.1 collective-permute-start.19
  78.4 1.3 %collective-permute-done.22.recv_ref = bf16[1,128,1024]{2,1,0:T(8,128)(2,1)S(1)} collective-permute-done((bf16[1,128,1024]{2,1,0:T(8,128)(2,1)S(1)}, bf16[1,128,1024]{2,1,0:T(8,128)(2,1)S(1)}, u32[]{:S(2)}, u32[]{:S(2)}) %collective-permute-start.22) | collective-permute-done | bytes 262176 | tf_op jit(solution)/shard_map/ppermute | solution.py:430
  79.8 0.8 collective-permute-done.24.rest_2_
  80.6 0.8 collective-permute-start.27
  81.4 4.2 %collective-permute-done.25.rest_3_ = bf16[3,128,256]{2,1,0:T(8,128)(2,1)S(1)} collective-permute-done((bf16[3,128,256]{2,1,0:T(8,128)(2,1)S(1)}, bf16[3,128,256]{2,1,0:T(8,128)(2,1)S(1)}, u32[]{:S(2)}, u32[]{:S(2)}) %collective-permute-start.25) | collective-permute-done | bytes 196640 | tf_op jit(solution)/shard_map/ppermute | solution.py:427
  85.6 1.1 %collective-permute-start.29 = (bf16[3,128,256]{2,1,0:T(8,128)(2,1)S(1)}, bf16[3,128,256]{2,1,0:T(8,128)(2,1)S(1)}, u32[]{:S(2)}, u32[]{:S(2)}) collective-permute-start(bf16[3,128,256]{2,1,0:T(8,128)(2,1)S(1)} %get-tuple-element.106), channel_id=1, source_target_pairs={{0,1},{1,0},{2,3},{3,2},{4,5},{5,4},{6,7},{7,6},{8,9},{9,8},{10,11... | collective-permute-start | bytes 589832 | tf_op jit(solution)/shard_map/ppermute | solution.py:427
  86.7 1.7 %collective-permute-done.27.rest_5_ = bf16[3,128,256]{2,1,0:T(8,128)(2,1)S(1)} collective-permute-done((bf16[3,128,256]{2,1,0:T(8,128)(2,1)S(1)}, bf16[3,128,256]{2,1,0:T(8,128)(2,1)S(1)}, u32[]{:S(2)}, u32[]{:S(2)}) %collective-permute-start.27) | collective-permute-done | bytes 196640 | tf_op jit(solution)/shard_map/ppermute | solution.py:427
  88.4 3.9 %collective-permute-done.28.rest_6_ = bf16[3,128,256]{2,1,0:T(8,128)(2,1)S(1)} collective-permute-done((bf16[3,128,256]{2,1,0:T(8,128)(2,1)S(1)}, bf16[3,128,256]{2,1,0:T(8,128)(2,1)S(1)}, u32[]{:S(2)}, u32[]{:S(2)}) %collective-permute-start.28) | collective-permute-done | bytes 196640 | tf_op jit(solution)/shard_map/ppermute | solution.py:427
  92.3 1.7 %shard_map.123 = (bf16[1,128,2048]{2,1,0:T(8,128)(2,1)}, bf16[1,128,2048]{2,1,0:T(8,128)(2,1)}, bf16[1,128,2048]{2,1,0:T(8,128)(2,1)}, bf16[1,128,2048]{2,1,0:T(8,128)(2,1)}, f32[64,2048]{1,0:T(8,128)}) custom-call(bf16[128,1024]{1,0:T(8,128)(2,1)S(1)} %get-tuple-element.92.keep_ref, bf16[128,1024]{1,0:T(8,128)(2,1)S(1)} %collective-permute-done.19.recv_ref, ...), custom_call_target="tpu_custom_call" | custom-call | bytes 4194304 | tf_op jit(solution)/shard_map/pallas_call | solution.py:43
  (30 shorter events, 0.4 us)
Async XLA Ops:
  2.3 33.9 %copy-start = (s32[1,8,8]{2,1,0:T(8,128)S(1)}, s32[1,8,8]{2,1,0:T(8,128)}, u32[]{:S(2)}) copy-start(s32[1,8,8]{2,1,0:T(8,128)} %adj_ref.1) | copy-start | bytes 772
  2.3 33.9 %copy-start.1 = (s32[1,8]{1,0:T(1,128)S(1)}, s32[1,8]{1,0:T(1,128)}, u32[]{:S(2)}) copy-start(s32[1,8]{1,0:T(1,128)} %cnt_ref.1) | copy-start | bytes 100
  2.3 8.8 %collective-permute-start = (bf16[3,128,256]{2,1,0:T(8,128)(2,1)S(1)}, bf16[3,128,256]{2,1,0:T(8,128)(2,1)S(1)}, u32[]{:S(2)}, u32[]{:S(2)}) collective-permute-start(bf16[3,128,256]{2,1,0:T(8,128)(2,1)S(1)} %get-tuple-element.57), channel_id=1, source_target_pairs={{0,6},{1,7},{2,4},{3,5},{4,2},{5,3},{6,0},{7,1},{8,14},{9,15},{10,... | collective-permute-start | bytes 589832 | tf_op jit(solution)/shard_map/ppermute | solution.py:427
  3.9 10.3 %collective-permute-start.1 = (bf16[3,128,256]{2,1,0:T(8,128)(2,1)S(1)}, bf16[3,128,256]{2,1,0:T(8,128)(2,1)S(1)}, u32[]{:S(2)}, u32[]{:S(2)}) collective-permute-start(bf16[3,128,256]{2,1,0:T(8,128)(2,1)S(1)} %get-tuple-element.58), channel_id=1, source_target_pairs={{0,2},{1,3},{2,0},{3,1},{4,6},{5,7},{6,4},{7,5},{8,10},{9,11},{10,... | collective-permute-start | bytes 589832 | tf_op jit(solution)/shard_map/ppermute | solution.py:427
  5.4 8.8 %collective-permute-start.10 = (bf16[128,1024]{1,0:T(8,128)(2,1)S(1)}, bf16[128,1024]{1,0:T(8,128)(2,1)S(1)}, u32[]{:S(2)}, u32[]{:S(2)}) collective-permute-start(bf16[128,1024]{1,0:T(8,128)(2,1)S(1)} %get-tuple-element.68), channel_id=1, source_target_pairs={{0,1},{1,0},{2,3},{3,2},{4,5},{5,4},{6,7},{7,6},{8,9},{9,8},{10,11... | collective-permute-start | bytes 786440 | tf_op jit(solution)/shard_map/ppermute | solution.py:427
  5.4 15.2 %collective-permute-start.8 = (bf16[1,128,1024]{2,1,0:T(8,128)(2,1)S(1)}, bf16[1,128,1024]{2,1,0:T(8,128)(2,1)S(1)}, u32[]{:S(2)}, u32[]{:S(2)}) collective-permute-start(bf16[1,128,1024]{2,1,0:T(8,128)(2,1)S(1)} %bitcast.4), channel_id=1, source_target_pairs={{0,16},{8,24},{16,0},{24,8},{1,17},{9,25},{17,1},{25,9},{2,18},{10... | collective-permute-start | bytes 786440 | tf_op jit(solution)/shard_map/ppermute | solution.py:430
  7.9 11.9 %collective-permute-start.2 = (bf16[3,128,256]{2,1,0:T(8,128)(2,1)S(1)}, bf16[3,128,256]{2,1,0:T(8,128)(2,1)S(1)}, u32[]{:S(2)}, u32[]{:S(2)}) collective-permute-start(bf16[3,128,256]{2,1,0:T(8,128)(2,1)S(1)} %get-tuple-element.59), channel_id=1, source_target_pairs={{0,4},{1,5},{2,6},{3,7},{4,0},{5,1},{6,2},{7,3},{8,12},{9,13},{10,... | collective-permute-start | bytes 589832 | tf_op jit(solution)/shard_map/ppermute | solution.py:427
  11.1 11.2 %collective-permute-start.3 = (bf16[3,128,256]{2,1,0:T(8,128)(2,1)S(1)}, bf16[3,128,256]{2,1,0:T(8,128)(2,1)S(1)}, u32[]{:S(2)}, u32[]{:S(2)}) collective-permute-start(bf16[3,128,256]{2,1,0:T(8,128)(2,1)S(1)} %get-tuple-element.60), channel_id=1, source_target_pairs={{0,7},{1,6},{2,5},{3,4},{4,3},{5,2},{6,1},{7,0},{8,15},{9,14},{10,... | collective-permute-start | bytes 589832 | tf_op jit(solution)/shard_map/ppermute | solution.py:427
  14.2 8.9 %collective-permute-start.4 = (bf16[3,128,256]{2,1,0:T(8,128)(2,1)S(1)}, bf16[3,128,256]{2,1,0:T(8,128)(2,1)S(1)}, u32[]{:S(2)}, u32[]{:S(2)}) collective-permute-start(bf16[3,128,256]{2,1,0:T(8,128)(2,1)S(1)} %get-tuple-element.61), channel_id=1, source_target_pairs={{0,3},{1,2},{2,1},{3,0},{4,7},{5,6},{6,5},{7,4},{8,11},{9,10},{10,... | collective-permute-start | bytes 589832 | tf_op jit(solution)/shard_map/ppermute | solution.py:427
  14.2 18.7 %collective-permute-start.5 = (bf16[3,128,256]{2,1,0:T(8,128)(2,1)S(1)}, bf16[3,128,256]{2,1,0:T(8,128)(2,1)S(1)}, u32[]{:S(2)}, u32[]{:S(2)}) collective-permute-start(bf16[3,128,256]{2,1,0:T(8,128)(2,1)S(1)} %get-tuple-element.62), channel_id=1, source_target_pairs={{0,5},{1,4},{2,7},{3,6},{4,1},{5,0},{6,3},{7,2},{8,13},{9,12},{10,... | collective-permute-start | bytes 589832 | tf_op jit(solution)/shard_map/ppermute | solution.py:427
  19.9 22.2 %collective-permute-start.13 = (bf16[256,1024]{1,0:T(8,128)(2,1)S(1)}, bf16[256,1024]{1,0:T(8,128)(2,1)S(1)}, u32[]{:S(2)}, u32[]{:S(2)}) collective-permute-start(bf16[256,1024]{1,0:T(8,128)(2,1)S(1)} %shard_map.114.rest_0_), channel_id=1, source_target_pairs={{0,6},{1,7},{2,4},{3,5},{4,2},{5,3},{6,0},{7,1},{8,14},{9,15},{10,... | collective-permute-start | bytes 1572872 | tf_op jit(solution)/shard_map/ppermute | solution.py:427
  20.7 21.3 %collective-permute-start.9 = (bf16[2,128,1024]{2,1,0:T(8,128)(2,1)S(1)}, bf16[2,128,1024]{2,1,0:T(8,128)(2,1)S(1)}, u32[]{:S(2)}, u32[]{:S(2)}) collective-permute-start(bf16[2,128,1024]{2,1,0:T(8,128)(2,1)S(1)} %shard_map.112.mine_ref), channel_id=1, source_target_pairs={{0,8},{8,0},{16,24},{24,16},{1,9},{9,1},{17,25},{25,17},{2,10},{10... | collective-permute-start | bytes 1572872 | tf_op jit(solution)/shard_map/ppermute | solution.py:430
  22.3 23.8 %collective-permute-start.12 = (bf16[256,1024]{1,0:T(8,128)(2,1)S(1)}, bf16[256,1024]{1,0:T(8,128)(2,1)S(1)}, u32[]{:S(2)}, u32[]{:S(2)}) collective-permute-start(bf16[256,1024]{1,0:T(8,128)(2,1)S(1)} %shard_map.114.rest_0_), channel_id=1, source_target_pairs={{0,4},{1,5},{2,6},{3,7},{4,0},{5,1},{6,2},{7,3},{8,12},{9,13},{10,... | collective-permute-start | bytes 1572872 | tf_op jit(solution)/shard_map/ppermute | solution.py:427
  23.1 23.0 %collective-permute-start.11 = (bf16[256,1024]{1,0:T(8,128)(2,1)S(1)}, bf16[256,1024]{1,0:T(8,128)(2,1)S(1)}, u32[]{:S(2)}, u32[]{:S(2)}) collective-permute-start(bf16[256,1024]{1,0:T(8,128)(2,1)S(1)} %shard_map.114.rest_0_), channel_id=1, source_target_pairs={{0,2},{1,3},{2,0},{3,1},{4,6},{5,7},{6,4},{7,5},{8,10},{9,11},{10,... | collective-permute-start | bytes 1572872 | tf_op jit(solution)/shard_map/ppermute | solution.py:427
  32.9 3.3 %collective-permute-start.6 = (bf16[3,128,256]{2,1,0:T(8,128)(2,1)S(1)}, bf16[3,128,256]{2,1,0:T(8,128)(2,1)S(1)}, u32[]{:S(2)}, u32[]{:S(2)}) collective-permute-start(bf16[3,128,256]{2,1,0:T(8,128)(2,1)S(1)} %get-tuple-element.63), channel_id=1, source_target_pairs={{0,1},{1,0},{2,3},{3,2},{4,5},{5,4},{6,7},{7,6},{8,9},{9,8},{10,11... | collective-permute-start | bytes 589832 | tf_op jit(solution)/shard_map/ppermute | solution.py:427
  41.6 5.8 %collective-permute-start.7 = (bf16[1024,256]{1,0:T(8,128)(2,1)S(1)}, bf16[1024,256]{1,0:T(8,128)(2,1)S(1)}, u32[]{:S(2)}, u32[]{:S(2)}) collective-permute-start(bf16[1024,256]{1,0:T(8,128)(2,1)S(1)} %get-tuple-element.65), channel_id=1, source_target_pairs={{0,1},{1,0},{2,3},{3,2},{4,5},{5,4},{6,7},{7,6},{8,9},{9,8},{10,11... | collective-permute-start | bytes 1572872 | tf_op jit(solution)/shard_map/ppermute | solution.py:427
  47.3 6.1 %collective-permute-start.14 = (bf16[256,1024]{1,0:T(8,128)(2,1)S(1)}, bf16[256,1024]{1,0:T(8,128)(2,1)S(1)}, u32[]{:S(2)}, u32[]{:S(2)}) collective-permute-start(bf16[256,1024]{1,0:T(8,128)(2,1)S(1)} %get-tuple-element.82), channel_id=1, source_target_pairs={{0,1},{1,0},{2,3},{3,2},{4,5},{5,4},{6,7},{7,6},{8,9},{9,8},{10,11... | collective-permute-start | bytes 1572872 | tf_op jit(solution)/shard_map/ppermute | solution.py:427
  48.7 9.3 %collective-permute-start.15 = (bf16[128,1024]{1,0:T(8,128)(2,1)S(1)}, bf16[128,1024]{1,0:T(8,128)(2,1)S(1)}, u32[]{:S(2)}, u32[]{:S(2)}) collective-permute-start(bf16[128,1024]{1,0:T(8,128)(2,1)S(1)} %get-tuple-element.87), channel_id=1, source_target_pairs={{0,2},{1,3},{2,0},{3,1},{4,6},{5,7},{6,4},{7,5},{8,10},{9,11},{10,... | collective-permute-start | bytes 786440 | tf_op jit(solution)/shard_map/ppermute | solution.py:427
  49.1 8.9 %collective-permute-start.16 = (bf16[128,1024]{1,0:T(8,128)(2,1)S(1)}, bf16[128,1024]{1,0:T(8,128)(2,1)S(1)}, u32[]{:S(2)}, u32[]{:S(2)}) collective-permute-start(bf16[128,1024]{1,0:T(8,128)(2,1)S(1)} %get-tuple-element.89), channel_id=1, source_target_pairs={{0,4},{1,5},{2,6},{3,7},{4,0},{5,1},{6,2},{7,3},{8,12},{9,13},{10,... | collective-permute-start | bytes 786440 | tf_op jit(solution)/shard_map/ppermute | solution.py:427
  51.8 13.8 %collective-permute-start.20 = (bf16[2,128,1024]{2,1,0:T(8,128)(2,1)S(1)}, bf16[2,128,1024]{2,1,0:T(8,128)(2,1)S(1)}, u32[]{:S(2)}, u32[]{:S(2)}) collective-permute-start(bf16[2,128,1024]{2,1,0:T(8,128)(2,1)S(1)} %get-tuple-element.94), channel_id=1, source_target_pairs={{0,8},{8,0},{16,24},{24,16},{1,9},{9,1},{17,25},{25,17},{2,10},{10... | collective-permute-start | bytes 1572872 | tf_op jit(solution)/shard_map/ppermute | solution.py:430
  58.2 14.9 %collective-permute-start.17 = (bf16[256,1024]{1,0:T(8,128)(2,1)S(1)}, bf16[256,1024]{1,0:T(8,128)(2,1)S(1)}, u32[]{:S(2)}, u32[]{:S(2)}) collective-permute-start(bf16[256,1024]{1,0:T(8,128)(2,1)S(1)} %get-tuple-element.90), channel_id=1, source_target_pairs={{0,2},{1,3},{2,0},{3,1},{4,6},{5,7},{6,4},{7,5},{8,10},{9,11},{10,... | collective-permute-start | bytes 1572872 | tf_op jit(solution)/shard_map/ppermute | solution.py:427
  59.7 18.3 %collective-permute-start.18 = (bf16[256,1024]{1,0:T(8,128)(2,1)S(1)}, bf16[256,1024]{1,0:T(8,128)(2,1)S(1)}, u32[]{:S(2)}, u32[]{:S(2)}) collective-permute-start(bf16[256,1024]{1,0:T(8,128)(2,1)S(1)} %get-tuple-element.91), channel_id=1, source_target_pairs={{0,4},{1,5},{2,6},{3,7},{4,0},{5,1},{6,2},{7,3},{8,12},{9,13},{10,... | collective-permute-start | bytes 1572872 | tf_op jit(solution)/shard_map/ppermute | solution.py:427
  65.8 13.8 %collective-permute-start.22 = (bf16[1,128,1024]{2,1,0:T(8,128)(2,1)S(1)}, bf16[1,128,1024]{2,1,0:T(8,128)(2,1)S(1)}, u32[]{:S(2)}, u32[]{:S(2)}) collective-permute-start(bf16[1,128,1024]{2,1,0:T(8,128)(2,1)S(1)} %get-tuple-element.98), channel_id=1, source_target_pairs={{0,16},{8,24},{16,0},{24,8},{1,17},{9,25},{17,1},{25,9},{2,18},{10... | collective-permute-start | bytes 786440 | tf_op jit(solution)/shard_map/ppermute | solution.py:430
  67.9 10.3 %collective-permute-start.21 = (bf16[3,128,256]{2,1,0:T(8,128)(2,1)S(1)}, bf16[3,128,256]{2,1,0:T(8,128)(2,1)S(1)}, u32[]{:S(2)}, u32[]{:S(2)}) collective-permute-start(bf16[3,128,256]{2,1,0:T(8,128)(2,1)S(1)} %get-tuple-element.96), channel_id=1, source_target_pairs={{0,6},{1,7},{2,4},{3,5},{4,2},{5,3},{6,0},{7,1},{8,14},{9,15},{10,... | collective-permute-start | bytes 589832 | tf_op jit(solution)/shard_map/ppermute | solution.py:427
  69.4 11.2 %collective-permute-start.24 = (bf16[3,128,256]{2,1,0:T(8,128)(2,1)S(1)}, bf16[3,128,256]{2,1,0:T(8,128)(2,1)S(1)}, u32[]{:S(2)}, u32[]{:S(2)}) collective-permute-start(bf16[3,128,256]{2,1,0:T(8,128)(2,1)S(1)} %get-tuple-element.101), channel_id=1, source_target_pairs={{0,2},{1,3},{2,0},{3,1},{4,6},{5,7},{6,4},{7,5},{8,10},{9,11},{10,... | collective-permute-start | bytes 589832 | tf_op jit(solution)/shard_map/ppermute | solution.py:427
  73.1 12.5 %collective-permute-start.25 = (bf16[3,128,256]{2,1,0:T(8,128)(2,1)S(1)}, bf16[3,128,256]{2,1,0:T(8,128)(2,1)S(1)}, u32[]{:S(2)}, u32[]{:S(2)}) collective-permute-start(bf16[3,128,256]{2,1,0:T(8,128)(2,1)S(1)} %get-tuple-element.102), channel_id=1, source_target_pairs={{0,4},{1,5},{2,6},{3,7},{4,0},{5,1},{6,2},{7,3},{8,12},{9,13},{10,... | collective-permute-start | bytes 589832 | tf_op jit(solution)/shard_map/ppermute | solution.py:427
  78.1 7.5 %collective-permute-start.26 = (bf16[3,128,256]{2,1,0:T(8,128)(2,1)S(1)}, bf16[3,128,256]{2,1,0:T(8,128)(2,1)S(1)}, u32[]{:S(2)}, u32[]{:S(2)}) collective-permute-start(bf16[3,128,256]{2,1,0:T(8,128)(2,1)S(1)} %get-tuple-element.103), channel_id=1, source_target_pairs={{0,7},{1,6},{2,5},{3,4},{4,3},{5,2},{6,1},{7,0},{8,15},{9,14},{10,... | collective-permute-start | bytes 589832 | tf_op jit(solution)/shard_map/ppermute | solution.py:427
  78.3 14.0 %collective-permute-start.19 = (bf16[128,1024]{1,0:T(8,128)(2,1)S(1)}, bf16[128,1024]{1,0:T(8,128)(2,1)S(1)}, u32[]{:S(2)}, u32[]{:S(2)}) collective-permute-start(bf16[128,1024]{1,0:T(8,128)(2,1)S(1)} %get-tuple-element.93), channel_id=1, source_target_pairs={{0,1},{1,0},{2,3},{3,2},{4,5},{5,4},{6,7},{7,6},{8,9},{9,8},{10,11... | collective-permute-start | bytes 786440 | tf_op jit(solution)/shard_map/ppermute | solution.py:427
  79.7 12.6 %collective-permute-start.23 = (f32[64,1024]{1,0:T(8,128)S(1)}, f32[64,1024]{1,0:T(8,128)S(1)}, u32[]{:S(2)}, u32[]{:S(2)}) collective-permute-start(f32[64,1024]{1,0:T(8,128)S(1)} %get-tuple-element.100), channel_id=1, source_target_pairs={{0,1},{1,0},{2,3},{3,2},{4,5},{5,4},{6,7},{7,6},{8,9},{9,8},{10,11... | collective-permute-start | bytes 786440 | tf_op jit(solution)/shard_map/ppermute | solution.py:427
  80.6 7.9 %collective-permute-start.27 = (bf16[3,128,256]{2,1,0:T(8,128)(2,1)S(1)}, bf16[3,128,256]{2,1,0:T(8,128)(2,1)S(1)}, u32[]{:S(2)}, u32[]{:S(2)}) collective-permute-start(bf16[3,128,256]{2,1,0:T(8,128)(2,1)S(1)} %get-tuple-element.104), channel_id=1, source_target_pairs={{0,3},{1,2},{2,1},{3,0},{4,7},{5,6},{6,5},{7,4},{8,11},{9,10},{10,... | collective-permute-start | bytes 589832 | tf_op jit(solution)/shard_map/ppermute | solution.py:427
  85.6 6.8 %collective-permute-start.28 = (bf16[3,128,256]{2,1,0:T(8,128)(2,1)S(1)}, bf16[3,128,256]{2,1,0:T(8,128)(2,1)S(1)}, u32[]{:S(2)}, u32[]{:S(2)}) collective-permute-start(bf16[3,128,256]{2,1,0:T(8,128)(2,1)S(1)} %get-tuple-element.105), channel_id=1, source_target_pairs={{0,5},{1,4},{2,7},{3,6},{4,1},{5,0},{6,3},{7,2},{8,13},{9,12},{10,... | collective-permute-start | bytes 589832 | tf_op jit(solution)/shard_map/ppermute | solution.py:427
  85.6 6.8 %collective-permute-start.29 = (bf16[3,128,256]{2,1,0:T(8,128)(2,1)S(1)}, bf16[3,128,256]{2,1,0:T(8,128)(2,1)S(1)}, u32[]{:S(2)}, u32[]{:S(2)}) collective-permute-start(bf16[3,128,256]{2,1,0:T(8,128)(2,1)S(1)} %get-tuple-element.106), channel_id=1, source_target_pairs={{0,1},{1,0},{2,3},{3,2},{4,5},{5,4},{6,7},{7,6},{8,9},{9,8},{10,11... | collective-permute-start | bytes 589832 | tf_op jit(solution)/shard_map/ppermute | solution.py:427

commit v5 on v4

--- a/solution.py
+++ b/solution.py
@@ -312,7 +312,7 @@
 def backward_kernel(n, per, expo, share_ref, queries, keys_t, vals, attn_t_ref, own_ref, recv_ref, *rest):
     outs, (dscores,) = by_slot(rest[:-1], n), rest[-1:]
     scale = HD**-0.5
-    tile = 2 * BLK
+    tile = 4 * BLK
     length = n * BLK
     for g in range(per):
         lanes = slice(g * HD, (g + 1) * HD)
@@ -328,11 +328,11 @@
             dvalue = mm(expo[g, rows, :], grad, NT).astype(BF16)
             dkey = (mm(dscores[rows, :], queries[g]) * scale).astype(BF16)
             dquery = (mm(keys_t[g], dscores[:, rows]).T * scale).astype(BF16)
-            for b in range(2):
+            for b in range(4):
                 part = slice(b * BLK, (b + 1) * BLK)
-                outs[2 * t + b][0, :, lanes] = dquery[part]
-                outs[2 * t + b][1, :, lanes] = dkey[part]
-                outs[2 * t + b][2, :, lanes] = dvalue[part]
+                outs[4 * t + b][0, :, lanes] = dquery[part]
+                outs[4 * t + b][1, :, lanes] = dkey[part]
+                outs[4 * t + b][2, :, lanes] = dvalue[part]
 
 
 def out_kernel(n, attn_ref, recv_ref, w_ref, *outs):

time: 94.3 us -> 94.3 us (level)
  no operation moved by 1% of the time
where the time goes in v5:
time: 94.3 us; the launch traced here: 94.1 us
  waiting for transfers between devices  46.6 us (49%)
  starting transfers between devices  28.6 us (30%)
  Pallas kernels  17.9 us (19%)
  between operations  0.98 us (1%)
    ppermute x26, waiting for transfers between devices, to(): return lax.ppermute(x, 'seq', [(i, i ^ j) for i in range(n)])  40.3 us
    ppermute x26, starting transfers between devices, to(): return lax.ppermute(x, 'seq', [(i, i ^ j) for i in range(n)])  20.6 us
    pallas_call x14, Pallas kernels, call(): pl.pallas_call(kernel, out_shape=tuple((shape for _, shape in outs)), in_...  17.9 us
    ppermute x4, starting transfers between devices, to_z(): return lax.ppermute(x, 'dp', [(i, i ^ j) for i in range(nz)])  7.96 us
    ppermute x4, waiting for transfers between devices, to_z(): return lax.ppermute(x, 'dp', [(i, i ^ j) for i in range(nz)])  6.29 us
  transfers between devices with their start and end apart: 30, of which 15 were waited for; matrix products, arithmetic and copies ran while one was open for 0% of the time, Pallas kernels for 16%

profile of v5, /device:TPU:2, one launch (start us, length us, event | category | flops | bytes accessed | tf_op | source)
XLA Modules:
  0.0 94.1 jit_solution(9793001147310338220)
XLA Ops:
  0.6 1.6 %shard_map.110 = (bf16[3,128,256]{2,1,0:T(8,128)(2,1)S(1)}, bf16[3,128,256]{2,1,0:T(8,128)(2,1)S(1)}, bf16[3,128,256]{2,1,0:T(8,128)(2,1)S(1)}, bf16[3,128,256]{...) custom-call(bf16[1,128,2048]{2,1,0:T(8,128)(2,1)} %q_ref.1, ...), custom_call_target="tpu_custom_call" | custom-call | bytes 8388608 | tf_op jit(solution)/shard_map/pallas_call | solution.py:43
  2.3 1.6 %collective-permute-start = (bf16[3,128,256]{2,1,0:T(8,128)(2,1)S(1)}, bf16[3,128,256]{2,1,0:T(8,128)(2,1)S(1)}, u32[]{:S(2)}, u32[]{:S(2)}) collective-permute-start(bf16[3,128,256]{2,1,0:T(8,128)(2,1)S(1)} %get-tuple-element.57), channel_id=1, source_target_pairs={{0,6},{1,7},{2,4},{3,5},{4,2},{5,3},{6,0},{7,1},{8,14},{9,15},{10,... | collective-permute-start | bytes 589832 | tf_op jit(solution)/shard_map/ppermute | solution.py:427
  3.9 1.5 %collective-permute-start.1 = (bf16[3,128,256]{2,1,0:T(8,128)(2,1)S(1)}, bf16[3,128,256]{2,1,0:T(8,128)(2,1)S(1)}, u32[]{:S(2)}, u32[]{:S(2)}) collective-permute-start(bf16[3,128,256]{2,1,0:T(8,128)(2,1)S(1)} %get-tuple-element.58), channel_id=1, source_target_pairs={{0,2},{1,3},{2,0},{3,1},{4,6},{5,7},{6,4},{7,5},{8,10},{9,11},{10,... | collective-permute-start | bytes 589832 | tf_op jit(solution)/shard_map/ppermute | solution.py:427
  5.4 2.6 %collective-permute-start.8 = (bf16[1,128,1024]{2,1,0:T(8,128)(2,1)S(1)}, bf16[1,128,1024]{2,1,0:T(8,128)(2,1)S(1)}, u32[]{:S(2)}, u32[]{:S(2)}) collective-permute-start(bf16[1,128,1024]{2,1,0:T(8,128)(2,1)S(1)} %bitcast.4), channel_id=1, source_target_pairs={{0,16},{8,24},{16,0},{24,8},{1,17},{9,25},{17,1},{25,9},{2,18},{10... | collective-permute-start | bytes 786440 | tf_op jit(solution)/shard_map/ppermute | solution.py:430
  7.9 0.5 collective-permute-start.2
  8.5 2.6 %collective-permute-done.rest_1_ = bf16[3,128,256]{2,1,0:T(8,128)(2,1)S(1)} collective-permute-done((bf16[3,128,256]{2,1,0:T(8,128)(2,1)S(1)}, bf16[3,128,256]{2,1,0:T(8,128)(2,1)S(1)}, u32[]{:S(2)}, u32[]{:S(2)}) %collective-permute-start) | collective-permute-done | bytes 196640 | tf_op jit(solution)/shard_map/ppermute | solution.py:427
  11.1 3.1 %collective-permute-done.1.rest_2_ = bf16[3,128,256]{2,1,0:T(8,128)(2,1)S(1)} collective-permute-done((bf16[3,128,256]{2,1,0:T(8,128)(2,1)S(1)}, bf16[3,128,256]{2,1,0:T(8,128)(2,1)S(1)}, u32[]{:S(2)}, u32[]{:S(2)}) %collective-permute-start.1) | collective-permute-done | bytes 196640 | tf_op jit(solution)/shard_map/ppermute | solution.py:427
  14.2 0.6 collective-permute-start.5
  14.8 5.1 %collective-permute-done.2.rest_3_ = bf16[3,128,256]{2,1,0:T(8,128)(2,1)S(1)} collective-permute-done((bf16[3,128,256]{2,1,0:T(8,128)(2,1)S(1)}, bf16[3,128,256]{2,1,0:T(8,128)(2,1)S(1)}, u32[]{:S(2)}, u32[]{:S(2)}) %collective-permute-start.2) | collective-permute-done | bytes 196640 | tf_op jit(solution)/shard_map/ppermute | solution.py:427
  19.9 0.6 collective-permute-start.13
  20.7 1.6 %collective-permute-start.9 = (bf16[2,128,1024]{2,1,0:T(8,128)(2,1)S(1)}, bf16[2,128,1024]{2,1,0:T(8,128)(2,1)S(1)}, u32[]{:S(2)}, u32[]{:S(2)}) collective-permute-start(bf16[2,128,1024]{2,1,0:T(8,128)(2,1)S(1)} %shard_map.112.mine_ref), channel_id=1, source_target_pairs={{0,8},{8,0},{16,24},{24,16},{1,9},{9,1},{17,25},{25,17},{2,10},{10... | collective-permute-start | bytes 1572872 | tf_op jit(solution)/shard_map/ppermute | solution.py:430
  22.3 0.8 collective-permute-start.12
  23.1 2.0 %collective-permute-start.11 = (bf16[256,1024]{1,0:T(8,128)(2,1)S(1)}, bf16[256,1024]{1,0:T(8,128)(2,1)S(1)}, u32[]{:S(2)}, u32[]{:S(2)}) collective-permute-start(bf16[256,1024]{1,0:T(8,128)(2,1)S(1)} %shard_map.114.rest_0_), channel_id=1, source_target_pairs={{0,2},{1,3},{2,0},{3,1},{4,6},{5,7},{6,4},{7,5},{8,10},{9,11},{10,... | collective-permute-start | bytes 1572872 | tf_op jit(solution)/shard_map/ppermute | solution.py:427
  25.1 7.8 %collective-permute-done.5.rest_6_ = bf16[3,128,256]{2,1,0:T(8,128)(2,1)S(1)} collective-permute-done((bf16[3,128,256]{2,1,0:T(8,128)(2,1)S(1)}, bf16[3,128,256]{2,1,0:T(8,128)(2,1)S(1)}, u32[]{:S(2)}, u32[]{:S(2)}) %collective-permute-start.5) | collective-permute-done | bytes 196640 | tf_op jit(solution)/shard_map/ppermute | solution.py:427
  32.9 2.2 %collective-permute-start.6 = (bf16[3,128,256]{2,1,0:T(8,128)(2,1)S(1)}, bf16[3,128,256]{2,1,0:T(8,128)(2,1)S(1)}, u32[]{:S(2)}, u32[]{:S(2)}) collective-permute-start(bf16[3,128,256]{2,1,0:T(8,128)(2,1)S(1)} %get-tuple-element.63), channel_id=1, source_target_pairs={{0,1},{1,0},{2,3},{3,2},{4,5},{5,4},{6,7},{7,6},{8,9},{9,8},{10,11... | collective-permute-start | bytes 589832 | tf_op jit(solution)/shard_map/ppermute | solution.py:427
  35.1 1.1 %collective-permute-done.6.rest_7_ = bf16[3,128,256]{2,1,0:T(8,128)(2,1)S(1)} collective-permute-done((bf16[3,128,256]{2,1,0:T(8,128)(2,1)S(1)}, bf16[3,128,256]{2,1,0:T(8,128)(2,1)S(1)}, u32[]{:S(2)}, u32[]{:S(2)}) %collective-permute-start.6) | collective-permute-done | bytes 196640 | tf_op jit(solution)/shard_map/ppermute | solution.py:427
  36.2 5.3 %shard_map.111 = (bf16[1024,256]{1,0:T(8,128)(2,1)S(1)}, bf16[1024,256]{1,0:T(8,128)(2,1)S(1)}, bf16[2,128,1024]{2,1,0:T(8,128)(2,1)S(1)}, bf16[2,1024,1024]{2,1...) custom-call(s32[1,8,8]{2,1,0:T(8,128)S(1)} %copy-done, ...), custom_call_target="tpu_custom_call" | custom-call | flops 1073741824 | bytes 8388608 | tf_op jit(solution)/shard_map/pallas_call | solution.py:43
  41.6 0.4 collective-permute-start.7
  42.0 0.1 shard_map.113
  42.1 3.9 %collective-permute-done.12.rest_2_ = bf16[256,1024]{1,0:T(8,128)(2,1)S(1)} collective-permute-done((bf16[256,1024]{1,0:T(8,128)(2,1)S(1)}, bf16[256,1024]{1,0:T(8,128)(2,1)S(1)}, u32[]{:S(2)}, u32[]{:S(2)}) %collective-permute-start.12) | collective-permute-done | bytes 524320 | tf_op jit(solution)/shard_map/ppermute | solution.py:427
  46.0 1.3 %shard_map.115 = (f32[256,1024]{1,0:T(8,128)S(1)}, bf16[256,1024]{1,0:T(8,128)(2,1)S(1)}, bf16[1024,1024]{1,0:T(8,128)(2,1)S(1)}) custom-call(bf16[256,1024]{1,0:T(8,128)(2,1)S(1)} %shard_map.114.rest_0_, bf16[256,1024]{1,0:T(8,128)(2,1)S(1)} %collective-permute-done.11.rest_1_, bf16[256,1024]{1,0:T(8,128)(2,1)S(1)} %collective-permute-done.12.rest_2_, ...), custom_call_target="tpu_custom_call" | custom-call | flops 1073741824 | bytes 8388608 | tf_op jit(solution)/shard_map/pallas_call | solution.py:43
  47.3 0.1 collective-permute-start.14
  47.4 1.3 %shard_map.116 = (f32[256,1024]{1,0:T(8,128)S(1)}, bf16[256,1024]{1,0:T(8,128)(2,1)S(1)}, bf16[256,1024]{1,0:T(8,128)(2,1)S(1)}, bf16[128,1024]{1,0:T(8,128)(2,1)S(1)}, bf16[128,1024]{1,0:T(8,128)(2,1)S(1)}) custom-call(bf16[1024,256]{1,0:T(8,128)(2,1)S(1)} %get-tuple-element.64.attn_ref, bf16[1024,256]{1,0:T(8,128)(2,1)S(1)} %collective-permute-done.7.recv_ref, ...), custom_call_target="tpu_custom_call" | custom-call | flops 1073741824 | bytes 6291456 | tf_op jit(solution)/shard_map/pallas_call | solution.py:43
  48.7 0.4 collective-permute-start.15
  49.1 1.2 %collective-permute-start.16 = (bf16[128,1024]{1,0:T(8,128)(2,1)S(1)}, bf16[128,1024]{1,0:T(8,128)(2,1)S(1)}, u32[]{:S(2)}, u32[]{:S(2)}) collective-permute-start(bf16[128,1024]{1,0:T(8,128)(2,1)S(1)} %get-tuple-element.89), channel_id=1, source_target_pairs={{0,4},{1,5},{2,6},{3,7},{4,0},{5,1},{6,2},{7,3},{8,12},{9,13},{10,... | collective-permute-start | bytes 786440 | tf_op jit(solution)/shard_map/ppermute | solution.py:427
  50.3 1.5 %shard_map.117 = (f32[2,128,1024]{2,1,0:T(8,128)S(1)}, bf16[2,128,1024]{2,1,0:T(8,128)(2,1)S(1)}) custom-call(bf16[2,128,1024]{2,1,0:T(8,128)(2,1)S(1)} %get-tuple-element.78.attn_t_ref, bf16[1024,256]{1,0:T(8,128)(2,1)S(1)} %collective-permute-done.7.recv_ref, bf16[1024,1024]{1,0:T(8,128)(2,1)S(1)} %get-tuple-element.79.cot_ref), custom_call_target="tpu_custom_call" | custom-call | flops 1073741824 | bytes 6291456 | tf_op jit(solution)/shard_map/pallas_call | solution.py:43
  51.8 1.6 %collective-permute-start.20 = (bf16[2,128,1024]{2,1,0:T(8,128)(2,1)S(1)}, bf16[2,128,1024]{2,1,0:T(8,128)(2,1)S(1)}, u32[]{:S(2)}, u32[]{:S(2)}) collective-permute-start(bf16[2,128,1024]{2,1,0:T(8,128)(2,1)S(1)} %get-tuple-element.94), channel_id=1, source_target_pairs={{0,8},{8,0},{16,24},{24,16},{1,9},{9,1},{17,25},{25,17},{2,10},{10... | collective-permute-start | bytes 1572872 | tf_op jit(solution)/shard_map/ppermute | solution.py:430
  53.5 4.5 %shard_map.118 = (bf16[3,128,256]{2,1,0:T(8,128)(2,1)S(1)}, bf16[3,128,256]{2,1,0:T(8,128)(2,1)S(1)}, bf16[3,128,256]{2,1,0:T(8,128)(2,1)S(1)}, bf16[3,128,256]{...) custom-call(bf16[2,1024,1024]{2,1,0:T(8,128)(2,1)S(1)} %get-tuple-el, ...), custom_call_target="tpu_custom_call" | custom-call | flops 2147483648 | bytes 8388608 | tf_op jit(solution)/shard_map/pallas_call | solution.py:43
  58.0 0.1 shard_map.119
  58.1 1.6 %collective-permute-start.17 = (bf16[256,1024]{1,0:T(8,128)(2,1)S(1)}, bf16[256,1024]{1,0:T(8,128)(2,1)S(1)}, u32[]{:S(2)}, u32[]{:S(2)}) collective-permute-start(bf16[256,1024]{1,0:T(8,128)(2,1)S(1)} %get-tuple-element.90), channel_id=1, source_target_pairs={{0,2},{1,3},{2,0},{3,1},{4,6},{5,7},{6,4},{7,5},{8,10},{9,11},{10,... | collective-permute-start | bytes 1572872 | tf_op jit(solution)/shard_map/ppermute | solution.py:427
  59.7 1.0 %collective-permute-start.18 = (bf16[256,1024]{1,0:T(8,128)(2,1)S(1)}, bf16[256,1024]{1,0:T(8,128)(2,1)S(1)}, u32[]{:S(2)}, u32[]{:S(2)}) collective-permute-start(bf16[256,1024]{1,0:T(8,128)(2,1)S(1)} %get-tuple-element.91), channel_id=1, source_target_pairs={{0,4},{1,5},{2,6},{3,7},{4,0},{5,1},{6,2},{7,3},{8,12},{9,13},{10,... | collective-permute-start | bytes 1572872 | tf_op jit(solution)/shard_map/ppermute | solution.py:427
  60.7 4.9 %collective-permute-done.20.recv_ref = bf16[2,128,1024]{2,1,0:T(8,128)(2,1)S(1)} collective-permute-done((bf16[2,128,1024]{2,1,0:T(8,128)(2,1)S(1)}, bf16[2,128,1024]{2,1,0:T(8,128)(2,1)S(1)}, u32[]{:S(2)}, u32[]{:S(2)}) %collective-permute-start.20) | collective-permute-done | bytes 524320 | tf_op jit(solution)/shard_map/ppermute | solution.py:430
  65.6 0.1 shard_map.121
  65.8 2.2 %collective-permute-start.22 = (bf16[1,128,1024]{2,1,0:T(8,128)(2,1)S(1)}, bf16[1,128,1024]{2,1,0:T(8,128)(2,1)S(1)}, u32[]{:S(2)}, u32[]{:S(2)}) collective-permute-start(bf16[1,128,1024]{2,1,0:T(8,128)(2,1)S(1)} %get-tuple-element.98), channel_id=1, source_target_pairs={{0,16},{8,24},{16,0},{24,8},{1,17},{9,25},{17,1},{25,9},{2,18},{10... | collective-permute-start | bytes 786440 | tf_op jit(solution)/shard_map/ppermute | solution.py:430
  67.9 1.5 %collective-permute-start.21 = (bf16[3,128,256]{2,1,0:T(8,128)(2,1)S(1)}, bf16[3,128,256]{2,1,0:T(8,128)(2,1)S(1)}, u32[]{:S(2)}, u32[]{:S(2)}) collective-permute-start(bf16[3,128,256]{2,1,0:T(8,128)(2,1)S(1)} %get-tuple-element.96), channel_id=1, source_target_pairs={{0,6},{1,7},{2,4},{3,5},{4,2},{5,3},{6,0},{7,1},{8,14},{9,15},{10,... | collective-permute-start | bytes 589832 | tf_op jit(solution)/shard_map/ppermute | solution.py:427
  69.4 1.4 %collective-permute-start.24 = (bf16[3,128,256]{2,1,0:T(8,128)(2,1)S(1)}, bf16[3,128,256]{2,1,0:T(8,128)(2,1)S(1)}, u32[]{:S(2)}, u32[]{:S(2)}) collective-permute-start(bf16[3,128,256]{2,1,0:T(8,128)(2,1)S(1)} %get-tuple-element.101), channel_id=1, source_target_pairs={{0,2},{1,3},{2,0},{3,1},{4,6},{5,7},{6,4},{7,5},{8,10},{9,11},{10,... | collective-permute-start | bytes 589832 | tf_op jit(solution)/shard_map/ppermute | solution.py:427
  70.8 2.2 %collective-permute-done.17.rest_0_ = bf16[256,1024]{1,0:T(8,128)(2,1)S(1)} collective-permute-done((bf16[256,1024]{1,0:T(8,128)(2,1)S(1)}, bf16[256,1024]{1,0:T(8,128)(2,1)S(1)}, u32[]{:S(2)}, u32[]{:S(2)}) %collective-permute-start.17) | collective-permute-done | bytes 524320 | tf_op jit(solution)/shard_map/ppermute | solution.py:427
  73.0 1.1 %collective-permute-start.25 = (bf16[3,128,256]{2,1,0:T(8,128)(2,1)S(1)}, bf16[3,128,256]{2,1,0:T(8,128)(2,1)S(1)}, u32[]{:S(2)}, u32[]{:S(2)}) collective-permute-start(bf16[3,128,256]{2,1,0:T(8,128)(2,1)S(1)} %get-tuple-element.102), channel_id=1, source_target_pairs={{0,4},{1,5},{2,6},{3,7},{4,0},{5,1},{6,2},{7,3},{8,12},{9,13},{10,... | collective-permute-start | bytes 589832 | tf_op jit(solution)/shard_map/ppermute | solution.py:427
  74.1 3.9 %collective-permute-done.18.rest_1_ = bf16[256,1024]{1,0:T(8,128)(2,1)S(1)} collective-permute-done((bf16[256,1024]{1,0:T(8,128)(2,1)S(1)}, bf16[256,1024]{1,0:T(8,128)(2,1)S(1)}, u32[]{:S(2)}, u32[]{:S(2)}) %collective-permute-start.18) | collective-permute-done | bytes 524320 | tf_op jit(solution)/shard_map/ppermute | solution.py:427
  78.0 0.2 shard_map.120
  78.3 1.3 %collective-permute-done.22.recv_ref = bf16[1,128,1024]{2,1,0:T(8,128)(2,1)S(1)} collective-permute-done((bf16[1,128,1024]{2,1,0:T(8,128)(2,1)S(1)}, bf16[1,128,1024]{2,1,0:T(8,128)(2,1)S(1)}, u32[]{:S(2)}, u32[]{:S(2)}) %collective-permute-start.22) | collective-permute-done | bytes 262176 | tf_op jit(solution)/shard_map/ppermute | solution.py:430
  79.8 0.7 collective-permute-done.24.rest_2_
  80.5 0.9 collective-permute-start.27
  81.4 4.1 %collective-permute-done.25.rest_3_ = bf16[3,128,256]{2,1,0:T(8,128)(2,1)S(1)} collective-permute-done((bf16[3,128,256]{2,1,0:T(8,128)(2,1)S(1)}, bf16[3,128,256]{2,1,0:T(8,128)(2,1)S(1)}, u32[]{:S(2)}, u32[]{:S(2)}) %collective-permute-start.25) | collective-permute-done | bytes 196640 | tf_op jit(solution)/shard_map/ppermute | solution.py:427
  85.5 1.1 %collective-permute-start.29 = (bf16[3,128,256]{2,1,0:T(8,128)(2,1)S(1)}, bf16[3,128,256]{2,1,0:T(8,128)(2,1)S(1)}, u32[]{:S(2)}, u32[]{:S(2)}) collective-permute-start(bf16[3,128,256]{2,1,0:T(8,128)(2,1)S(1)} %get-tuple-element.106), channel_id=1, source_target_pairs={{0,1},{1,0},{2,3},{3,2},{4,5},{5,4},{6,7},{7,6},{8,9},{9,8},{10,11... | collective-permute-start | bytes 589832 | tf_op jit(solution)/shard_map/ppermute | solution.py:427
  86.6 1.7 %collective-permute-done.27.rest_5_ = bf16[3,128,256]{2,1,0:T(8,128)(2,1)S(1)} collective-permute-done((bf16[3,128,256]{2,1,0:T(8,128)(2,1)S(1)}, bf16[3,128,256]{2,1,0:T(8,128)(2,1)S(1)}, u32[]{:S(2)}, u32[]{:S(2)}) %collective-permute-start.27) | collective-permute-done | bytes 196640 | tf_op jit(solution)/shard_map/ppermute | solution.py:427
  88.4 3.9 %collective-permute-done.28.rest_6_ = bf16[3,128,256]{2,1,0:T(8,128)(2,1)S(1)} collective-permute-done((bf16[3,128,256]{2,1,0:T(8,128)(2,1)S(1)}, bf16[3,128,256]{2,1,0:T(8,128)(2,1)S(1)}, u32[]{:S(2)}, u32[]{:S(2)}) %collective-permute-start.28) | collective-permute-done | bytes 196640 | tf_op jit(solution)/shard_map/ppermute | solution.py:427
  92.3 1.7 %shard_map.123 = (bf16[1,128,2048]{2,1,0:T(8,128)(2,1)}, bf16[1,128,2048]{2,1,0:T(8,128)(2,1)}, bf16[1,128,2048]{2,1,0:T(8,128)(2,1)}, bf16[1,128,2048]{2,1,0:T(8,128)(2,1)}, f32[64,2048]{1,0:T(8,128)}) custom-call(bf16[128,1024]{1,0:T(8,128)(2,1)S(1)} %get-tuple-element.92.keep_ref, bf16[128,1024]{1,0:T(8,128)(2,1)S(1)} %collective-permute-done.19.recv_ref, ...), custom_call_target="tpu_custom_call" | custom-call | bytes 4194304 | tf_op jit(solution)/shard_map/pallas_call | solution.py:43
  (30 shorter events, 0.4 us)
Async XLA Ops:
  2.3 33.9 %copy-start = (s32[1,8,8]{2,1,0:T(8,128)S(1)}, s32[1,8,8]{2,1,0:T(8,128)}, u32[]{:S(2)}) copy-start(s32[1,8,8]{2,1,0:T(8,128)} %adj_ref.1) | copy-start | bytes 772
  2.3 33.9 %copy-start.1 = (s32[1,8]{1,0:T(1,128)S(1)}, s32[1,8]{1,0:T(1,128)}, u32[]{:S(2)}) copy-start(s32[1,8]{1,0:T(1,128)} %cnt_ref.1) | copy-start | bytes 100
  2.3 8.8 %collective-permute-start = (bf16[3,128,256]{2,1,0:T(8,128)(2,1)S(1)}, bf16[3,128,256]{2,1,0:T(8,128)(2,1)S(1)}, u32[]{:S(2)}, u32[]{:S(2)}) collective-permute-start(bf16[3,128,256]{2,1,0:T(8,128)(2,1)S(1)} %get-tuple-element.57), channel_id=1, source_target_pairs={{0,6},{1,7},{2,4},{3,5},{4,2},{5,3},{6,0},{7,1},{8,14},{9,15},{10,... | collective-permute-start | bytes 589832 | tf_op jit(solution)/shard_map/ppermute | solution.py:427
  3.9 10.3 %collective-permute-start.1 = (bf16[3,128,256]{2,1,0:T(8,128)(2,1)S(1)}, bf16[3,128,256]{2,1,0:T(8,128)(2,1)S(1)}, u32[]{:S(2)}, u32[]{:S(2)}) collective-permute-start(bf16[3,128,256]{2,1,0:T(8,128)(2,1)S(1)} %get-tuple-element.58), channel_id=1, source_target_pairs={{0,2},{1,3},{2,0},{3,1},{4,6},{5,7},{6,4},{7,5},{8,10},{9,11},{10,... | collective-permute-start | bytes 589832 | tf_op jit(solution)/shard_map/ppermute | solution.py:427
  5.4 8.8 %collective-permute-start.10 = (bf16[128,1024]{1,0:T(8,128)(2,1)S(1)}, bf16[128,1024]{1,0:T(8,128)(2,1)S(1)}, u32[]{:S(2)}, u32[]{:S(2)}) collective-permute-start(bf16[128,1024]{1,0:T(8,128)(2,1)S(1)} %get-tuple-element.68), channel_id=1, source_target_pairs={{0,1},{1,0},{2,3},{3,2},{4,5},{5,4},{6,7},{7,6},{8,9},{9,8},{10,11... | collective-permute-start | bytes 786440 | tf_op jit(solution)/shard_map/ppermute | solution.py:427
  5.4 15.2 %collective-permute-start.8 = (bf16[1,128,1024]{2,1,0:T(8,128)(2,1)S(1)}, bf16[1,128,1024]{2,1,0:T(8,128)(2,1)S(1)}, u32[]{:S(2)}, u32[]{:S(2)}) collective-permute-start(bf16[1,128,1024]{2,1,0:T(8,128)(2,1)S(1)} %bitcast.4), channel_id=1, source_target_pairs={{0,16},{8,24},{16,0},{24,8},{1,17},{9,25},{17,1},{25,9},{2,18},{10... | collective-permute-start | bytes 786440 | tf_op jit(solution)/shard_map/ppermute | solution.py:430
  7.9 11.9 %collective-permute-start.2 = (bf16[3,128,256]{2,1,0:T(8,128)(2,1)S(1)}, bf16[3,128,256]{2,1,0:T(8,128)(2,1)S(1)}, u32[]{:S(2)}, u32[]{:S(2)}) collective-permute-start(bf16[3,128,256]{2,1,0:T(8,128)(2,1)S(1)} %get-tuple-element.59), channel_id=1, source_target_pairs={{0,4},{1,5},{2,6},{3,7},{4,0},{5,1},{6,2},{7,3},{8,12},{9,13},{10,... | collective-permute-start | bytes 589832 | tf_op jit(solution)/shard_map/ppermute | solution.py:427
  11.1 11.2 %collective-permute-start.3 = (bf16[3,128,256]{2,1,0:T(8,128)(2,1)S(1)}, bf16[3,128,256]{2,1,0:T(8,128)(2,1)S(1)}, u32[]{:S(2)}, u32[]{:S(2)}) collective-permute-start(bf16[3,128,256]{2,1,0:T(8,128)(2,1)S(1)} %get-tuple-element.60), channel_id=1, source_target_pairs={{0,7},{1,6},{2,5},{3,4},{4,3},{5,2},{6,1},{7,0},{8,15},{9,14},{10,... | collective-permute-start | bytes 589832 | tf_op jit(solution)/shard_map/ppermute | solution.py:427
  14.2 8.9 %collective-permute-start.4 = (bf16[3,128,256]{2,1,0:T(8,128)(2,1)S(1)}, bf16[3,128,256]{2,1,0:T(8,128)(2,1)S(1)}, u32[]{:S(2)}, u32[]{:S(2)}) collective-permute-start(bf16[3,128,256]{2,1,0:T(8,128)(2,1)S(1)} %get-tuple-element.61), channel_id=1, source_target_pairs={{0,3},{1,2},{2,1},{3,0},{4,7},{5,6},{6,5},{7,4},{8,11},{9,10},{10,... | collective-permute-start | bytes 589832 | tf_op jit(solution)/shard_map/ppermute | solution.py:427
  14.2 18.7 %collective-permute-start.5 = (bf16[3,128,256]{2,1,0:T(8,128)(2,1)S(1)}, bf16[3,128,256]{2,1,0:T(8,128)(2,1)S(1)}, u32[]{:S(2)}, u32[]{:S(2)}) collective-permute-start(bf16[3,128,256]{2,1,0:T(8,128)(2,1)S(1)} %get-tuple-element.62), channel_id=1, source_target_pairs={{0,5},{1,4},{2,7},{3,6},{4,1},{5,0},{6,3},{7,2},{8,13},{9,12},{10,... | collective-permute-start | bytes 589832 | tf_op jit(solution)/shard_map/ppermute | solution.py:427
  19.9 22.2 %collective-permute-start.13 = (bf16[256,1024]{1,0:T(8,128)(2,1)S(1)}, bf16[256,1024]{1,0:T(8,128)(2,1)S(1)}, u32[]{:S(2)}, u32[]{:S(2)}) collective-permute-start(bf16[256,1024]{1,0:T(8,128)(2,1)S(1)} %shard_map.114.rest_0_), channel_id=1, source_target_pairs={{0,6},{1,7},{2,4},{3,5},{4,2},{5,3},{6,0},{7,1},{8,14},{9,15},{10,... | collective-permute-start | bytes 1572872 | tf_op jit(solution)/shard_map/ppermute | solution.py:427
  20.7 21.3 %collective-permute-start.9 = (bf16[2,128,1024]{2,1,0:T(8,128)(2,1)S(1)}, bf16[2,128,1024]{2,1,0:T(8,128)(2,1)S(1)}, u32[]{:S(2)}, u32[]{:S(2)}) collective-permute-start(bf16[2,128,1024]{2,1,0:T(8,128)(2,1)S(1)} %shard_map.112.mine_ref), channel_id=1, source_target_pairs={{0,8},{8,0},{16,24},{24,16},{1,9},{9,1},{17,25},{25,17},{2,10},{10... | collective-permute-start | bytes 1572872 | tf_op jit(solution)/shard_map/ppermute | solution.py:430
  22.3 23.8 %collective-permute-start.12 = (bf16[256,1024]{1,0:T(8,128)(2,1)S(1)}, bf16[256,1024]{1,0:T(8,128)(2,1)S(1)}, u32[]{:S(2)}, u32[]{:S(2)}) collective-permute-start(bf16[256,1024]{1,0:T(8,128)(2,1)S(1)} %shard_map.114.rest_0_), channel_id=1, source_target_pairs={{0,4},{1,5},{2,6},{3,7},{4,0},{5,1},{6,2},{7,3},{8,12},{9,13},{10,... | collective-permute-start | bytes 1572872 | tf_op jit(solution)/shard_map/ppermute | solution.py:427
  23.1 23.0 %collective-permute-start.11 = (bf16[256,1024]{1,0:T(8,128)(2,1)S(1)}, bf16[256,1024]{1,0:T(8,128)(2,1)S(1)}, u32[]{:S(2)}, u32[]{:S(2)}) collective-permute-start(bf16[256,1024]{1,0:T(8,128)(2,1)S(1)} %shard_map.114.rest_0_), channel_id=1, source_target_pairs={{0,2},{1,3},{2,0},{3,1},{4,6},{5,7},{6,4},{7,5},{8,10},{9,11},{10,... | collective-permute-start | bytes 1572872 | tf_op jit(solution)/shard_map/ppermute | solution.py:427
  32.9 3.3 %collective-permute-start.6 = (bf16[3,128,256]{2,1,0:T(8,128)(2,1)S(1)}, bf16[3,128,256]{2,1,0:T(8,128)(2,1)S(1)}, u32[]{:S(2)}, u32[]{:S(2)}) collective-permute-start(bf16[3,128,256]{2,1,0:T(8,128)(2,1)S(1)} %get-tuple-element.63), channel_id=1, source_target_pairs={{0,1},{1,0},{2,3},{3,2},{4,5},{5,4},{6,7},{7,6},{8,9},{9,8},{10,11... | collective-permute-start | bytes 589832 | tf_op jit(solution)/shard_map/ppermute | solution.py:427
  41.6 5.8 %collective-permute-start.7 = (bf16[1024,256]{1,0:T(8,128)(2,1)S(1)}, bf16[1024,256]{1,0:T(8,128)(2,1)S(1)}, u32[]{:S(2)}, u32[]{:S(2)}) collective-permute-start(bf16[1024,256]{1,0:T(8,128)(2,1)S(1)} %get-tuple-element.65), channel_id=1, source_target_pairs={{0,1},{1,0},{2,3},{3,2},{4,5},{5,4},{6,7},{7,6},{8,9},{9,8},{10,11... | collective-permute-start | bytes 1572872 | tf_op jit(solution)/shard_map/ppermute | solution.py:427
  47.3 6.1 %collective-permute-start.14 = (bf16[256,1024]{1,0:T(8,128)(2,1)S(1)}, bf16[256,1024]{1,0:T(8,128)(2,1)S(1)}, u32[]{:S(2)}, u32[]{:S(2)}) collective-permute-start(bf16[256,1024]{1,0:T(8,128)(2,1)S(1)} %get-tuple-element.82), channel_id=1, source_target_pairs={{0,1},{1,0},{2,3},{3,2},{4,5},{5,4},{6,7},{7,6},{8,9},{9,8},{10,11... | collective-permute-start | bytes 1572872 | tf_op jit(solution)/shard_map/ppermute | solution.py:427
  48.7 9.2 %collective-permute-start.15 = (bf16[128,1024]{1,0:T(8,128)(2,1)S(1)}, bf16[128,1024]{1,0:T(8,128)(2,1)S(1)}, u32[]{:S(2)}, u32[]{:S(2)}) collective-permute-start(bf16[128,1024]{1,0:T(8,128)(2,1)S(1)} %get-tuple-element.87), channel_id=1, source_target_pairs={{0,2},{1,3},{2,0},{3,1},{4,6},{5,7},{6,4},{7,5},{8,10},{9,11},{10,... | collective-permute-start | bytes 786440 | tf_op jit(solution)/shard_map/ppermute | solution.py:427
  49.1 8.8 %collective-permute-start.16 = (bf16[128,1024]{1,0:T(8,128)(2,1)S(1)}, bf16[128,1024]{1,0:T(8,128)(2,1)S(1)}, u32[]{:S(2)}, u32[]{:S(2)}) collective-permute-start(bf16[128,1024]{1,0:T(8,128)(2,1)S(1)} %get-tuple-element.89), channel_id=1, source_target_pairs={{0,4},{1,5},{2,6},{3,7},{4,0},{5,1},{6,2},{7,3},{8,12},{9,13},{10,... | collective-permute-start | bytes 786440 | tf_op jit(solution)/shard_map/ppermute | solution.py:427
  51.8 13.8 %collective-permute-start.20 = (bf16[2,128,1024]{2,1,0:T(8,128)(2,1)S(1)}, bf16[2,128,1024]{2,1,0:T(8,128)(2,1)S(1)}, u32[]{:S(2)}, u32[]{:S(2)}) collective-permute-start(bf16[2,128,1024]{2,1,0:T(8,128)(2,1)S(1)} %get-tuple-element.94), channel_id=1, source_target_pairs={{0,8},{8,0},{16,24},{24,16},{1,9},{9,1},{17,25},{25,17},{2,10},{10... | collective-permute-start | bytes 1572872 | tf_op jit(solution)/shard_map/ppermute | solution.py:430
  58.1 14.9 %collective-permute-start.17 = (bf16[256,1024]{1,0:T(8,128)(2,1)S(1)}, bf16[256,1024]{1,0:T(8,128)(2,1)S(1)}, u32[]{:S(2)}, u32[]{:S(2)}) collective-permute-start(bf16[256,1024]{1,0:T(8,128)(2,1)S(1)} %get-tuple-element.90), channel_id=1, source_target_pairs={{0,2},{1,3},{2,0},{3,1},{4,6},{5,7},{6,4},{7,5},{8,10},{9,11},{10,... | collective-permute-start | bytes 1572872 | tf_op jit(solution)/shard_map/ppermute | solution.py:427
  59.7 18.3 %collective-permute-start.18 = (bf16[256,1024]{1,0:T(8,128)(2,1)S(1)}, bf16[256,1024]{1,0:T(8,128)(2,1)S(1)}, u32[]{:S(2)}, u32[]{:S(2)}) collective-permute-start(bf16[256,1024]{1,0:T(8,128)(2,1)S(1)} %get-tuple-element.91), channel_id=1, source_target_pairs={{0,4},{1,5},{2,6},{3,7},{4,0},{5,1},{6,2},{7,3},{8,12},{9,13},{10,... | collective-permute-start | bytes 1572872 | tf_op jit(solution)/shard_map/ppermute | solution.py:427
  65.8 13.8 %collective-permute-start.22 = (bf16[1,128,1024]{2,1,0:T(8,128)(2,1)S(1)}, bf16[1,128,1024]{2,1,0:T(8,128)(2,1)S(1)}, u32[]{:S(2)}, u32[]{:S(2)}) collective-permute-start(bf16[1,128,1024]{2,1,0:T(8,128)(2,1)S(1)} %get-tuple-element.98), channel_id=1, source_target_pairs={{0,16},{8,24},{16,0},{24,8},{1,17},{9,25},{17,1},{25,9},{2,18},{10... | collective-permute-start | bytes 786440 | tf_op jit(solution)/shard_map/ppermute | solution.py:430
  67.9 10.3 %collective-permute-start.21 = (bf16[3,128,256]{2,1,0:T(8,128)(2,1)S(1)}, bf16[3,128,256]{2,1,0:T(8,128)(2,1)S(1)}, u32[]{:S(2)}, u32[]{:S(2)}) collective-permute-start(bf16[3,128,256]{2,1,0:T(8,128)(2,1)S(1)} %get-tuple-element.96), channel_id=1, source_target_pairs={{0,6},{1,7},{2,4},{3,5},{4,2},{5,3},{6,0},{7,1},{8,14},{9,15},{10,... | collective-permute-start | bytes 589832 | tf_op jit(solution)/shard_map/ppermute | solution.py:427
  69.4 11.1 %collective-permute-start.24 = (bf16[3,128,256]{2,1,0:T(8,128)(2,1)S(1)}, bf16[3,128,256]{2,1,0:T(8,128)(2,1)S(1)}, u32[]{:S(2)}, u32[]{:S(2)}) collective-permute-start(bf16[3,128,256]{2,1,0:T(8,128)(2,1)S(1)} %get-tuple-element.101), channel_id=1, source_target_pairs={{0,2},{1,3},{2,0},{3,1},{4,6},{5,7},{6,4},{7,5},{8,10},{9,11},{10,... | collective-permute-start | bytes 589832 | tf_op jit(solution)/shard_map/ppermute | solution.py:427
  73.0 12.5 %collective-permute-start.25 = (bf16[3,128,256]{2,1,0:T(8,128)(2,1)S(1)}, bf16[3,128,256]{2,1,0:T(8,128)(2,1)S(1)}, u32[]{:S(2)}, u32[]{:S(2)}) collective-permute-start(bf16[3,128,256]{2,1,0:T(8,128)(2,1)S(1)} %get-tuple-element.102), channel_id=1, source_target_pairs={{0,4},{1,5},{2,6},{3,7},{4,0},{5,1},{6,2},{7,3},{8,12},{9,13},{10,... | collective-permute-start | bytes 589832 | tf_op jit(solution)/shard_map/ppermute | solution.py:427
  78.0 7.5 %collective-permute-start.26 = (bf16[3,128,256]{2,1,0:T(8,128)(2,1)S(1)}, bf16[3,128,256]{2,1,0:T(8,128)(2,1)S(1)}, u32[]{:S(2)}, u32[]{:S(2)}) collective-permute-start(bf16[3,128,256]{2,1,0:T(8,128)(2,1)S(1)} %get-tuple-element.103), channel_id=1, source_target_pairs={{0,7},{1,6},{2,5},{3,4},{4,3},{5,2},{6,1},{7,0},{8,15},{9,14},{10,... | collective-permute-start | bytes 589832 | tf_op jit(solution)/shard_map/ppermute | solution.py:427
  78.2 14.0 %collective-permute-start.19 = (bf16[128,1024]{1,0:T(8,128)(2,1)S(1)}, bf16[128,1024]{1,0:T(8,128)(2,1)S(1)}, u32[]{:S(2)}, u32[]{:S(2)}) collective-permute-start(bf16[128,1024]{1,0:T(8,128)(2,1)S(1)} %get-tuple-element.93), channel_id=1, source_target_pairs={{0,1},{1,0},{2,3},{3,2},{4,5},{5,4},{6,7},{7,6},{8,9},{9,8},{10,11... | collective-permute-start | bytes 786440 | tf_op jit(solution)/shard_map/ppermute | solution.py:427
  79.7 12.6 %collective-permute-start.23 = (f32[64,1024]{1,0:T(8,128)S(1)}, f32[64,1024]{1,0:T(8,128)S(1)}, u32[]{:S(2)}, u32[]{:S(2)}) collective-permute-start(f32[64,1024]{1,0:T(8,128)S(1)} %get-tuple-element.100), channel_id=1, source_target_pairs={{0,1},{1,0},{2,3},{3,2},{4,5},{5,4},{6,7},{7,6},{8,9},{9,8},{10,11... | collective-permute-start | bytes 786440 | tf_op jit(solution)/shard_map/ppermute | solution.py:427
  80.5 7.9 %collective-permute-start.27 = (bf16[3,128,256]{2,1,0:T(8,128)(2,1)S(1)}, bf16[3,128,256]{2,1,0:T(8,128)(2,1)S(1)}, u32[]{:S(2)}, u32[]{:S(2)}) collective-permute-start(bf16[3,128,256]{2,1,0:T(8,128)(2,1)S(1)} %get-tuple-element.104), channel_id=1, source_target_pairs={{0,3},{1,2},{2,1},{3,0},{4,7},{5,6},{6,5},{7,4},{8,11},{9,10},{10,... | collective-permute-start | bytes 589832 | tf_op jit(solution)/shard_map/ppermute | solution.py:427
  85.5 6.8 %collective-permute-start.28 = (bf16[3,128,256]{2,1,0:T(8,128)(2,1)S(1)}, bf16[3,128,256]{2,1,0:T(8,128)(2,1)S(1)}, u32[]{:S(2)}, u32[]{:S(2)}) collective-permute-start(bf16[3,128,256]{2,1,0:T(8,128)(2,1)S(1)} %get-tuple-element.105), channel_id=1, source_target_pairs={{0,5},{1,4},{2,7},{3,6},{4,1},{5,0},{6,3},{7,2},{8,13},{9,12},{10,... | collective-permute-start | bytes 589832 | tf_op jit(solution)/shard_map/ppermute | solution.py:427
  85.5 6.8 %collective-permute-start.29 = (bf16[3,128,256]{2,1,0:T(8,128)(2,1)S(1)}, bf16[3,128,256]{2,1,0:T(8,128)(2,1)S(1)}, u32[]{:S(2)}, u32[]{:S(2)}) collective-permute-start(bf16[3,128,256]{2,1,0:T(8,128)(2,1)S(1)} %get-tuple-element.106), channel_id=1, source_target_pairs={{0,1},{1,0},{2,3},{3,2},{4,5},{5,4},{6,7},{7,6},{8,9},{9,8},{10,11... | collective-permute-start | bytes 589832 | tf_op jit(solution)/shard_map/ppermute | solution.py:427
